TPU v7x, 128 devices: a whole 4x4x4 slice. The times are simulated.
128 devices in a mesh: rep: 8 (over x_hi, z), shard: 16 (over y, x_lo, core).
Axes of the slice: x: 4 (x_hi: 2, x_lo: 2; x = x_hi * 2 + x_lo), y: 4, z: 4, core: 2. Of those that a mesh axis runs over, the one named last changes fastest.
Arguments:
- hidden: bfloat16 [131072, 1536], P(('rep', 'shard')), may hold values from -24 to 24
- out_grad: bfloat16 [131072, 5120], P(('rep', 'shard')), may hold values from -0.046875 to 0.046875
- inner_params: float32 [8, 1536, 5120], P('rep', 'shard'), may hold values from -4.8 to 4.8
- first_moment: bfloat16 [8, 1536, 5120], P('rep', 'shard'), may hold values from -6 to 6
- second_moment: bfloat16 [8, 1536, 5120], P('rep', 'shard'), may hold values from 0.25 to 4
- anchor: float32 [1536, 5120], P('shard'), may hold values from -4 to 4
- outer_moment: float32 [1536, 5120], P('shard', 'rep'), may hold values from -0.6 to 0.6
Outputs:
- new_params: float32 [1536, 5120], P('shard')
- new_first: bfloat16 [8, 1536, 5120], P('rep', 'shard')
- new_second: bfloat16 [8, 1536, 5120], P('rep', 'shard')
- new_moment: float32 [1536, 5120], P('shard', 'rep')
All inputs are finite; a program needn't handle non-finite values.
Results may differ from a plain program's by a relative error of at most 0.012.
Values may be sent and summed in bfloat16 or wider, within the bound.
No kernel may reach another device: no remote copies, remote signals or barrier semaphores. Data moves between devices by JAX's collectives and lax.ppermute only.
A program may use at most 128 MiB of HBM per device.

v0:
```python
import jax
import jax.numpy as jnp
from jax import lax
from jax.sharding import PartitionSpec as P

beta_first = 0.9
beta_second = 0.95
bias_first = 1.0 - 0.9**30
bias_second = 1.0 - 0.95**30
inner_rate = 0.05
decay_rate = 0.1
epsilon = 1e-08
outer_beta = 0.9
outer_rate = 0.7


def adam_rows(gradient, first_rows, second_rows, param_rows):
    first_fresh = beta_first * first_rows.astype(jnp.float32) + (1.0 - beta_first) * gradient
    second_fresh = (
        beta_second * second_rows.astype(jnp.float32) + (1.0 - beta_second) * gradient * gradient
    )
    update = (
        first_fresh / bias_first / (jnp.sqrt(second_fresh / bias_second) + epsilon)
        + decay_rate * param_rows
    )
    stepped = param_rows - inner_rate * update
    return (first_fresh, second_fresh, stepped)


def body(hidden, out_grad, inner_params, first_moment, second_moment, anchor, outer_moment):
    shard_count = lax.axis_size("shard")
    replica_count = lax.axis_size("rep")
    token_rows = hidden.shape[0]
    local_rows = anchor.shape[0]
    share_width = outer_moment.shape[1]
    group_count = 1
    group_rows = local_rows // group_count
    column_start = lax.axis_index("rep") * share_width
    columns = hidden.reshape(token_rows, shard_count, group_count, group_rows)[:, :, 0, :]
    columns = columns.reshape(token_rows, shard_count * group_rows)

    def partial_term(first_row, row_count, columns=columns):
        return lax.dot_general(
            columns, out_grad, (((0,), (0,)), ((), ())), preferred_element_type=jnp.float32
        )

    gradient = lax.psum_scatter(
        partial_term(jnp.int32(0), lax.axis_size("shard") * group_rows).astype(jnp.bfloat16),
        "shard",
        scatter_dimension=0,
        tiled=True,
    ).astype(jnp.float32)
    first_fresh, second_fresh, stepped = adam_rows(
        gradient,
        first_moment[0, 0:group_rows],
        second_moment[0, 0:group_rows],
        inner_params[0, 0:group_rows],
    )
    departure = anchor - stepped
    pseudo = lax.psum(departure.astype(jnp.bfloat16), "rep").astype(jnp.float32) / replica_count
    moment_whole = lax.all_gather(
        outer_moment.astype(jnp.bfloat16), "rep", axis=1, tiled=True
    ).astype(outer_moment.dtype)
    moment_full = outer_beta * moment_whole + pseudo
    params_new = anchor - outer_rate * (pseudo + outer_beta * moment_full)
    moment_new = lax.dynamic_slice_in_dim(moment_full, column_start, share_width, 1)
    first_list = first_fresh.astype(jnp.bfloat16)
    second_list = second_fresh.astype(jnp.bfloat16)
    first_out = first_list[None]
    second_out = second_list[None]
    return (params_new, first_out, second_out, moment_new)


def solution(mesh):
    placed = (
        P(("rep", "shard"), None),
        P(("rep", "shard"), None),
        P("rep", "shard", None),
        P("rep", "shard", None),
        P("rep", "shard", None),
        P("shard", None),
        P("shard", "rep"),
    )
    return jax.shard_map(
        body,
        mesh=mesh,
        in_specs=placed,
        out_specs=(
            P("shard", None),
            P("rep", "shard", None),
            P("rep", "shard", None),
            P("shard", "rep"),
        ),
        check_vma=False,
    )
```

profile of v0, /device:TPU:0, one launch (start us, length us, event | category | flops | bytes accessed | tf_op | source)
XLA Modules:
  0.0 313.1 jit_solution(1758192788235122236)
XLA Ops:
  7.2 0.0 copy-start
  7.2 0.0 reduce-scatter.2.cloned.1.call-start
  7.2 1.8 copy-done
  9.1 23.3 %convolution_convert_fusion = bf16[1536,5120]{1,0:T(8,128)(2,1)} fusion(bf16[1024,1536]{1,0:T(8,128)(2,1)S(1)} %copy-done, bf16[1024,5120]{1,0:T(8,128)(2,1)} %param.8), kind=kOutput, calls=%fused_computation | convolution fusion | flops 16113991680 | bytes 29360128 | tf_op jit(solution)/shard_map/dot_general | solution.py:43
  32.4 0.0 reduce-scatter.2.cloned.1.call-update
  32.4 0.0 copy-start.1
  32.4 0.0 all-reduce.2.cloned.1.call-start
  32.4 174.3 %reduce-scatter.2.cloned.1.call-done = bf16[96,5120]{1,0:T(8,128)(2,1)} async-done(((bf16[1536,5120]{1,0:T(8,128)(2,1)}), bf16[96,5120]{1,0:T(8,128)(2,1)}) %reduce-scatter.2.cloned.1.call-update) | async-done | bytes 983056 | tf_op jit(solution)/shard_map/reduce_scatter | solution.py:47
  206.8 6.8 %fusion.8 = (bf16[1,96,5120]{2,1,0:T(8,128)(2,1)}, bf16[96,5120]{1,0:T(8,128)(2,1)}, bf16[1,96,5120]{2,1,0:T(8,128)(2,1)}) fusion(bf16[96,5120]{1,0:T(8,128)(2,1)} %reduce-scatter.2.cloned.1.call-done, bf16[1,96,5120]{2,1,0:T(8,128)(2,1)} %param.11, f32[96,5120]{1,0:T(8,128)} %param.12, bf16[1,96,5120]{2,1,0:T(8,128)(2,1)} %param.10, f32[1,96,5120]{2,1,0:T(8,128)} %param.9), kind=kLoop, calls=%fused_computation.16 | loop fusion | flops 10813440 | bytes 9830400 | tf_op jit(solution)/shard_map/broadcast_in_dim | solution.py:70
  213.6 0.0 all-reduce.2.cloned.1.call-update
  213.6 0.0 copy-done.1
  213.7 39.2 %all_gather.3 = bf16[96,5120]{1,0:T(8,128)(2,1)} all-gather(bf16[96,640]{1,0:T(8,128)(2,1)S(1)} %convert_element_type.38), channel_id=1, replica_groups=mesh['rep'=8,'shard'=16] {'rep'}, dimensions={1}, use_global_device_ids=true | all-gather | bytes 1105920 | tf_op jit(solution)/shard_map/all_gather | solution.py:61
  252.8 48.8 %all-reduce.2.cloned.1.call-done = bf16[96,5120]{1,0:T(8,128)(2,1)} async-done(((bf16[96,5120]{1,0:T(8,128)(2,1)}), bf16[96,5120]{1,0:T(8,128)(2,1)}) %all-reduce.2.cloned.1.call-update) | async-done | bytes 983056 | tf_op jit(solution)/shard_map/psum | solution.py:60
  301.6 4.0 %multiply_add_fusion = (f32[96,5120]{1,0:T(8,128)S(1)}, f32[96,5120]{1,0:T(8,128)}) fusion(bf16[96,5120]{1,0:T(8,128)(2,1)} %all_gather.3, bf16[96,5120]{1,0:T(8,128)(2,1)} %all-reduce.2.cloned.1.call-done, f32[96,5120]{1,0:T(8,128)} %param.12), kind=kLoop, calls=%fused_computation.12 | loop fusion | flops 4423680 | bytes 7864320 | tf_op jit(solution)/shard_map/add | solution.py:64
  305.6 0.7 constant_dynamic-slice_fusion
  (1 shorter events, 0.0 us)
Async XLA Ops:
  7.2 1.9 copy-start
  7.2 199.6 %reduce-scatter.2.cloned.1.call-start = ((), (), s32[]{:S(2)}) async-start(), calls=%async_computation.1 | async-start | bytes 16711680 | tf_op jit(solution)/shard_map/reduce_scatter | solution.py:47
  32.4 181.3 %copy-start.1 = (f32[96,640]{1,0:T(8,128)S(1)}, f32[96,640]{1,0:T(8,128)}, u32[]{:S(2)}) copy-start(f32[96,640]{1,0:T(8,128)} %param.13) | copy-start | bytes 737284
  32.4 269.2 %all-reduce.2.cloned.1.call-start = ((), (), s32[]{:S(2)}) async-start(), calls=%async_computation.2 | async-start | bytes 1966080 | tf_op jit(solution)/shard_map/psum | solution.py:60
Sparse Core Ops, SparseCore 0:
  32.5 174.2 reduce-scatter.1
  213.7 87.8 all-reduce.1
where the time goes:
time: 313 us
  waiting for transfers between devices  223 us (71%)
  blocking collectives  39.2 us (13%)
  matrix products  23.3 us (7%)
  between operations  14.1 us (5%)
  other arithmetic  10.9 us (3%)
    reduce_scatter x1, waiting for transfers between devices, body(): lax.psum_scatter(partial_term(jnp.int32(0), lax.axis_size('shard') * grou...  174 us
    psum x1, waiting for transfers between devices, body(): lax.psum(departure.astype(jnp.bfloat16), 'rep').astype(jnp.float32)  48.8 us
    all_gather x1, blocking collectives, body(): lax.all_gather(outer_moment.astype(jnp.bfloat16), 'rep', axis=1, tiled=True)  39.2 us
    dot_general x1, matrix products, partial_term(): lax.dot_general(columns, out_grad, (((0,), (0,)), ((), ())), preferred_el...  23.3 us
    broadcast_in_dim x1, other arithmetic, body(): second_out = second_list[None]  6.84 us
  transfers between devices with their start and end apart: 2, of which 2 were waited for; matrix products, arithmetic and copies ran while one was open for 0% of the time, Pallas kernels for 0%

commit v1 on v0

v1 whole, which is shorter than its diff:
```python
import functools

import jax
import jax.numpy as jnp
from jax import lax
from jax.experimental import pallas as pl
from jax.experimental.pallas import tpu as pltpu
from jax.sharding import PartitionSpec as P

beta_first = 0.9
beta_second = 0.95
bias_first = 1.0 - 0.9**30
bias_second = 1.0 - 0.95**30
inner_rate = 0.05
decay_rate = 0.1
epsilon = 1e-08
outer_beta = 0.9
outer_rate = 0.7

pseudo_weight = 1.0 + outer_beta
moment_weight = outer_beta * outer_beta

SHARDS = 16
REPLICAS = 8
BF = jnp.bfloat16
F32 = jnp.float32
LIMIT = 40 * 1024 * 1024

CORE = 1
MASKS = (2, 4, 12)
CHUNKS = (
    (0, 1792, (0, 1, 2)),
    (1792, 1792, (1, 2, 0)),
    (3584, 1536, (2, 0, 1)),
)
GROUPS = ((0,), (1, 2))
TILE = 256


def swap(value, mask):
    return lax.ppermute(value, "shard", [(i, i ^ mask) for i in range(SHARDS)])


def swap_rep(value, mask):
    return lax.ppermute(value, "rep", [(i, i ^ mask) for i in range(REPLICAS)])


def params(**kw):
    return pltpu.CompilerParams(vmem_limit_bytes=LIMIT, **kw)


def turn_kernel(rows, place, hidden_ref, own_ref, other_ref, turned):
    turned[...] = hidden_ref[...].T.reshape(turned.shape)
    me = place[0]
    for bx in range(2):
        for ba in range(2):
            for bb in range(2):
                mask = (bx * MASKS[0]) ^ (ba * MASKS[1]) ^ (bb * MASKS[2])
                own_ref[bx, ba, bb] = turned[me ^ mask]
                other_ref[bx, ba, bb] = turned[me ^ mask ^ CORE]


def turn(hidden, place):
    tokens, width = hidden.shape
    rows = width // SHARDS
    step = min(256, tokens)
    shape = jax.ShapeDtypeStruct((2, 2, 2, rows, tokens), BF)
    block = pl.BlockSpec((2, 2, 2, rows, step), lambda i, p: (0, 0, 0, 0, i))
    return pl.pallas_call(
        functools.partial(turn_kernel, rows),
        grid_spec=pltpu.PrefetchScalarGridSpec(
            num_scalar_prefetch=1,
            grid=(tokens // step,),
            in_specs=[pl.BlockSpec((step, width), lambda i, p: (i, 0))],
            out_specs=[block, block],
            scratch_shapes=[pltpu.VMEM((SHARDS, rows, step), BF)],
        ),
        out_shape=[shape, shape],
        compiler_params=params(),
        cost_estimate=pl.CostEstimate(flops=0, bytes_accessed=4 * tokens * width, transcendentals=0),
        name="turn",
    )(place, hidden)


def product_kernel(left_ref, left_far_ref, right_ref, right_far_ref, out_ref):
    depth = left_ref.shape[-1]
    left = left_ref[...].reshape(-1, depth)
    left_far = left_far_ref[...].reshape(-1, depth)
    total = jnp.dot(left, right_ref[...], preferred_element_type=F32)
    total += jnp.dot(left_far, right_far_ref[...], preferred_element_type=F32)
    out_ref[...] = total.astype(BF).reshape(out_ref.shape)


def product(left, left_far, right, right_far, dim, bit, first, width):
    rows, depth = left.shape[3:]
    halves = [2, 2, 2]
    halves[dim] = 1
    place = [0, 0, 0]
    place[dim] = bit
    lhs = pl.BlockSpec((*halves, rows, depth), lambda i: (*place, 0, 0))
    flops = 2 * 2 * 4 * rows * depth * width
    return pl.pallas_call(
        product_kernel,
        grid=(width // TILE,),
        in_specs=[
            lhs,
            lhs,
            pl.BlockSpec((depth, TILE), lambda i: (0, first // TILE + i)),
            pl.BlockSpec((depth, TILE), lambda i: (0, i)),
        ],
        out_specs=pl.BlockSpec((2, 2, rows, TILE), lambda i: (0, 0, 0, i)),
        out_shape=jax.ShapeDtypeStruct((2, 2, rows, width), BF),
        compiler_params=params(),
        cost_estimate=pl.CostEstimate(
            flops=flops,
            bytes_accessed=2 * (4 * depth * rows * 2 + 2 * depth * width + 4 * rows * width),
            transcendentals=0,
        ),
        name="product",
    )(left, left_far, right, right_far)


def adam_kernel(chained, place, *refs):
    grads, rest = refs[:2], refs[2:]
    first_ref, second_ref, param_ref, anchor_ref, moment_ref = rest[:5]
    outs = rest[5 + chained :]
    first_out, second_out = outs[:2]
    parts = outs[2:6]
    quarters = outs[6]
    gradient = grads[0][...].astype(F32) + grads[1][...].astype(F32)
    first_fresh = beta_first * first_ref[0].astype(F32) + (1.0 - beta_first) * gradient
    second_fresh = beta_second * second_ref[0].astype(F32) + (1.0 - beta_second) * gradient * gradient
    rows = param_ref[0]
    update = first_fresh / bias_first / (jnp.sqrt(second_fresh / bias_second) + epsilon) + decay_rate * rows
    stepped = rows - inner_rate * update
    first_out[0] = first_fresh.astype(BF)
    second_out[0] = second_fresh.astype(BF)
    departure = (anchor_ref[...] - stepped) * (pseudo_weight / REPLICAS) + moment_ref[...]
    quarters[...] = departure.reshape(quarters.shape)
    for distance in range(4):
        parts[distance][...] = quarters[place[1] ^ distance].astype(BF)


def adam(place, grads, first, second, param, anchor, moment, column, width, before, group_column, group_width):
    rows, total_width = anchor.shape
    step = TILE
    part = rows // 4

    def at(offset):
        return lambda i, p: (0, offset // step + i)

    def at3(offset):
        return lambda i, p: (0, 0, offset // step + i)

    flat = pl.BlockSpec((rows, step), at(column))
    deep = pl.BlockSpec((1, rows, step), at3(column))
    part_spec = pl.BlockSpec((part, step), at(group_column))
    part_shape = jax.ShapeDtypeStruct((part, group_width), BF)
    firsts, seconds, parts = before
    chain = [(0, firsts), (1, seconds)] + [(2 + d, p) for d, p in enumerate(parts or ())]
    chain = [(o, a) for o, a in chain if a is not None]
    aliases = {1 + 7 + n: o for n, (o, _) in enumerate(chain)}
    outs = pl.pallas_call(
        functools.partial(adam_kernel, len(chain)),
        grid_spec=pltpu.PrefetchScalarGridSpec(
            num_scalar_prefetch=1,
            grid=(width // step,),
            in_specs=[pl.BlockSpec((rows, step), at(0))] * 2
            + [deep, deep, deep, flat, flat]
            + [pl.BlockSpec(memory_space=pl.ANY)] * len(chain),
            out_specs=[deep, deep] + [part_spec] * 4,
            scratch_shapes=[pltpu.VMEM((4, part, step), F32)],
        ),
        out_shape=[jax.ShapeDtypeStruct(first.shape, BF)] * 2 + [part_shape] * 4,
        input_output_aliases=aliases,
        compiler_params=params(),
        cost_estimate=pl.CostEstimate(flops=20 * rows * width, bytes_accessed=24 * rows * width, transcendentals=0),
        name="adam",
    )(place, *grads, first, second, param, anchor, moment, *(a for _, a in chain))
    return outs[0], outs[1], outs[2:]


def last_kernel(chained, place, p0, p1, p2, p3, anchor_ref, *refs):
    params_out, total_out, quarters = refs[chained:]
    for distance, piece in enumerate((p0, p1, p2, p3)):
        quarters[place[1] ^ distance] = piece[...].astype(F32)
    total = quarters[...].reshape(anchor_ref.shape)
    params_out[...] = anchor_ref[...] - outer_rate * total
    total_out[...] = total


def last(place, pieces, anchor, column, width, before):
    rows, total_width = anchor.shape
    part = rows // 4
    step = TILE
    piece = pl.BlockSpec((part, step), lambda i, p: (0, i))
    flat = pl.BlockSpec((rows, step), lambda i, p: (0, column // step + i))
    shape = jax.ShapeDtypeStruct(anchor.shape, F32)
    chain = [a for a in before if a is not None]
    return pl.pallas_call(
        functools.partial(last_kernel, len(chain)),
        grid_spec=pltpu.PrefetchScalarGridSpec(
            num_scalar_prefetch=1,
            grid=(width // step,),
            in_specs=[piece] * 4 + [flat] + [pl.BlockSpec(memory_space=pl.ANY)] * len(chain),
            out_specs=[flat, flat],
            scratch_shapes=[pltpu.VMEM((4, part, step), F32)],
        ),
        out_shape=[shape, shape],
        input_output_aliases={6 + n: n for n in range(len(chain))},
        compiler_params=params(),
        cost_estimate=pl.CostEstimate(flops=2 * rows * width, bytes_accessed=14 * rows * width, transcendentals=0),
        name="last",
    )(place, *pieces, anchor, *chain)


def add(*values):
    total = values[0].astype(F32)
    for value in values[1:]:
        total = total + value.astype(F32)
    return total.astype(BF)


def body(hidden, out_grad, inner_params, first_moment, second_moment, anchor, outer_moment):
    me = lax.axis_index("shard")
    rep = lax.axis_index("rep")
    share = outer_moment.shape[1]
    place = jnp.stack([me, rep % 4]).astype(jnp.int32)
    placed_moment = lax.dynamic_update_slice(
        jnp.zeros(anchor.shape, F32), moment_weight * outer_moment, (0, rep * share)
    )

    own, other = turn(hidden, place)
    far = swap(other, CORE)
    grads_far = [swap(out_grad[:, c : c + w], CORE) for c, w, _ in CHUNKS]

    arrived = []
    for (column, width, order), grad_far in zip(CHUNKS, grads_far):
        sent = product(own, far, out_grad, grad_far, order[0], 1, column, width)
        arrived.append(swap(sent, MASKS[order[0]]))
    kept = []
    for (column, width, order), grad_far in zip(CHUNKS, grads_far):
        kept.append(product(own, far, out_grad, grad_far, order[0], 0, column, width))
    seconds = []
    for (column, width, order), mine, came in zip(CHUNKS, kept, arrived):
        if order[1] == min(order[1:]):
            go = add(mine[1], came[1])
            stay = add(mine[0], came[0])
        else:
            go = add(mine[:, 1], came[:, 1])
            stay = add(mine[:, 0], came[:, 0])
        seconds.append((stay, swap(go, MASKS[order[1]])))
    thirds = []
    for (column, width, order), (mine, came) in zip(CHUNKS, seconds):
        go = add(mine[1], came[1])
        stay = add(mine[0], came[0])
        thirds.append((stay, swap(go, MASKS[order[2]])))

    firsts = secs = None
    result = [None, None]
    for group in GROUPS:
        group_column = CHUNKS[group[0]][0]
        group_width = sum(CHUNKS[n][1] for n in group)
        parts = None
        for n in group:
            column, width, _ = CHUNKS[n]
            firsts, secs, parts = adam(
                place, thirds[n], first_moment, second_moment, inner_params, anchor, placed_moment,
                column, width, (firsts, secs, parts), column - group_column, group_width,
            )
        mine = add(parts[0], *(swap_rep(parts[d], d) for d in (1, 3, 2)))
        mine = add(mine, swap_rep(mine, 4))
        pieces = [mine] + [swap_rep(mine, d) for d in (1, 2, 3)]
        result = last(place, pieces, anchor, group_column, group_width, result)
    params_new, total = result
    total_share = lax.dynamic_slice_in_dim(total, rep * share, share, 1)
    moment_new = outer_beta * outer_moment + (total_share - moment_weight * outer_moment) / pseudo_weight
    return (params_new, firsts, secs, moment_new)


def solution(mesh):
    placed = (
        P(("rep", "shard"), None),
        P(("rep", "shard"), None),
        P("rep", "shard", None),
        P("rep", "shard", None),
        P("rep", "shard", None),
        P("shard", None),
        P("shard", "rep"),
    )
    return jax.shard_map(
        body,
        mesh=mesh,
        in_specs=placed,
        out_specs=(
            P("shard", None),
            P("rep", "shard", None),
            P("rep", "shard", None),
            P("shard", "rep"),
        ),
        check_vma=False,
    )
```

time: 313 us -> 159 us (0.51)
  waiting for transfers between devices: 223 us -> 42.4 us
  Pallas kernels: 0 us -> 63.9 us
  blocking collectives: 39.2 us -> 0 us
  starting transfers between devices: 0.08 us -> 34.3 us
  matrix products: 23.3 us -> 0 us
  between operations: 14.1 us -> 0.82 us
  local copies, waits for them, and re-layouts: 2.56 us -> 13 us
  other arithmetic: 10.9 us -> 3.72 us
    reduce_scatter x1 -> x0, waiting for transfers between devices: 174 us -> none  [body(): lax.psum_scatter(partial_term(jnp.int32(0), lax.axis_size('shard') * grou...]
    pallas_call x0 -> x12, Pallas kernels: none -> 63.9 us  [the longest x6 42.4 us: product(): pl.pallas_call(product_kernel, grid=(width // TILE,), in_specs=[lhs, lhs,...]
    psum x1 -> x0, waiting for transfers between devices: 48.8 us -> none  [body(): lax.psum(departure.astype(jnp.bfloat16), 'rep').astype(jnp.float32)]
    ppermute x0 -> x27, waiting for transfers between devices: none -> 42.4 us  [the longest x13 30.4 us: swap(): return lax.ppermute(value, 'shard', [(i, i ^ mask) for i in range(SHARDS)])]
    all_gather x1 -> x0, blocking collectives: 39.2 us -> none  [body(): lax.all_gather(outer_moment.astype(jnp.bfloat16), 'rep', axis=1, tiled=True)]
    ppermute x0 -> x27, starting transfers between devices: none -> 34.3 us  [the longest x14 22.9 us: swap_rep(): return lax.ppermute(value, 'rep', [(i, i ^ mask) for i in range(REPLICAS)])]
    dot_general x1 -> x0, matrix products: 23.3 us -> none  [partial_term(): lax.dot_general(columns, out_grad, (((0,), (0,)), ((), ())), preferred_el...]
    slice x0 -> x2, local copies, waits for them, and re-layouts: none -> 10.4 us  [body(): grads_far = [swap(out_grad[:, c:c + w], CORE) for c, w, _ in CHUNKS]]
  transfers between devices with their start and end apart: 2 -> 27, of which waited for: 2 -> 9; matrix products, arithmetic and copies ran while one was open for 0% -> 4% of each run, Pallas kernels for 0% -> 37%
where the time goes in v1:
time: 159 us; the launch traced here: 158 us
  Pallas kernels  63.9 us (40%)
  waiting for transfers between devices  42.4 us (27%)
  starting transfers between devices  34.3 us (22%)
  local copies, waits for them, and re-layouts  13 us (8%)
  other arithmetic  3.72 us (2%)
    pallas_call x6, Pallas kernels, product(): pl.pallas_call(product_kernel, grid=(width // TILE,), in_specs=[lhs, lhs,...  42.4 us
    ppermute x13, waiting for transfers between devices, swap(): return lax.ppermute(value, 'shard', [(i, i ^ mask) for i in range(SHARDS)])  30.4 us
    ppermute x14, starting transfers between devices, swap_rep(): return lax.ppermute(value, 'rep', [(i, i ^ mask) for i in range(REPLICAS)])  22.9 us
    ppermute x14, waiting for transfers between devices, swap_rep(): return lax.ppermute(value, 'rep', [(i, i ^ mask) for i in range(REPLICAS)])  12 us
    ppermute x13, starting transfers between devices, swap(): return lax.ppermute(value, 'shard', [(i, i ^ mask) for i in range(SHARDS)])  11.4 us
    pallas_call x3, Pallas kernels, adam(): pl.pallas_call(functools.partial(adam_kernel, len(chain)), grid_spec=pltp...  10.7 us
    slice x2, local copies, waits for them, and re-layouts, body(): grads_far = [swap(out_grad[:, c:c + w], CORE) for c, w, _ in CHUNKS]  10.4 us
    pallas_call x2, Pallas kernels, last(): pl.pallas_call(functools.partial(last_kernel, len(chain)), grid_spec=pltp...  8.62 us
  transfers between devices with their start and end apart: 27, of which 9 were waited for; matrix products, arithmetic and copies ran while one was open for 4% of the time, Pallas kernels for 37%

profile of v1, /device:TPU:0, one launch (start us, length us, event | category | flops | bytes accessed | tf_op | source)
XLA Modules:
  0.0 158.1 jit_solution(149688919222349360)
XLA Ops:
  0.6 6.6 %fusion.15 = (bf16[1024,1792]{1,0:T(8,128)(2,1)}, bf16[1024,1792]{1,0:T(8,128)(2,1)}) fusion(bf16[1024,5120]{1,0:T(8,128)(2,1)} %right_ref.11), kind=kLoop, calls=%fused_computation.40 | loop fusion | bytes 14680064 | tf_op jit(solution)/shard_map/slice | solution.py:235
  7.3 0.0 collective-permute-start.5
  7.3 0.5 collective-permute-start.9
  7.8 3.7 %slice.87 = bf16[1024,1536]{1,0:T(8,128)(2,1)} slice(bf16[1024,5120]{1,0:T(8,128)(2,1)} %right_ref.11), slice={[0:1024], [3584:5120]} | slice | bytes 6291456 | tf_op jit(solution)/shard_map/slice | solution.py:235
  11.5 0.0 collective-permute-start.1
  11.5 0.1 pad_add_fusion.place
  11.6 1.9 %copy-done.4 = bf16[1024,1536]{1,0:T(8,128)(2,1)S(1)} copy-done((bf16[1024,1536]{1,0:T(8,128)(2,1)S(1)}, bf16[1024,1536]{1,0:T(8,128)(2,1)}, u32[]{:S(2)}) %copy-start.4) | copy-done | bytes 3145752
  13.5 2.2 %turn.1 = (bf16[2,2,2,96,1024]{4,3,2,1,0:T(8,128)(2,1)S(1)}, bf16[2,2,2,96,1024]{4,3,2,1,0:T(8,128)(2,1)S(1)}) custom-call(s32[2]{0:T(128)S(1)} %pad_add_fusion.place, bf16[1024,1536]{1,0:T(8,128)(2,1)S(1)} %copy-done.4), custom_call_target="tpu_custom_call" | custom-call | bytes 6291456 | tf_op jit(solution)/shard_map/turn/pallas_call | solution.py:69
  15.7 0.6 collective-permute-start
  16.3 7.1 %collective-permute-done.left_far_ref = bf16[2,2,2,96,1024]{4,3,2,1,0:T(8,128)(2,1)S(1)} collective-permute-done((bf16[2,2,2,96,1024]{4,3,2,1,0:T(8,128)(2,1)S(1)}, bf16[2,2,2,96,1024]{4,3,2,1,0:T(8,128)(2,1)S(1)}, u32[]{:S(2)}, u32[]{:S(2)}) %collective-permute-start) | collective-permute-done | bytes 1572896 | tf_op jit(solution)/shard_map/ppermute | solution.py:41
  23.4 8.1 %product.9 = bf16[2,2,96,1792]{3,2,1,0:T(8,128)(2,1)} custom-call(bf16[2,2,2,96,1024]{4,3,2,1,0:T(8,128)(2,1)S(1)} %get-tuple-element.28.left_ref, bf16[2,2,2,96,1024]{4,3,2,1,0:T(8,128)(2,1)S(1)} %collective-permute-done.left_far_ref, bf16[1024,5120]{1,0:T(8,128)(2,1)} %right_ref.11, bf16[1024,1792]{1,0:T(8,128)(2,1)} %collective-permute-done.5.right_far_ref), custom_call_target="tpu_custom_call" | custom-call | flops 2818572288 | bytes 10289152 | tf_op jit(solution)/shard_map/product/pallas_call | solution.py:102
  31.6 1.7 %collective-permute-start.6 = (bf16[2,2,96,1792]{3,2,1,0:T(8,128)(2,1)}, bf16[2,2,96,1792]{3,2,1,0:T(8,128)(2,1)}, u32[]{:S(2)}, u32[]{:S(2)}) collective-permute-start(bf16[2,2,96,1792]{3,2,1,0:T(8,128)(2,1)} %product.9), channel_id=1, source_target_pairs={{0,4},{1,5},{2,6},{3,7},{4,0},{5,1},{6,2},{7,3},{8,12},{9,13},{10,... | collective-permute-start | bytes 4128776 | tf_op jit(solution)/shard_map/ppermute | solution.py:41
  33.2 7.2 %product.11 = bf16[2,2,96,1792]{3,2,1,0:T(8,128)(2,1)S(1)} custom-call(bf16[2,2,2,96,1024]{4,3,2,1,0:T(8,128)(2,1)S(1)} %get-tuple-element.28.left_ref, bf16[2,2,2,96,1024]{4,3,2,1,0:T(8,128)(2,1)S(1)} %collective-permute-done.left_far_ref, bf16[1024,5120]{1,0:T(8,128)(2,1)} %right_ref.11, bf16[1024,1792]{1,0:T(8,128)(2,1)} %collective-permute-done.9.right_far_ref), custom_call_target="tpu_custom_call" | custom-call | flops 2818572288 | bytes 10289152 | tf_op jit(solution)/shard_map/product/pallas_call | solution.py:102
  40.5 1.6 collective-permute-start.10
  42.0 6.2 %product.7 = bf16[2,2,96,1536]{3,2,1,0:T(8,128)(2,1)S(1)} custom-call(bf16[2,2,2,96,1024]{4,3,2,1,0:T(8,128)(2,1)S(1)} %get-tuple-element.28.left_ref, bf16[2,2,2,96,1024]{4,3,2,1,0:T(8,128)(2,1)S(1)} %collective-permute-done.left_far_ref, bf16[1024,5120]{1,0:T(8,128)(2,1)} %right_ref.11, bf16[1024,1536]{1,0:T(8,128)(2,1)} %collective-permute-done.1.right_far_ref), custom_call_target="tpu_custom_call" | custom-call | flops 2415919104 | bytes 9043968 | tf_op jit(solution)/shard_map/product/pallas_call | solution.py:102
  48.3 2.3 %collective-permute-start.2 = (bf16[2,2,96,1536]{3,2,1,0:T(8,128)(2,1)S(1)}, bf16[2,2,96,1536]{3,2,1,0:T(8,128)(2,1)S(1)}, u32[]{:S(2)}, u32[]{:S(2)}) collective-permute-start(bf16[2,2,96,1536]{3,2,1,0:T(8,128)(2,1)S(1)} %product.7), channel_id=1, source_target_pairs={{0,12},{1,13},{2,14},{3,15},{4,8},{5,9},{6,10},{7,11},{8,4},{9,5},... | collective-permute-start | bytes 3538952 | tf_op jit(solution)/shard_map/ppermute | solution.py:41
  50.5 6.2 %product.6 = bf16[2,2,96,1536]{3,2,1,0:T(8,128)(2,1)S(1)} custom-call(bf16[2,2,2,96,1024]{4,3,2,1,0:T(8,128)(2,1)S(1)} %get-tuple-element.28.left_ref, bf16[2,2,2,96,1024]{4,3,2,1,0:T(8,128)(2,1)S(1)} %collective-permute-done.left_far_ref, bf16[1024,5120]{1,0:T(8,128)(2,1)} %right_ref.11, bf16[1024,1536]{1,0:T(8,128)(2,1)} %collective-permute-done.1.right_far_ref), custom_call_target="tpu_custom_call" | custom-call | flops 2415919104 | bytes 9043968 | tf_op jit(solution)/shard_map/product/pallas_call | solution.py:102
  56.7 7.3 %product.8 = bf16[2,2,96,1792]{3,2,1,0:T(8,128)(2,1)S(1)} custom-call(bf16[2,2,2,96,1024]{4,3,2,1,0:T(8,128)(2,1)S(1)} %get-tuple-element.28.left_ref, bf16[2,2,2,96,1024]{4,3,2,1,0:T(8,128)(2,1)S(1)} %collective-permute-done.left_far_ref, bf16[1024,5120]{1,0:T(8,128)(2,1)} %right_ref.11, bf16[1024,1792]{1,0:T(8,128)(2,1)} %collective-permute-done.5.right_far_ref), custom_call_target="tpu_custom_call" | custom-call | flops 2818572288 | bytes 10289152 | tf_op jit(solution)/shard_map/product/pallas_call | solution.py:102
  64.1 7.2 %product.10 = bf16[2,2,96,1792]{3,2,1,0:T(8,128)(2,1)S(1)} custom-call(bf16[2,2,2,96,1024]{4,3,2,1,0:T(8,128)(2,1)S(1)} %get-tuple-element.28.left_ref, bf16[2,2,2,96,1024]{4,3,2,1,0:T(8,128)(2,1)S(1)} %collective-permute-done.left_far_ref, bf16[1024,5120]{1,0:T(8,128)(2,1)} %right_ref.11, bf16[1024,1792]{1,0:T(8,128)(2,1)} %collective-permute-done.9.right_far_ref), custom_call_target="tpu_custom_call" | custom-call | flops 2818572288 | bytes 10289152 | tf_op jit(solution)/shard_map/product/pallas_call | solution.py:102
  71.3 1.6 %add_convert_fusion.3 = (bf16[2,1,96,1792]{3,2,1,0:T(8,128)(2,1)S(1)}, bf16[2,96,1792]{2,1,0:T(8,128)(2,1)S(1)}) fusion(bf16[2,2,96,1792]{3,2,1,0:T(8,128)(2,1)} %collective-permute-done.6, bf16[2,2,96,1792]{3,2,1,0:T(8,128)(2,1)S(1)} %product.8), kind=kLoop, calls=%fused_computation.3 | loop fusion | flops 2752512 | bytes 4128768 | tf_op jit(solution)/shard_map/convert_element_type | solution.py:221
  73.0 1.1 collective-permute-start.7
  74.1 0.3 add_convert_fusion.1
  74.4 0.1 collective-permute-start.11
  74.5 3.3 %collective-permute-done.2 = bf16[2,2,96,1536]{3,2,1,0:T(8,128)(2,1)S(1)} collective-permute-done((bf16[2,2,96,1536]{3,2,1,0:T(8,128)(2,1)S(1)}, bf16[2,2,96,1536]{3,2,1,0:T(8,128)(2,1)S(1)}, u32[]{:S(2)}, u32[]{:S(2)}) %collective-permute-start.2) | collective-permute-done | bytes 1179680 | tf_op jit(solution)/shard_map/ppermute | solution.py:41
  77.8 0.3 add_convert_fusion.5
  78.1 0.6 collective-permute-start.3
  78.7 13.1 %collective-permute-done.7 = bf16[2,96,1792]{2,1,0:T(8,128)(2,1)S(1)} collective-permute-done((bf16[2,96,1792]{2,1,0:T(8,128)(2,1)S(1)}, bf16[2,96,1792]{2,1,0:T(8,128)(2,1)S(1)}, u32[]{:S(2)}, u32[]{:S(2)}) %collective-permute-start.7) | collective-permute-done | bytes 688160 | tf_op jit(solution)/shard_map/ppermute | solution.py:41
  91.7 0.2 fusion.10
  91.9 0.6 collective-permute-start.8
  92.5 0.2 fusion.12
  92.7 2.3 %collective-permute-start.12 = (bf16[96,1792]{1,0:T(8,128)(2,1)S(1)}, bf16[96,1792]{1,0:T(8,128)(2,1)S(1)}, u32[]{:S(2)}, u32[]{:S(2)}) collective-permute-start(bf16[96,1792]{1,0:T(8,128)(2,1)S(1)} %get-tuple-element.60), channel_id=1, source_target_pairs={{0,12},{1,13},{2,14},{3,15},{4,8},{5,9},{6,10},{7,11},{8,4},{9,5},... | collective-permute-start | bytes 1032200 | tf_op jit(solution)/shard_map/ppermute | solution.py:41
  95.0 0.1 fusion.14
  95.1 0.0 copy-start
  95.1 0.1 collective-permute-start.4
  95.2 0.2 broadcast_in_dim.3
  95.4 0.5 copy-done.5
  95.9 7.0 %collective-permute-done.12.refs_1_ = bf16[96,1792]{1,0:T(8,128)(2,1)S(1)} collective-permute-done((bf16[96,1792]{1,0:T(8,128)(2,1)S(1)}, bf16[96,1792]{1,0:T(8,128)(2,1)S(1)}, u32[]{:S(2)}, u32[]{:S(2)}) %collective-permute-start.12) | collective-permute-done | bytes 344096 | tf_op jit(solution)/shard_map/ppermute | solution.py:41
  102.9 3.7 %adam.3 = (bf16[1,96,5120]{2,1,0:T(8,128)(2,1)}, bf16[1,96,5120]{2,1,0:T(8,128)(2,1)}, bf16[24,1792]{1,0:T(8,128)(2,1)S(1)}, bf16[24,1792]{1,0:T(8,128)(2,1)S(1)...) custom-call(s32[2]{0:T(128)S(1)} %pad_add_fusion.place, bf16[96,1792]{1,0:T(8,128)(2,1)S(1)} %get-tuple-element.61.refs_0_, ...), custom_call_target="tpu_custom_call" | custom-call | flops 3440640 | bytes 4128768 | tf_op jit(solution)/shard_map/adam/pallas_call | solution.py:163
  106.7 3.9 %collective-permute-start.22 = (bf16[24,1792]{1,0:T(8,128)(2,1)S(1)}, bf16[24,1792]{1,0:T(8,128)(2,1)S(1)}, u32[]{:S(2)}, u32[]{:S(2)}) collective-permute-start(bf16[24,1792]{1,0:T(8,128)(2,1)S(1)} %get-tuple-element.45), channel_id=1, source_target_pairs={{0,32},{16,48},{32,0},{48,16},{64,96},{80,112},{96,64},{112,80},{1... | collective-permute-start | bytes 258056 | tf_op jit(solution)/shard_map/ppermute | solution.py:45
  110.6 0.7 collective-permute-start.21
  111.3 0.3 collective-permute-start.20
  111.6 3.7 %adam.4 = (bf16[1,96,5120]{2,1,0:T(8,128)(2,1)}, bf16[1,96,5120]{2,1,0:T(8,128)(2,1)}, bf16[24,3328]{1,0:T(8,128)(2,1)S(1)}, bf16[24,3328]{1,0:T(8,128)(2,1)S(1)...) custom-call(s32[2]{0:T(128)S(1)} %pad_add_fusion.place, ...), custom_call_target="tpu_custom_call", output_to_operand_aliasing={{0}: (8, {}), {1}: (9, {})} | custom-call | flops 3440640 | bytes 4128768 | tf_op jit(solution)/shard_map/adam/pallas_call | solution.py:163
  115.3 3.2 %adam.5 = (bf16[1,96,5120]{2,1,0:T(8,128)(2,1)}, bf16[1,96,5120]{2,1,0:T(8,128)(2,1)}, bf16[24,3328]{1,0:T(8,128)(2,1)S(1)}, bf16[24,3328]{1,0:T(8,128)(2,1)S(1)...) custom-call(s32[2]{0:T(128)S(1)} %pad_add_fusion.place, ...), custom_call_target="tpu_custom_call", output_to_operand_aliasing={{0}: (8, {}), {1}: (9, {}), {2}: (10, {}), {3}: (11, {}), {... | custom-call | flops 2949120 | bytes 3538944 | tf_op jit(solution)/shard_map/adam/pallas_call | solution.py:163
  118.5 3.7 %collective-permute-start.15 = (bf16[24,3328]{1,0:T(8,128)(2,1)S(1)}, bf16[24,3328]{1,0:T(8,128)(2,1)S(1)}, u32[]{:S(2)}, u32[]{:S(2)}) collective-permute-start(bf16[24,3328]{1,0:T(8,128)(2,1)S(1)} %get-tuple-element.41), channel_id=1, source_target_pairs={{0,32},{16,48},{32,0},{48,16},{64,96},{80,112},{96,64},{112,80},{1... | collective-permute-start | bytes 479240 | tf_op jit(solution)/shard_map/ppermute | solution.py:45
  122.2 0.7 collective-permute-start.14
  122.9 0.0 collective-permute-start.13
  122.9 0.1 add_convert_fusion.9
  123.0 3.1 %collective-permute-start.23 = (bf16[24,1792]{1,0:T(8,128)(2,1)S(1)}, bf16[24,1792]{1,0:T(8,128)(2,1)S(1)}, u32[]{:S(2)}, u32[]{:S(2)}) collective-permute-start(bf16[24,1792]{1,0:T(8,128)(2,1)S(1)} %add_convert_fusion.9), channel_id=1, source_target_pairs={{0,64},{16,80},{32,96},{48,112},{64,0},{80,16},{96,32},{112,48},{1... | collective-permute-start | bytes 258056 | tf_op jit(solution)/shard_map/ppermute | solution.py:45
  126.1 0.8 collective-permute-done.15
  126.9 1.8 %collective-permute-done.14 = bf16[24,3328]{1,0:T(8,128)(2,1)S(1)} collective-permute-done((bf16[24,3328]{1,0:T(8,128)(2,1)S(1)}, bf16[24,3328]{1,0:T(8,128)(2,1)S(1)}, u32[]{:S(2)}, u32[]{:S(2)}) %collective-permute-start.14) | collective-permute-done | bytes 159776 | tf_op jit(solution)/shard_map/ppermute | solution.py:45
  128.7 0.1 add_convert_fusion.7
  128.8 3.1 %collective-permute-start.16 = (bf16[24,3328]{1,0:T(8,128)(2,1)S(1)}, bf16[24,3328]{1,0:T(8,128)(2,1)S(1)}, u32[]{:S(2)}, u32[]{:S(2)}) collective-permute-start(bf16[24,3328]{1,0:T(8,128)(2,1)S(1)} %add_convert_fusion.7), channel_id=1, source_target_pairs={{0,64},{16,80},{32,96},{48,112},{64,0},{80,16},{96,32},{112,48},{1... | collective-permute-start | bytes 479240 | tf_op jit(solution)/shard_map/ppermute | solution.py:45
  131.9 0.6 collective-permute-start.24
  132.6 3.1 %collective-permute-done.16 = bf16[24,3328]{1,0:T(8,128)(2,1)S(1)} collective-permute-done((bf16[24,3328]{1,0:T(8,128)(2,1)S(1)}, bf16[24,3328]{1,0:T(8,128)(2,1)S(1)}, u32[]{:S(2)}, u32[]{:S(2)}) %collective-permute-start.16) | collective-permute-done | bytes 159776 | tf_op jit(solution)/shard_map/ppermute | solution.py:45
  135.7 0.6 collective-permute-start.17
  136.3 2.9 %collective-permute-start.18 = (bf16[24,3328]{1,0:T(8,128)(2,1)S(1)}, bf16[24,3328]{1,0:T(8,128)(2,1)S(1)}, u32[]{:S(2)}, u32[]{:S(2)}) collective-permute-start(bf16[24,3328]{1,0:T(8,128)(2,1)S(1)} %add_convert_fusion.6.p0), channel_id=1, source_target_pairs={{0,32},{16,48},{32,0},{48,16},{64,96},{80,112},{96,64},{112,80},{1... | collective-permute-start | bytes 479240 | tf_op jit(solution)/shard_map/ppermute | solution.py:45
  139.3 1.2 collective-permute-start.19
  140.5 0.3 collective-permute-start.25
  140.8 1.7 %collective-permute-start.26 = (bf16[24,1792]{1,0:T(8,128)(2,1)S(1)}, bf16[24,1792]{1,0:T(8,128)(2,1)S(1)}, u32[]{:S(2)}, u32[]{:S(2)}) collective-permute-start(bf16[24,1792]{1,0:T(8,128)(2,1)S(1)} %add_convert_fusion.8.p0), channel_id=1, source_target_pairs={{0,48},{16,32},{32,16},{48,0},{64,112},{80,96},{96,80},{112,64},{1... | collective-permute-start | bytes 258056 | tf_op jit(solution)/shard_map/ppermute | solution.py:45
  142.5 4.0 %collective-permute-done.25.p2 = bf16[24,1792]{1,0:T(8,128)(2,1)S(1)} collective-permute-done((bf16[24,1792]{1,0:T(8,128)(2,1)S(1)}, bf16[24,1792]{1,0:T(8,128)(2,1)S(1)}, u32[]{:S(2)}, u32[]{:S(2)}) %collective-permute-start.25) | collective-permute-done | bytes 86048 | tf_op jit(solution)/shard_map/ppermute | solution.py:45
  146.5 2.2 %collective-permute-done.26.p3 = bf16[24,1792]{1,0:T(8,128)(2,1)S(1)} collective-permute-done((bf16[24,1792]{1,0:T(8,128)(2,1)S(1)}, bf16[24,1792]{1,0:T(8,128)(2,1)S(1)}, u32[]{:S(2)}, u32[]{:S(2)}) %collective-permute-start.26) | collective-permute-done | bytes 86048 | tf_op jit(solution)/shard_map/ppermute | solution.py:45
  148.8 3.3 %last.2 = (f32[96,5120]{1,0:T(8,128)}, f32[96,5120]{1,0:T(8,128)S(1)}) custom-call(s32[2]{0:T(128)S(1)} %pad_add_fusion.place, bf16[24,1792]{1,0:T(8,128)(2,1)S(1)} %add_convert_fusion.8.p0, bf16[24,1792]{1,0:T(8,128)(2,1)S(1)} %collective-permute-done.24.p1, bf16[24,1792]{1,0:T(8,128)(2,1)S(1)} %collective-permute-done.25.p2, ...), custom_call_target="tpu_custom_call" | custom-call | flops 344064 | bytes 2408448 | tf_op jit(solution)/shard_map/last/pallas_call | solution.py:200
  152.1 5.3 %last.3 = (f32[96,5120]{1,0:T(8,128)}, f32[96,5120]{1,0:T(8,128)S(1)}) custom-call(s32[2]{0:T(128)S(1)} %pad_add_fusion.place, bf16[24,3328]{1,0:T(8,128)(2,1)S(1)} %add_convert_fusion.6.p0, bf16[24,3328]{1,0:T(8,128)(2,1)S(1)} %collective-permute-done.17.p1, ...), custom_call_target="tpu_custom_call", output_to_operand_aliasing={{0}: (6, {}), {1}: (7, {})} | custom-call | flops 638976 | bytes 4472832 | tf_op jit(solution)/shard_map/last/pallas_call | solution.py:200
  157.4 0.7 multiply_add_fusion
  (30 shorter events, 0.2 us)
Async XLA Ops:
  7.3 16.2 %collective-permute-start.5 = (bf16[1024,1792]{1,0:T(8,128)(2,1)}, bf16[1024,1792]{1,0:T(8,128)(2,1)}, u32[]{:S(2)}, u32[]{:S(2)}) collective-permute-start(bf16[1024,1792]{1,0:T(8,128)(2,1)} %get-tuple-element.53), channel_id=1, source_target_pairs={{0,1},{1,0},{2,3},{3,2},{4,5},{5,4},{6,7},{7,6},{8,9},{9,8},{10,11... | collective-permute-start | bytes 11010056 | tf_op jit(solution)/shard_map/ppermute | solution.py:41
  7.3 26.0 %collective-permute-start.9 = (bf16[1024,1792]{1,0:T(8,128)(2,1)}, bf16[1024,1792]{1,0:T(8,128)(2,1)}, u32[]{:S(2)}, u32[]{:S(2)}) collective-permute-start(bf16[1024,1792]{1,0:T(8,128)(2,1)} %get-tuple-element.52), channel_id=1, source_target_pairs={{0,1},{1,0},{2,3},{3,2},{4,5},{5,4},{6,7},{7,6},{8,9},{9,8},{10,11... | collective-permute-start | bytes 11010056 | tf_op jit(solution)/shard_map/ppermute | solution.py:41
  11.5 30.5 %collective-permute-start.1 = (bf16[1024,1536]{1,0:T(8,128)(2,1)}, bf16[1024,1536]{1,0:T(8,128)(2,1)}, u32[]{:S(2)}, u32[]{:S(2)}) collective-permute-start(bf16[1024,1536]{1,0:T(8,128)(2,1)} %slice.87), channel_id=1, source_target_pairs={{0,1},{1,0},{2,3},{3,2},{4,5},{5,4},{6,7},{7,6},{8,9},{9,8},{10,11... | collective-permute-start | bytes 9437192 | tf_op jit(solution)/shard_map/ppermute | solution.py:41
  11.6 1.9 %copy-start.4 = (bf16[1024,1536]{1,0:T(8,128)(2,1)S(1)}, bf16[1024,1536]{1,0:T(8,128)(2,1)}, u32[]{:S(2)}) copy-start(bf16[1024,1536]{1,0:T(8,128)(2,1)} %hidden_ref.1) | copy-start | bytes 9437188
  15.7 7.7 %collective-permute-start = (bf16[2,2,2,96,1024]{4,3,2,1,0:T(8,128)(2,1)S(1)}, bf16[2,2,2,96,1024]{4,3,2,1,0:T(8,128)(2,1)S(1)}, u32[]{:S(2)}, u32[]{:S(2)}) collective-permute-start(bf16[2,2,2,96,1024]{4,3,2,1,0:T(8,128)(2,1)S(1)} %get-tuple-element.29), channel_id=1, source_target_pairs={{0,1},{1,0},{2,3},{3,2},{4,5},{5,4},{6,7},{7,6},{8,9},{9,8},{10,11... | collective-permute-start | bytes 4718600 | tf_op jit(solution)/shard_map/ppermute | solution.py:41
  31.6 39.8 %collective-permute-start.6 = (bf16[2,2,96,1792]{3,2,1,0:T(8,128)(2,1)}, bf16[2,2,96,1792]{3,2,1,0:T(8,128)(2,1)}, u32[]{:S(2)}, u32[]{:S(2)}) collective-permute-start(bf16[2,2,96,1792]{3,2,1,0:T(8,128)(2,1)} %product.9), channel_id=1, source_target_pairs={{0,4},{1,5},{2,6},{3,7},{4,0},{5,1},{6,2},{7,3},{8,12},{9,13},{10,... | collective-permute-start | bytes 4128776 | tf_op jit(solution)/shard_map/ppermute | solution.py:41
  40.5 33.6 %collective-permute-start.10 = (bf16[2,2,96,1792]{3,2,1,0:T(8,128)(2,1)S(1)}, bf16[2,2,96,1792]{3,2,1,0:T(8,128)(2,1)S(1)}, u32[]{:S(2)}, u32[]{:S(2)}) collective-permute-start(bf16[2,2,96,1792]{3,2,1,0:T(8,128)(2,1)S(1)} %product.11), channel_id=1, source_target_pairs={{0,2},{1,3},{2,0},{3,1},{4,6},{5,7},{6,4},{7,5},{8,10},{9,11},{10,... | collective-permute-start | bytes 4128776 | tf_op jit(solution)/shard_map/ppermute | solution.py:41
  48.3 29.5 %collective-permute-start.2 = (bf16[2,2,96,1536]{3,2,1,0:T(8,128)(2,1)S(1)}, bf16[2,2,96,1536]{3,2,1,0:T(8,128)(2,1)S(1)}, u32[]{:S(2)}, u32[]{:S(2)}) collective-permute-start(bf16[2,2,96,1536]{3,2,1,0:T(8,128)(2,1)S(1)} %product.7), channel_id=1, source_target_pairs={{0,12},{1,13},{2,14},{3,15},{4,8},{5,9},{6,10},{7,11},{8,4},{9,5},... | collective-permute-start | bytes 3538952 | tf_op jit(solution)/shard_map/ppermute | solution.py:41
  73.0 18.8 %collective-permute-start.7 = (bf16[2,96,1792]{2,1,0:T(8,128)(2,1)S(1)}, bf16[2,96,1792]{2,1,0:T(8,128)(2,1)S(1)}, u32[]{:S(2)}, u32[]{:S(2)}) collective-permute-start(bf16[2,96,1792]{2,1,0:T(8,128)(2,1)S(1)} %get-tuple-element.57), channel_id=1, source_target_pairs={{0,12},{1,13},{2,14},{3,15},{4,8},{5,9},{6,10},{7,11},{8,4},{9,5},... | collective-permute-start | bytes 2064392 | tf_op jit(solution)/shard_map/ppermute | solution.py:41
  74.4 18.1 %collective-permute-start.11 = (bf16[2,96,1792]{2,1,0:T(8,128)(2,1)S(1)}, bf16[2,96,1792]{2,1,0:T(8,128)(2,1)S(1)}, u32[]{:S(2)}, u32[]{:S(2)}) collective-permute-start(bf16[2,96,1792]{2,1,0:T(8,128)(2,1)S(1)} %get-tuple-element.55), channel_id=1, source_target_pairs={{0,4},{1,5},{2,6},{3,7},{4,0},{5,1},{6,2},{7,3},{8,12},{9,13},{10,... | collective-permute-start | bytes 2064392 | tf_op jit(solution)/shard_map/ppermute | solution.py:41
  78.1 16.9 %collective-permute-start.3 = (bf16[2,96,1536]{2,1,0:T(8,128)(2,1)S(1)}, bf16[2,96,1536]{2,1,0:T(8,128)(2,1)S(1)}, u32[]{:S(2)}, u32[]{:S(2)}) collective-permute-start(bf16[2,96,1536]{2,1,0:T(8,128)(2,1)S(1)} %get-tuple-element.59), channel_id=1, source_target_pairs={{0,2},{1,3},{2,0},{3,1},{4,6},{5,7},{6,4},{7,5},{8,10},{9,11},{10,... | collective-permute-start | bytes 1769480 | tf_op jit(solution)/shard_map/ppermute | solution.py:41
  91.9 19.7 %collective-permute-start.8 = (bf16[96,1792]{1,0:T(8,128)(2,1)S(1)}, bf16[96,1792]{1,0:T(8,128)(2,1)S(1)}, u32[]{:S(2)}, u32[]{:S(2)}) collective-permute-start(bf16[96,1792]{1,0:T(8,128)(2,1)S(1)} %get-tuple-element.62), channel_id=1, source_target_pairs={{0,2},{1,3},{2,0},{3,1},{4,6},{5,7},{6,4},{7,5},{8,10},{9,11},{10,... | collective-permute-start | bytes 1032200 | tf_op jit(solution)/shard_map/ppermute | solution.py:41
  92.5 10.4 %copy-start.2 = (bf16[1,96,5120]{2,1,0:T(8,128)(2,1)S(1)}, bf16[1,96,5120]{2,1,0:T(8,128)(2,1)}, u32[]{:S(2)}) copy-start(bf16[1,96,5120]{2,1,0:T(8,128)(2,1)} %refs_2_.5) | copy-start | bytes 2949124
  92.5 10.4 %copy-start.3 = (bf16[1,96,5120]{2,1,0:T(8,128)(2,1)S(1)}, bf16[1,96,5120]{2,1,0:T(8,128)(2,1)}, u32[]{:S(2)}) copy-start(bf16[1,96,5120]{2,1,0:T(8,128)(2,1)} %refs_3_.5) | copy-start | bytes 2949124
  92.7 10.2 %collective-permute-start.12 = (bf16[96,1792]{1,0:T(8,128)(2,1)S(1)}, bf16[96,1792]{1,0:T(8,128)(2,1)S(1)}, u32[]{:S(2)}, u32[]{:S(2)}) collective-permute-start(bf16[96,1792]{1,0:T(8,128)(2,1)S(1)} %get-tuple-element.60), channel_id=1, source_target_pairs={{0,12},{1,13},{2,14},{3,15},{4,8},{5,9},{6,10},{7,11},{8,4},{9,5},... | collective-permute-start | bytes 1032200 | tf_op jit(solution)/shard_map/ppermute | solution.py:41
  95.0 0.9 copy-start.5
  95.0 8.0 %copy-start.1 = (f32[1,96,5120]{2,1,0:T(8,128)S(1)}, f32[1,96,5120]{2,1,0:T(8,128)}, u32[]{:S(2)}) copy-start(f32[1,96,5120]{2,1,0:T(8,128)} %refs_4_.5) | copy-start | bytes 5898244
  95.1 7.8 %copy-start = (f32[96,5120]{1,0:T(8,128)S(1)}, f32[96,5120]{1,0:T(8,128)}, u32[]{:S(2)}) copy-start(f32[96,5120]{1,0:T(8,128)} %anchor_ref.3) | copy-start | bytes 5898244
  95.1 20.2 %collective-permute-start.4 = (bf16[96,1536]{1,0:T(8,128)(2,1)S(1)}, bf16[96,1536]{1,0:T(8,128)(2,1)S(1)}, u32[]{:S(2)}, u32[]{:S(2)}) collective-permute-start(bf16[96,1536]{1,0:T(8,128)(2,1)S(1)} %get-tuple-element.64), channel_id=1, source_target_pairs={{0,4},{1,5},{2,6},{3,7},{4,0},{5,1},{6,2},{7,3},{8,12},{9,13},{10,... | collective-permute-start | bytes 884744 | tf_op jit(solution)/shard_map/ppermute | solution.py:41
  106.7 16.2 %collective-permute-start.22 = (bf16[24,1792]{1,0:T(8,128)(2,1)S(1)}, bf16[24,1792]{1,0:T(8,128)(2,1)S(1)}, u32[]{:S(2)}, u32[]{:S(2)}) collective-permute-start(bf16[24,1792]{1,0:T(8,128)(2,1)S(1)} %get-tuple-element.45), channel_id=1, source_target_pairs={{0,32},{16,48},{32,0},{48,16},{64,96},{80,112},{96,64},{112,80},{1... | collective-permute-start | bytes 258056 | tf_op jit(solution)/shard_map/ppermute | solution.py:45
  110.6 12.4 %collective-permute-start.21 = (bf16[24,1792]{1,0:T(8,128)(2,1)S(1)}, bf16[24,1792]{1,0:T(8,128)(2,1)S(1)}, u32[]{:S(2)}, u32[]{:S(2)}) collective-permute-start(bf16[24,1792]{1,0:T(8,128)(2,1)S(1)} %get-tuple-element.44), channel_id=1, source_target_pairs={{0,48},{16,32},{32,16},{48,0},{64,112},{80,96},{96,80},{112,64},{1... | collective-permute-start | bytes 258056 | tf_op jit(solution)/shard_map/ppermute | solution.py:45
  111.3 11.7 %collective-permute-start.20 = (bf16[24,1792]{1,0:T(8,128)(2,1)S(1)}, bf16[24,1792]{1,0:T(8,128)(2,1)S(1)}, u32[]{:S(2)}, u32[]{:S(2)}) collective-permute-start(bf16[24,1792]{1,0:T(8,128)(2,1)S(1)} %get-tuple-element.43), channel_id=1, source_target_pairs={{0,16},{16,0},{32,48},{48,32},{64,80},{80,64},{96,112},{112,96},{1... | collective-permute-start | bytes 258056 | tf_op jit(solution)/shard_map/ppermute | solution.py:45
  118.5 8.4 %collective-permute-start.15 = (bf16[24,3328]{1,0:T(8,128)(2,1)S(1)}, bf16[24,3328]{1,0:T(8,128)(2,1)S(1)}, u32[]{:S(2)}, u32[]{:S(2)}) collective-permute-start(bf16[24,3328]{1,0:T(8,128)(2,1)S(1)} %get-tuple-element.41), channel_id=1, source_target_pairs={{0,32},{16,48},{32,0},{48,16},{64,96},{80,112},{96,64},{112,80},{1... | collective-permute-start | bytes 479240 | tf_op jit(solution)/shard_map/ppermute | solution.py:45
  122.2 6.5 %collective-permute-start.14 = (bf16[24,3328]{1,0:T(8,128)(2,1)S(1)}, bf16[24,3328]{1,0:T(8,128)(2,1)S(1)}, u32[]{:S(2)}, u32[]{:S(2)}) collective-permute-start(bf16[24,3328]{1,0:T(8,128)(2,1)S(1)} %get-tuple-element.40), channel_id=1, source_target_pairs={{0,48},{16,32},{32,16},{48,0},{64,112},{80,96},{96,80},{112,64},{1... | collective-permute-start | bytes 479240 | tf_op jit(solution)/shard_map/ppermute | solution.py:45
  122.9 5.8 %collective-permute-start.13 = (bf16[24,3328]{1,0:T(8,128)(2,1)S(1)}, bf16[24,3328]{1,0:T(8,128)(2,1)S(1)}, u32[]{:S(2)}, u32[]{:S(2)}) collective-permute-start(bf16[24,3328]{1,0:T(8,128)(2,1)S(1)} %get-tuple-element.39), channel_id=1, source_target_pairs={{0,16},{16,0},{32,48},{48,32},{64,80},{80,64},{96,112},{112,96},{1... | collective-permute-start | bytes 479240 | tf_op jit(solution)/shard_map/ppermute | solution.py:45
  123.0 8.9 %collective-permute-start.23 = (bf16[24,1792]{1,0:T(8,128)(2,1)S(1)}, bf16[24,1792]{1,0:T(8,128)(2,1)S(1)}, u32[]{:S(2)}, u32[]{:S(2)}) collective-permute-start(bf16[24,1792]{1,0:T(8,128)(2,1)S(1)} %add_convert_fusion.9), channel_id=1, source_target_pairs={{0,64},{16,80},{32,96},{48,112},{64,0},{80,16},{96,32},{112,48},{1... | collective-permute-start | bytes 258056 | tf_op jit(solution)/shard_map/ppermute | solution.py:45
  128.8 6.9 %collective-permute-start.16 = (bf16[24,3328]{1,0:T(8,128)(2,1)S(1)}, bf16[24,3328]{1,0:T(8,128)(2,1)S(1)}, u32[]{:S(2)}, u32[]{:S(2)}) collective-permute-start(bf16[24,3328]{1,0:T(8,128)(2,1)S(1)} %add_convert_fusion.7), channel_id=1, source_target_pairs={{0,64},{16,80},{32,96},{48,112},{64,0},{80,16},{96,32},{112,48},{1... | collective-permute-start | bytes 479240 | tf_op jit(solution)/shard_map/ppermute | solution.py:45
  131.9 8.9 %collective-permute-start.24 = (bf16[24,1792]{1,0:T(8,128)(2,1)S(1)}, bf16[24,1792]{1,0:T(8,128)(2,1)S(1)}, u32[]{:S(2)}, u32[]{:S(2)}) collective-permute-start(bf16[24,1792]{1,0:T(8,128)(2,1)S(1)} %add_convert_fusion.8.p0), channel_id=1, source_target_pairs={{0,16},{16,0},{32,48},{48,32},{64,80},{80,64},{96,112},{112,96},{1... | collective-permute-start | bytes 258056 | tf_op jit(solution)/shard_map/ppermute | solution.py:45
  135.7 16.4 %collective-permute-start.17 = (bf16[24,3328]{1,0:T(8,128)(2,1)S(1)}, bf16[24,3328]{1,0:T(8,128)(2,1)S(1)}, u32[]{:S(2)}, u32[]{:S(2)}) collective-permute-start(bf16[24,3328]{1,0:T(8,128)(2,1)S(1)} %add_convert_fusion.6.p0), channel_id=1, source_target_pairs={{0,16},{16,0},{32,48},{48,32},{64,80},{80,64},{96,112},{112,96},{1... | collective-permute-start | bytes 479240 | tf_op jit(solution)/shard_map/ppermute | solution.py:45
  136.3 15.7 %collective-permute-start.18 = (bf16[24,3328]{1,0:T(8,128)(2,1)S(1)}, bf16[24,3328]{1,0:T(8,128)(2,1)S(1)}, u32[]{:S(2)}, u32[]{:S(2)}) collective-permute-start(bf16[24,3328]{1,0:T(8,128)(2,1)S(1)} %add_convert_fusion.6.p0), channel_id=1, source_target_pairs={{0,32},{16,48},{32,0},{48,16},{64,96},{80,112},{96,64},{112,80},{1... | collective-permute-start | bytes 479240 | tf_op jit(solution)/shard_map/ppermute | solution.py:45
  139.3 12.8 %collective-permute-start.19 = (bf16[24,3328]{1,0:T(8,128)(2,1)S(1)}, bf16[24,3328]{1,0:T(8,128)(2,1)S(1)}, u32[]{:S(2)}, u32[]{:S(2)}) collective-permute-start(bf16[24,3328]{1,0:T(8,128)(2,1)S(1)} %add_convert_fusion.6.p0), channel_id=1, source_target_pairs={{0,48},{16,32},{32,16},{48,0},{64,112},{80,96},{96,80},{112,64},{1... | collective-permute-start | bytes 479240 | tf_op jit(solution)/shard_map/ppermute | solution.py:45
  140.5 6.0 %collective-permute-start.25 = (bf16[24,1792]{1,0:T(8,128)(2,1)S(1)}, bf16[24,1792]{1,0:T(8,128)(2,1)S(1)}, u32[]{:S(2)}, u32[]{:S(2)}) collective-permute-start(bf16[24,1792]{1,0:T(8,128)(2,1)S(1)} %add_convert_fusion.8.p0), channel_id=1, source_target_pairs={{0,32},{16,48},{32,0},{48,16},{64,96},{80,112},{96,64},{112,80},{1... | collective-permute-start | bytes 258056 | tf_op jit(solution)/shard_map/ppermute | solution.py:45
  140.8 7.9 %collective-permute-start.26 = (bf16[24,1792]{1,0:T(8,128)(2,1)S(1)}, bf16[24,1792]{1,0:T(8,128)(2,1)S(1)}, u32[]{:S(2)}, u32[]{:S(2)}) collective-permute-start(bf16[24,1792]{1,0:T(8,128)(2,1)S(1)} %add_convert_fusion.8.p0), channel_id=1, source_target_pairs={{0,48},{16,32},{32,16},{48,0},{64,112},{80,96},{96,80},{112,64},{1... | collective-permute-start | bytes 258056 | tf_op jit(solution)/shard_map/ppermute | solution.py:45

commit v2 on v0

v2 whole, which is shorter than its diff:
```python
import functools

import jax
import jax.numpy as jnp
from jax import lax
from jax.experimental import pallas as pl
from jax.experimental.pallas import tpu as pltpu
from jax.sharding import PartitionSpec as P

beta_first = 0.9
beta_second = 0.95
bias_first = 1.0 - 0.9**30
bias_second = 1.0 - 0.95**30
inner_rate = 0.05
decay_rate = 0.1
epsilon = 1e-08
outer_beta = 0.9
outer_rate = 0.7

pseudo_weight = 1.0 + outer_beta
moment_weight = outer_beta * outer_beta

SHARDS = 16
REPLICAS = 8
BF = jnp.bfloat16
F32 = jnp.float32
LIMIT = 20 * 1024 * 1024
LIGHT = pl.CostEstimate(flops=0, bytes_accessed=1024, transcendentals=0)

CORE = 1
MASKS = (2, 4, 12)
CHUNKS = (
    (0, 1792, (0, 1, 2)),
    (1792, 1792, (1, 2, 0)),
    (3584, 1536, (2, 0, 1)),
)
GROUPS = ((0, 1), (2,))
PLAN = (
    *(("other", n) for n in range(3)),
    *(("send", n) for n in range(3)),
    *(("keep", n) for n in range(3)),
    ("hold", 0),
    *(("fold", n) for n in range(3)),
    *(("again", n) for n in range(3)),
    *(("adam", n) for n in range(3)),
    *((kind, n) for kind in ("sum", "total", "last") for n in range(2)),
)


def swap(value, mask):
    return lax.ppermute(value, "shard", [(i, i ^ mask) for i in range(SHARDS)])


def swap_rep(value, mask):
    return lax.ppermute(value, "rep", [(i, i ^ mask) for i in range(REPLICAS)])


def params(**kw):
    return pltpu.CompilerParams(vmem_limit_bytes=LIMIT, **kw)


def turn_kernel(place, hidden_ref, grad_ref, own_ref, other_ref, held_ref, landed, turned, sems, grad_sems):
    count, step, _ = landed.shape
    strip = grad_ref.shape[0] // count

    def fetch(n):
        return pltpu.make_async_copy(hidden_ref.at[pl.ds(n * step, step)], landed.at[n], sems.at[n])

    def hold(n):
        rows = pl.ds(n * strip, strip)
        return pltpu.make_async_copy(grad_ref.at[rows], held_ref.at[rows], grad_sems.at[n])

    for n in range(count):
        fetch(n).start()
    for n in range(count):
        hold(n).start()
    me = place[0]
    for n in range(count):
        fetch(n).wait()
        turned[...] = landed[n].T.reshape(turned.shape)
        tokens = slice(n * step, (n + 1) * step)
        for bx in range(2):
            for ba in range(2):
                for bb in range(2):
                    mask = (bx * MASKS[0]) ^ (ba * MASKS[1]) ^ (bb * MASKS[2])
                    own_ref[bx, ba, bb, :, tokens] = turned[me ^ mask]
                    other_ref[bx, ba, bb, :, tokens] = turned[me ^ mask ^ CORE]
    for n in range(count):
        hold(n).wait()


def in_vmem(value):
    return pltpu.with_memory_space_constraint(value, pltpu.VMEM)


def in_hbm(value):
    return pltpu.with_memory_space_constraint(value, pltpu.HBM)


WHOLE = pl.BlockSpec(memory_space=pltpu.VMEM)
SCALARS = pl.BlockSpec(memory_space=pltpu.SMEM)


def turn(hidden, out_grad, place):
    tokens, width = hidden.shape
    rows = width // SHARDS
    step = min(256, tokens)
    steps = tokens // step
    shape = pltpu.VMEM((2, 2, 2, rows, tokens), BF)
    far = pl.BlockSpec(memory_space=pltpu.HBM)
    return pl.pallas_call(
        turn_kernel,
        in_specs=[SCALARS, far, far],
        out_specs=[WHOLE] * 3,
        scratch_shapes=[
            pltpu.VMEM((steps, step, width), BF),
            pltpu.VMEM((SHARDS, rows, step), BF),
            pltpu.SemaphoreType.DMA((steps,)),
            pltpu.SemaphoreType.DMA((steps,)),
        ],
        out_shape=[shape, shape, pltpu.VMEM(out_grad.shape, BF)],
        compiler_params=params(),
        cost_estimate=LIGHT,
        name="turn",
    )(place, in_hbm(hidden), in_hbm(out_grad))


def product_kernel(added, spot, turned, first, step, place, left_ref, right_ref, *refs):
    depth = left_ref.shape[-1]
    out_ref = refs[-1]
    left = left_ref[spot].reshape(-1, depth)
    flat = len(out_ref.shape) - 1

    def columns(t, _):
        here = pl.ds(pl.multiple_of(t * step, 128), step)
        total = jnp.dot(left, right_ref[:, pl.ds(pl.multiple_of(first + t * step, 128), step)], preferred_element_type=F32)
        total = total.reshape(*out_ref.shape[:-1], step)
        for n in range(added):
            total += refs[n][(*spot, slice(None), here)].astype(F32)
        total = total.astype(BF)
        if turned:
            for p in range(2):
                for q in range(2):
                    out_ref[q, p, :, here] = total[p, q]
        else:
            out_ref[(*(slice(None),) * flat, here)] = total
        return 0

    lax.fori_loop(0, out_ref.shape[-1] // step, columns, 0)


def product(place, left, right, first, width, order=None, bit=0, add=None):
    rows = left.shape[3]
    dim = order[0] if order else None
    turned = bool(order) and order[1] > order[2]
    spot = tuple(bit if d == dim else slice(None) for d in range(3))
    kept = (2,) * (3 if dim is None else 2)
    args = [left, right] + ([] if add is None else [add])
    return pl.pallas_call(
        functools.partial(product_kernel, int(add is not None), spot, turned, first, width // 2),
        in_specs=[SCALARS] + [WHOLE] * len(args),
        out_specs=WHOLE,
        out_shape=pltpu.VMEM((*kept, rows, width), BF),
        compiler_params=params(),
        cost_estimate=LIGHT,
        name="product",
    )(place, *(in_vmem(a) for a in args))


def adam_kernel(chained, column, group_column, place, *refs):
    mine_ref, came_ref, first_ref, second_ref, param_ref, anchor_ref, moment_ref = refs[:7]
    first_out, second_out = refs[7 + chained : 9 + chained]
    parts = refs[9 + chained : 13 + chained]
    quarters = refs[13 + chained]
    step = quarters.shape[-1]

    def columns(t, _):
        near = pl.ds(pl.multiple_of(t * step, 128), step)
        here = pl.ds(pl.multiple_of(column + t * step, 128), step)
        gradient = mine_ref[:, near].astype(F32) + came_ref[:, near].astype(F32)
        first_fresh = beta_first * first_ref[0, :, here].astype(F32) + (1.0 - beta_first) * gradient
        second_fresh = beta_second * second_ref[0, :, here].astype(F32) + (1.0 - beta_second) * gradient * gradient
        level = second_fresh * (1.0 / bias_second)
        root = level * lax.rsqrt(level)
        stepped = (1.0 - inner_rate * decay_rate) * param_ref[0, :, here]
        stepped = stepped - first_fresh * (inner_rate / bias_first) / (root + epsilon)
        first_out[0, :, here] = first_fresh.astype(BF)
        second_out[0, :, here] = second_fresh.astype(BF)
        departure = (anchor_ref[:, here] - stepped) * (pseudo_weight / REPLICAS) + moment_ref[:, here]
        quarters[...] = departure.reshape(quarters.shape)
        wide = pl.ds(pl.multiple_of(group_column + t * step, 128), step)
        for distance in range(4):
            parts[distance][:, wide] = quarters[place[1] ^ distance].astype(BF)
        return 0

    lax.fori_loop(0, mine_ref.shape[-1] // step, columns, 0)


def adam(place, grads, first, second, param, anchor, moment, column, width, before, group_column, group_width):
    rows, total_width = anchor.shape
    part = rows // 4
    part_shape = pltpu.VMEM((part, group_width), BF)
    firsts, seconds, parts = before
    chain = [(0, firsts), (1, seconds)] + [(2 + d, p) for d, p in enumerate(parts or ())]
    chain = [(o, a) for o, a in chain if a is not None]
    outs = pl.pallas_call(
        functools.partial(adam_kernel, len(chain), column, group_column),
        in_specs=[SCALARS] + [WHOLE] * (7 + len(chain)),
        out_specs=[WHOLE] * 6,
        scratch_shapes=[pltpu.VMEM((4, part, 128), F32)],
        out_shape=[pltpu.VMEM(first.shape, BF)] * 2 + [part_shape] * 4,
        input_output_aliases={8 + n: o for n, (o, _) in enumerate(chain)},
        compiler_params=params(),
        cost_estimate=LIGHT,
        name="adam",
    )(place, *(in_vmem(a) for a in (*grads, first, second, param, anchor, moment)), *(in_vmem(a) for _, a in chain))
    return outs[0], outs[1], outs[2:]


def hold_kernel(place, first, second, param, anchor, moment, *refs):
    outs, sems = refs[:5], refs[6]
    share_ref = refs[5]
    copies = [
        pltpu.make_async_copy(source, target, sems.at[n])
        for n, (source, target) in enumerate(zip((first, second, param, anchor, moment), (*outs[:4], share_ref)))
    ]
    for copy in copies:
        copy.start()
    placed = outs[4]
    width = share_ref.shape[1]
    placed[...] = jnp.zeros_like(placed)
    copies[4].wait()
    placed[:, pl.ds(pl.multiple_of(place[2] * width, 128), width)] = moment_weight * share_ref[...]
    for copy in copies[:4]:
        copy.wait()


def hold(place, first, second, param, anchor, moment):
    far = pl.BlockSpec(memory_space=pltpu.HBM)
    args = (first, second, param, anchor, moment)
    return pl.pallas_call(
        hold_kernel,
        in_specs=[SCALARS] + [far] * 5,
        out_specs=[WHOLE] * 5,
        out_shape=[pltpu.VMEM(a.shape, a.dtype) for a in args[:4]] + [pltpu.VMEM(anchor.shape, F32)],
        scratch_shapes=[pltpu.VMEM(moment.shape, F32), pltpu.SemaphoreType.DMA((5,))],
        compiler_params=params(),
        cost_estimate=LIGHT,
        name="hold",
    )(place, *(in_hbm(a) for a in args))


def last_kernel(chained, column, place, p0, p1, p2, p3, anchor_ref, *refs):
    params_out, total_out, fresh, quarters, sem = refs[chained:]
    step = quarters.shape[-1]

    def columns(t, _):
        near = pl.ds(pl.multiple_of(t * step, 128), step)
        here = pl.ds(pl.multiple_of(column + t * step, 128), step)
        for distance, piece in enumerate((p0, p1, p2, p3)):
            quarters[place[1] ^ distance] = piece[:, near].astype(F32)
        total = quarters[...].reshape(-1, step)
        fresh[:, near] = anchor_ref[:, here] - outer_rate * total
        total_out[:, here] = total.astype(BF)
        return 0

    lax.fori_loop(0, fresh.shape[-1] // step, columns, 0)
    copy = pltpu.make_async_copy(fresh, params_out.at[:, pl.ds(column, fresh.shape[-1])], sem)
    copy.start()
    copy.wait()


def last(place, pieces, anchor, column, width, before):
    rows = anchor.shape[0]
    chain = [a for a in before if a is not None]
    if chain:
        chain = [in_hbm(chain[0]), in_vmem(chain[1])]
    far = pl.BlockSpec(memory_space=pltpu.HBM)
    return pl.pallas_call(
        functools.partial(last_kernel, len(chain), column),
        in_specs=[SCALARS] + [WHOLE] * 5 + [far, WHOLE][: len(chain)],
        out_specs=[far, WHOLE],
        out_shape=[pltpu.HBM(anchor.shape, F32), pltpu.VMEM(anchor.shape, BF)],
        scratch_shapes=[
            pltpu.VMEM((rows, width), F32),
            pltpu.VMEM((4, rows // 4, 128), F32),
            pltpu.SemaphoreType.DMA(()),
        ],
        input_output_aliases={6 + n: n for n in range(len(chain))},
        compiler_params=params(),
        cost_estimate=LIGHT,
        name="last",
    )(place, *(in_vmem(p) for p in pieces), in_vmem(anchor), *chain)


def add(*values):
    total = values[0].astype(F32)
    for value in values[1:]:
        total = total + value.astype(F32)
    return total.astype(BF)


def body(hidden, out_grad, inner_params, first_moment, second_moment, anchor, outer_moment):
    me = lax.axis_index("shard")
    rep = lax.axis_index("rep")
    share = outer_moment.shape[1]
    place = jnp.stack([me, rep % 4, rep]).astype(jnp.int32)
    own, other, held = turn(hidden, out_grad, place)
    count = len(CHUNKS)
    across, kept, arrived, twice, thrice = ([None] * count for _ in range(5))
    group_of = {n: g for g, group in enumerate(GROUPS) for n in group}
    parts, sums = [None] * len(GROUPS), [None] * len(GROUPS)
    firsts = seconds = None
    result = [None, None]
    token = place

    for kind, n in PLAN:
        column, width, order = CHUNKS[n]
        if kind == "other":
            done = product(token, other, held, column, width)
            across[n] = swap(done, CORE)
        elif kind == "send":
            done = product(token, own, held, column, width, order, 1, across[n])
            arrived[n] = swap(done, MASKS[order[0]])
        elif kind == "keep":
            done = kept[n] = product(token, own, held, column, width, order, 0, across[n])
        elif kind == "hold":
            first_held, second_held, param_held, anchor_held, moment_held = hold(
                token, first_moment, second_moment, inner_params, anchor, outer_moment
            )
            done = moment_held
        elif kind == "fold":
            mine, token = lax.optimization_barrier((kept[n], token))
            done = add(mine[1], arrived[n][1])
            twice[n] = (add(mine[0], arrived[n][0]), swap(done, MASKS[order[1]]))
        elif kind == "again":
            came = twice[n][1]
            mine, token = lax.optimization_barrier((twice[n][0], token))
            done = add(mine[1], came[1])
            thrice[n] = (add(mine[0], came[0]), swap(done, MASKS[order[2]]))
        elif kind == "adam":
            group = group_of[n]
            group_column = CHUNKS[GROUPS[group][0]][0]
            group_width = sum(CHUNKS[m][1] for m in GROUPS[group])
            firsts, seconds, parts[group] = adam(
                token, thrice[n], first_held, second_held, param_held, anchor_held, moment_held,
                column, width, (firsts, seconds, parts[group]), column - group_column, group_width,
            )
            done = parts[group][0]
            if n == GROUPS[group][-1]:
                parts[group] = [done] + [swap_rep(parts[group][d], d) for d in (1, 2, 3)]
        elif kind == "sum":
            mine, token = lax.optimization_barrier((parts[n][0], token))
            done = add(mine, *parts[n][1:])
            sums[n] = (done, swap_rep(done, 4))
        elif kind == "total":
            mine, token = lax.optimization_barrier((sums[n][0], token))
            done = add(mine, sums[n][1])
            sums[n] = [done] + [swap_rep(done, d) for d in (1, 2, 3)]
        elif kind == "last":
            column = CHUNKS[GROUPS[n][0]][0]
            width = sum(CHUNKS[m][1] for m in GROUPS[n])
            result = last(token, sums[n], anchor_held, column, width, result)
            done = result[1]
        token, _ = lax.optimization_barrier((token, done))
    params_new, total = result
    total_share = lax.dynamic_slice_in_dim(total, rep * share, share, 1).astype(F32)
    moment_new = outer_beta * outer_moment + (total_share - moment_weight * outer_moment) / pseudo_weight
    return (params_new, firsts, seconds, moment_new)


def solution(mesh):
    placed = (
        P(("rep", "shard"), None),
        P(("rep", "shard"), None),
        P("rep", "shard", None),
        P("rep", "shard", None),
        P("rep", "shard", None),
        P("shard", None),
        P("shard", "rep"),
    )
    return jax.shard_map(
        body,
        mesh=mesh,
        in_specs=placed,
        out_specs=(
            P("shard", None),
            P("rep", "shard", None),
            P("rep", "shard", None),
            P("shard", "rep"),
        ),
        check_vma=False,
    )
```

time: 313 us -> 128 us (0.41)
  waiting for transfers between devices: 223 us -> 41.1 us
  Pallas kernels: 0 us -> 43.9 us
  blocking collectives: 39.2 us -> 0 us
  starting transfers between devices: 0.08 us -> 36.2 us
  matrix products: 23.3 us -> 0 us
  between operations: 14.1 us -> 0.92 us
  other arithmetic: 10.9 us -> 2.45 us
    reduce_scatter x1 -> x0, waiting for transfers between devices: 174 us -> none  [body(): lax.psum_scatter(partial_term(jnp.int32(0), lax.axis_size('shard') * grou...]
    psum x1 -> x0, waiting for transfers between devices: 48.8 us -> none  [body(): lax.psum(departure.astype(jnp.bfloat16), 'rep').astype(jnp.float32)]
    pallas_call x0 -> x16, Pallas kernels: none -> 43.9 us  [the longest x9 27 us: product(): pl.pallas_call(functools.partial(product_kernel, int(add is not None), sp...]
    ppermute x0 -> x26, waiting for transfers between devices: none -> 41.1 us  [the longest x12 30.4 us: swap(): return lax.ppermute(value, 'shard', [(i, i ^ mask) for i in range(SHARDS)])]
    all_gather x1 -> x0, blocking collectives: 39.2 us -> none  [body(): lax.all_gather(outer_moment.astype(jnp.bfloat16), 'rep', axis=1, tiled=True)]
    ppermute x0 -> x26, starting transfers between devices: none -> 36.2 us  [the longest x14 20.4 us: swap_rep(): return lax.ppermute(value, 'rep', [(i, i ^ mask) for i in range(REPLICAS)])]
    dot_general x1 -> x0, matrix products: 23.3 us -> none  [partial_term(): lax.dot_general(columns, out_grad, (((0,), (0,)), ((), ())), preferred_el...]
    broadcast_in_dim x1 -> x0, other arithmetic: 6.84 us -> none  [body(): second_out = second_list[None]]
  transfers between devices with their start and end apart: 2 -> 26, of which waited for: 2 -> 10; matrix products, arithmetic and copies ran while one was open for 0% -> 3% of each run, Pallas kernels for 0% -> 25%
where the time goes in v2:
time: 128 us; the launch traced here: 127 us
  Pallas kernels  43.9 us (34%)
  waiting for transfers between devices  41.1 us (32%)
  starting transfers between devices  36.2 us (28%)
  local copies, waits for them, and re-layouts  2.85 us (2%)
  other arithmetic  2.45 us (2%)
    ppermute x12, waiting for transfers between devices, swap(): return lax.ppermute(value, 'shard', [(i, i ^ mask) for i in range(SHARDS)])  30.4 us
    pallas_call x9, Pallas kernels, product(): pl.pallas_call(functools.partial(product_kernel, int(add is not None), sp...  27 us
    ppermute x14, starting transfers between devices, swap_rep(): return lax.ppermute(value, 'rep', [(i, i ^ mask) for i in range(REPLICAS)])  20.4 us
    ppermute x12, starting transfers between devices, swap(): return lax.ppermute(value, 'shard', [(i, i ^ mask) for i in range(SHARDS)])  15.8 us
    ppermute x14, waiting for transfers between devices, swap_rep(): return lax.ppermute(value, 'rep', [(i, i ^ mask) for i in range(REPLICAS)])  10.7 us
    pallas_call x1, Pallas kernels, turn(): pl.pallas_call(turn_kernel, in_specs=[SCALARS, far, far], out_specs=[WHOL...  5.7 us
    pallas_call x3, Pallas kernels, adam(): pl.pallas_call(functools.partial(adam_kernel, len(chain), column, group_c...  3.97 us
    pallas_call x2, Pallas kernels, last(): pl.pallas_call(functools.partial(last_kernel, len(chain), column), in_spe...  3.9 us
  transfers between devices with their start and end apart: 26, of which 10 were waited for; matrix products, arithmetic and copies ran while one was open for 3% of the time, Pallas kernels for 25%

profile of v2, /device:TPU:0, one launch (start us, length us, event | category | flops | bytes accessed | tf_op | source)
XLA Modules:
  0.0 127.5 jit_solution(2419700983094186381)
XLA Ops:
  0.6 0.1 pad_add_fusion.place
  0.7 5.7 %turn.1 = (bf16[2,2,2,96,1024]{4,3,2,1,0:T(8,128)(2,1)S(1)}, bf16[2,2,2,96,1024]{4,3,2,1,0:T(8,128)(2,1)S(1)}, bf16[1024,5120]{1,0:T(8,128)(2,1)S(1)}) custom-call(s32[3]{0:T(128)S(1)} %pad_add_fusion.place, bf16[1024,1536]{1,0:T(8,128)(2,1)} %hidden_ref.1, bf16[1024,5120]{1,0:T(8,128)(2,1)} %grad_ref.1), custom_call_target="tpu_custom_call" | custom-call | bytes 1024 | tf_op jit(solution)/shard_map/turn/pallas_call | solution.py:111
  6.4 4.3 %product.9 = bf16[2,2,2,96,1792]{4,3,2,1,0:T(8,128)(2,1)S(1)} custom-call(s32[3]{0:T(128)S(1)} %pad_add_fusion.place, bf16[2,2,2,96,1024]{4,3,2,1,0:T(8,128)(2,1)S(1)} %get-tuple-element.78.left_ref, bf16[1024,5120]{1,0:T(8,128)(2,1)S(1)} %get-tuple-element.79.right_ref), custom_call_target="tpu_custom_call" | custom-call | bytes 1024 | tf_op jit(solution)/shard_map/product/pallas_call | solution.py:159
  10.7 0.1 collective-permute-start
  10.8 4.3 %product.10 = bf16[2,2,2,96,1792]{4,3,2,1,0:T(8,128)(2,1)S(1)} custom-call(s32[3]{0:T(128)S(1)} %pad_add_fusion.place, bf16[2,2,2,96,1024]{4,3,2,1,0:T(8,128)(2,1)S(1)} %get-tuple-element.78.left_ref, bf16[1024,5120]{1,0:T(8,128)(2,1)S(1)} %get-tuple-element.79.right_ref), custom_call_target="tpu_custom_call" | custom-call | bytes 1024 | tf_op jit(solution)/shard_map/product/pallas_call | solution.py:159
  15.1 0.6 collective-permute-start.1
  15.7 3.5 %product.11 = bf16[2,2,2,96,1536]{4,3,2,1,0:T(8,128)(2,1)S(1)} custom-call(s32[3]{0:T(128)S(1)} %pad_add_fusion.place, bf16[2,2,2,96,1024]{4,3,2,1,0:T(8,128)(2,1)S(1)} %get-tuple-element.78.left_ref, bf16[1024,5120]{1,0:T(8,128)(2,1)S(1)} %get-tuple-element.79.right_ref), custom_call_target="tpu_custom_call" | custom-call | bytes 1024 | tf_op jit(solution)/shard_map/product/pallas_call | solution.py:159
  19.1 0.1 collective-permute-start.2
  19.2 0.0 collective-permute-done.refs_0_
  19.2 2.6 %product.12 = bf16[2,2,96,1792]{3,2,1,0:T(8,128)(2,1)S(1)} custom-call(s32[3]{0:T(128)S(1)} %pad_add_fusion.place, bf16[2,2,2,96,1024]{4,3,2,1,0:T(8,128)(2,1)S(1)} %get-tuple-element.83.left_ref, bf16[1024,5120]{1,0:T(8,128)(2,1)S(1)} %get-tuple-element.79.right_ref, bf16[2,2,2,96,1792]{4,3,2,1,0:T(8,128)(2,1)S(1)} %collective-permute-done.refs_0_), custom_call_target="tpu_custom_call" | custom-call | bytes 1024 | tf_op jit(solution)/shard_map/product/pallas_call | solution.py:159
  21.9 1.7 %collective-permute-start.3 = (bf16[2,2,96,1792]{3,2,1,0:T(8,128)(2,1)S(1)}, bf16[2,2,96,1792]{3,2,1,0:T(8,128)(2,1)S(1)}, u32[]{:S(2)}, u32[]{:S(2)}) collective-permute-start(bf16[2,2,96,1792]{3,2,1,0:T(8,128)(2,1)S(1)} %product.12), channel_id=1, source_target_pairs={{0,2},{1,3},{2,0},{3,1},{4,6},{5,7},{6,4},{7,5},{8,10},{9,11},{10,... | collective-permute-start | bytes 4128776 | tf_op jit(solution)/shard_map/ppermute | solution.py:51
  23.6 2.6 %product.13 = bf16[2,2,96,1792]{3,2,1,0:T(8,128)(2,1)S(1)} custom-call(s32[3]{0:T(128)S(1)} %pad_add_fusion.place, bf16[2,2,2,96,1024]{4,3,2,1,0:T(8,128)(2,1)S(1)} %get-tuple-element.83.left_ref, bf16[1024,5120]{1,0:T(8,128)(2,1)S(1)} %get-tuple-element.79.right_ref, bf16[2,2,2,96,1792]{4,3,2,1,0:T(8,128)(2,1)S(1)} %collective-permute-done.1.refs_0_), custom_call_target="tpu_custom_call" | custom-call | bytes 1024 | tf_op jit(solution)/shard_map/product/pallas_call | solution.py:159
  26.2 1.6 %collective-permute-start.4 = (bf16[2,2,96,1792]{3,2,1,0:T(8,128)(2,1)S(1)}, bf16[2,2,96,1792]{3,2,1,0:T(8,128)(2,1)S(1)}, u32[]{:S(2)}, u32[]{:S(2)}) collective-permute-start(bf16[2,2,96,1792]{3,2,1,0:T(8,128)(2,1)S(1)} %product.13), channel_id=1, source_target_pairs={{0,4},{1,5},{2,6},{3,7},{4,0},{5,1},{6,2},{7,3},{8,12},{9,13},{10,... | collective-permute-start | bytes 4128776 | tf_op jit(solution)/shard_map/ppermute | solution.py:51
  27.9 2.2 %product.14 = bf16[2,2,96,1536]{3,2,1,0:T(8,128)(2,1)S(1)} custom-call(s32[3]{0:T(128)S(1)} %pad_add_fusion.place, bf16[2,2,2,96,1024]{4,3,2,1,0:T(8,128)(2,1)S(1)} %get-tuple-element.83.left_ref, bf16[1024,5120]{1,0:T(8,128)(2,1)S(1)} %get-tuple-element.79.right_ref, bf16[2,2,2,96,1536]{4,3,2,1,0:T(8,128)(2,1)S(1)} %collective-permute-done.2.refs_0_), custom_call_target="tpu_custom_call" | custom-call | bytes 1024 | tf_op jit(solution)/shard_map/product/pallas_call | solution.py:159
  30.1 2.4 %collective-permute-start.5 = (bf16[2,2,96,1536]{3,2,1,0:T(8,128)(2,1)S(1)}, bf16[2,2,96,1536]{3,2,1,0:T(8,128)(2,1)S(1)}, u32[]{:S(2)}, u32[]{:S(2)}) collective-permute-start(bf16[2,2,96,1536]{3,2,1,0:T(8,128)(2,1)S(1)} %product.14), channel_id=1, source_target_pairs={{0,12},{1,13},{2,14},{3,15},{4,8},{5,9},{6,10},{7,11},{8,4},{9,5},... | collective-permute-start | bytes 3538952 | tf_op jit(solution)/shard_map/ppermute | solution.py:51
  32.5 2.7 %product.15 = bf16[2,2,96,1792]{3,2,1,0:T(8,128)(2,1)S(1)} custom-call(s32[3]{0:T(128)S(1)} %pad_add_fusion.place, bf16[2,2,2,96,1024]{4,3,2,1,0:T(8,128)(2,1)S(1)} %get-tuple-element.83.left_ref, bf16[1024,5120]{1,0:T(8,128)(2,1)S(1)} %get-tuple-element.79.right_ref, bf16[2,2,2,96,1792]{4,3,2,1,0:T(8,128)(2,1)S(1)} %collective-permute-done.refs_0_), custom_call_target="tpu_custom_call" | custom-call | bytes 1024 | tf_op jit(solution)/shard_map/product/pallas_call | solution.py:159
  35.2 2.6 %product.16 = bf16[2,2,96,1792]{3,2,1,0:T(8,128)(2,1)S(1)} custom-call(s32[3]{0:T(128)S(1)} %pad_add_fusion.place, bf16[2,2,2,96,1024]{4,3,2,1,0:T(8,128)(2,1)S(1)} %get-tuple-element.83.left_ref, bf16[1024,5120]{1,0:T(8,128)(2,1)S(1)} %get-tuple-element.79.right_ref, bf16[2,2,2,96,1792]{4,3,2,1,0:T(8,128)(2,1)S(1)} %collective-permute-done.1.refs_0_), custom_call_target="tpu_custom_call" | custom-call | bytes 1024 | tf_op jit(solution)/shard_map/product/pallas_call | solution.py:159
  37.8 2.2 %product.17 = bf16[2,2,96,1536]{3,2,1,0:T(8,128)(2,1)S(1)} custom-call(s32[3]{0:T(128)S(1)} %pad_add_fusion.place, bf16[2,2,2,96,1024]{4,3,2,1,0:T(8,128)(2,1)S(1)} %get-tuple-element.83.left_ref, bf16[1024,5120]{1,0:T(8,128)(2,1)S(1)} %get-tuple-element.79.right_ref, bf16[2,2,2,96,1536]{4,3,2,1,0:T(8,128)(2,1)S(1)} %collective-permute-done.2.refs_0_), custom_call_target="tpu_custom_call" | custom-call | bytes 1024 | tf_op jit(solution)/shard_map/product/pallas_call | solution.py:159
  40.0 3.3 %hold.1 = (bf16[1,96,5120]{2,1,0:T(8,128)(2,1)S(1)}, bf16[1,96,5120]{2,1,0:T(8,128)(2,1)S(1)}, f32[1,96,5120]{2,1,0:T(8,128)S(1)}, f32[96,5120]{1,0:T(8,128)S(1)}, f32[96,5120]{1,0:T(8,128)S(1)}) custom-call(s32[3]{0:T(128)S(1)} %pad_add_fusion.place, bf16[1,96,5120]{2,1,0:T(8,128)(2,1)} %first.1, bf16[1,96,5120]{2,1,0:T(8,128)(2,1)} %second.1, ...), custom_call_target="tpu_custom_call" | custom-call | bytes 1024 | tf_op jit(solution)/shard_map/hold/pallas_call | solution.py:241
  43.4 0.0 copy-start
  43.4 11.2 %collective-permute-done.3 = bf16[2,2,96,1792]{3,2,1,0:T(8,128)(2,1)S(1)} collective-permute-done((bf16[2,2,96,1792]{3,2,1,0:T(8,128)(2,1)S(1)}, bf16[2,2,96,1792]{3,2,1,0:T(8,128)(2,1)S(1)}, u32[]{:S(2)}, u32[]{:S(2)}) %collective-permute-start.3) | collective-permute-done | bytes 1376288 | tf_op jit(solution)/shard_map/ppermute | solution.py:51
  54.6 0.3 fusion.3
  54.9 1.7 %collective-permute-start.6 = (bf16[2,96,1792]{2,1,0:T(8,128)(2,1)S(1)}, bf16[2,96,1792]{2,1,0:T(8,128)(2,1)S(1)}, u32[]{:S(2)}, u32[]{:S(2)}) collective-permute-start(bf16[2,96,1792]{2,1,0:T(8,128)(2,1)S(1)} %get-tuple-element.153), channel_id=1, source_target_pairs={{0,4},{1,5},{2,6},{3,7},{4,0},{5,1},{6,2},{7,3},{8,12},{9,13},{10,... | collective-permute-start | bytes 2064392 | tf_op jit(solution)/shard_map/ppermute | solution.py:51
  56.6 2.7 %collective-permute-done.4 = bf16[2,2,96,1792]{3,2,1,0:T(8,128)(2,1)S(1)} collective-permute-done((bf16[2,2,96,1792]{3,2,1,0:T(8,128)(2,1)S(1)}, bf16[2,2,96,1792]{3,2,1,0:T(8,128)(2,1)S(1)}, u32[]{:S(2)}, u32[]{:S(2)}) %collective-permute-start.4) | collective-permute-done | bytes 1376288 | tf_op jit(solution)/shard_map/ppermute | solution.py:51
  59.3 0.3 fusion.2
  59.6 3.1 %collective-permute-start.7 = (bf16[2,96,1792]{2,1,0:T(8,128)(2,1)S(1)}, bf16[2,96,1792]{2,1,0:T(8,128)(2,1)S(1)}, u32[]{:S(2)}, u32[]{:S(2)}) collective-permute-start(bf16[2,96,1792]{2,1,0:T(8,128)(2,1)S(1)} %get-tuple-element.155), channel_id=1, source_target_pairs={{0,12},{1,13},{2,14},{3,15},{4,8},{5,9},{6,10},{7,11},{8,4},{9,5},... | collective-permute-start | bytes 2064392 | tf_op jit(solution)/shard_map/ppermute | solution.py:51
  62.7 0.3 fusion.5
  63.0 0.1 collective-permute-start.8
  63.1 10.2 %collective-permute-done.6 = bf16[2,96,1792]{2,1,0:T(8,128)(2,1)S(1)} collective-permute-done((bf16[2,96,1792]{2,1,0:T(8,128)(2,1)S(1)}, bf16[2,96,1792]{2,1,0:T(8,128)(2,1)S(1)}, u32[]{:S(2)}, u32[]{:S(2)}) %collective-permute-start.6) | collective-permute-done | bytes 688160 | tf_op jit(solution)/shard_map/ppermute | solution.py:51
  73.3 0.2 fusion.8
  73.5 3.1 %collective-permute-start.9 = (bf16[96,1792]{1,0:T(8,128)(2,1)S(1)}, bf16[96,1792]{1,0:T(8,128)(2,1)S(1)}, u32[]{:S(2)}, u32[]{:S(2)}) collective-permute-start(bf16[96,1792]{1,0:T(8,128)(2,1)S(1)} %get-tuple-element.161), channel_id=1, source_target_pairs={{0,12},{1,13},{2,14},{3,15},{4,8},{5,9},{6,10},{7,11},{8,4},{9,5},... | collective-permute-start | bytes 1032200 | tf_op jit(solution)/shard_map/ppermute | solution.py:51
  76.6 0.5 collective-permute-done.7
  77.1 0.2 fusion.9
  77.2 0.9 collective-permute-start.10
  78.2 0.1 fusion.11
  78.3 0.4 collective-permute-start.11
  78.7 5.6 %collective-permute-done.9.refs_1_ = bf16[96,1792]{1,0:T(8,128)(2,1)S(1)} collective-permute-done((bf16[96,1792]{1,0:T(8,128)(2,1)S(1)}, bf16[96,1792]{1,0:T(8,128)(2,1)S(1)}, u32[]{:S(2)}, u32[]{:S(2)}) %collective-permute-start.9) | collective-permute-done | bytes 344096 | tf_op jit(solution)/shard_map/ppermute | solution.py:51
  84.3 1.4 %adam.3 = (bf16[1,96,5120]{2,1,0:T(8,128)(2,1)S(1)}, bf16[1,96,5120]{2,1,0:T(8,128)(2,1)S(1)}, bf16[24,3584]{1,0:T(8,128)(2,1)S(1)}, bf16[24,3584]{1,0:T(8,128)(...) custom-call(s32[3]{0:T(128)S(1)} %pad_add_fusion.place, ...), custom_call_target="tpu_custom_call" | custom-call | bytes 1024 | tf_op jit(solution)/shard_map/adam/pallas_call | solution.py:206
  85.7 0.2 collective-permute-done.10.refs_1_
  85.9 1.4 %adam.4 = (bf16[1,96,5120]{2,1,0:T(8,128)(2,1)S(1)}, bf16[1,96,5120]{2,1,0:T(8,128)(2,1)S(1)}, bf16[24,3584]{1,0:T(8,128)(2,1)S(1)}, bf16[24,3584]{1,0:T(8,128)(...) custom-call(s32[3]{0:T(128)S(1)} %pad_add_fusion.place, ...), custom_call_target="tpu_custom_call", output_to_operand_aliasing={{0}: (8, {}), {1}: (9, {}), {2}: (10, {}), {3}: (11, {}), {... | custom-call | bytes 1024 | tf_op jit(solution)/shard_map/adam/pallas_call | solution.py:206
  87.2 2.0 %collective-permute-start.12 = (bf16[24,3584]{1,0:T(8,128)(2,1)S(1)}, bf16[24,3584]{1,0:T(8,128)(2,1)S(1)}, u32[]{:S(2)}, u32[]{:S(2)}) collective-permute-start(bf16[24,3584]{1,0:T(8,128)(2,1)S(1)} %get-tuple-element.129), channel_id=1, source_target_pairs={{0,16},{16,0},{32,48},{48,32},{64,80},{80,64},{96,112},{112,96},{1... | collective-permute-start | bytes 516104 | tf_op jit(solution)/shard_map/ppermute | solution.py:55
  89.3 3.6 %collective-permute-start.13 = (bf16[24,3584]{1,0:T(8,128)(2,1)S(1)}, bf16[24,3584]{1,0:T(8,128)(2,1)S(1)}, u32[]{:S(2)}, u32[]{:S(2)}) collective-permute-start(bf16[24,3584]{1,0:T(8,128)(2,1)S(1)} %get-tuple-element.130), channel_id=1, source_target_pairs={{0,32},{16,48},{32,0},{48,16},{64,96},{80,112},{96,64},{112,80},{1... | collective-permute-start | bytes 516104 | tf_op jit(solution)/shard_map/ppermute | solution.py:55
  92.9 1.3 adam.5
  94.2 0.1 collective-permute-start.15
  94.3 4.7 %collective-permute-start.16 = (bf16[24,1536]{1,0:T(8,128)(2,1)S(1)}, bf16[24,1536]{1,0:T(8,128)(2,1)S(1)}, u32[]{:S(2)}, u32[]{:S(2)}) collective-permute-start(bf16[24,1536]{1,0:T(8,128)(2,1)S(1)} %get-tuple-element.135), channel_id=1, source_target_pairs={{0,32},{16,48},{32,0},{48,16},{64,96},{80,112},{96,64},{112,80},{1... | collective-permute-start | bytes 221192 | tf_op jit(solution)/shard_map/ppermute | solution.py:55
  99.0 2.1 %collective-permute-done.13 = bf16[24,3584]{1,0:T(8,128)(2,1)S(1)} collective-permute-done((bf16[24,3584]{1,0:T(8,128)(2,1)S(1)}, bf16[24,3584]{1,0:T(8,128)(2,1)S(1)}, u32[]{:S(2)}, u32[]{:S(2)}) %collective-permute-start.13) | collective-permute-done | bytes 172064 | tf_op jit(solution)/shard_map/ppermute | solution.py:55
  101.1 2.6 %collective-permute-done.14 = bf16[24,3584]{1,0:T(8,128)(2,1)S(1)} collective-permute-done((bf16[24,3584]{1,0:T(8,128)(2,1)S(1)}, bf16[24,3584]{1,0:T(8,128)(2,1)S(1)}, u32[]{:S(2)}, u32[]{:S(2)}) %collective-permute-start.14) | collective-permute-done | bytes 172064 | tf_op jit(solution)/shard_map/ppermute | solution.py:55
  103.7 0.1 add_convert_fusion.13
  103.8 2.8 %collective-permute-start.18 = (bf16[24,3584]{1,0:T(8,128)(2,1)S(1)}, bf16[24,3584]{1,0:T(8,128)(2,1)S(1)}, u32[]{:S(2)}, u32[]{:S(2)}) collective-permute-start(bf16[24,3584]{1,0:T(8,128)(2,1)S(1)} %add_convert_fusion.13), channel_id=1, source_target_pairs={{0,64},{16,80},{32,96},{48,112},{64,0},{80,16},{96,32},{112,48},{1... | collective-permute-start | bytes 516104 | tf_op jit(solution)/shard_map/ppermute | solution.py:55
  106.7 0.9 collective-permute-start.19
  107.6 3.2 %collective-permute-done.18 = bf16[24,3584]{1,0:T(8,128)(2,1)S(1)} collective-permute-done((bf16[24,3584]{1,0:T(8,128)(2,1)S(1)}, bf16[24,3584]{1,0:T(8,128)(2,1)S(1)}, u32[]{:S(2)}, u32[]{:S(2)}) %collective-permute-start.18) | collective-permute-done | bytes 172064 | tf_op jit(solution)/shard_map/ppermute | solution.py:55
  110.8 0.7 collective-permute-start.22
  111.5 0.8 collective-permute-start.21
  112.3 2.8 %collective-permute-start.20 = (bf16[24,3584]{1,0:T(8,128)(2,1)S(1)}, bf16[24,3584]{1,0:T(8,128)(2,1)S(1)}, u32[]{:S(2)}, u32[]{:S(2)}) collective-permute-start(bf16[24,3584]{1,0:T(8,128)(2,1)S(1)} %add_convert_fusion.12.p0), channel_id=1, source_target_pairs={{0,16},{16,0},{32,48},{48,32},{64,80},{80,64},{96,112},{112,96},{1... | collective-permute-start | bytes 516104 | tf_op jit(solution)/shard_map/ppermute | solution.py:55
  115.0 0.7 collective-permute-start.25
  115.7 1.5 %collective-permute-start.24 = (bf16[24,1536]{1,0:T(8,128)(2,1)S(1)}, bf16[24,1536]{1,0:T(8,128)(2,1)S(1)}, u32[]{:S(2)}, u32[]{:S(2)}) collective-permute-start(bf16[24,1536]{1,0:T(8,128)(2,1)S(1)} %add_convert_fusion.14.p0), channel_id=1, source_target_pairs={{0,32},{16,48},{32,0},{48,16},{64,96},{80,112},{96,64},{112,80},{1... | collective-permute-start | bytes 221192 | tf_op jit(solution)/shard_map/ppermute | solution.py:55
  117.2 2.7 %collective-permute-done.22.p3 = bf16[24,3584]{1,0:T(8,128)(2,1)S(1)} collective-permute-done((bf16[24,3584]{1,0:T(8,128)(2,1)S(1)}, bf16[24,3584]{1,0:T(8,128)(2,1)S(1)}, u32[]{:S(2)}, u32[]{:S(2)}) %collective-permute-start.22) | collective-permute-done | bytes 172064 | tf_op jit(solution)/shard_map/ppermute | solution.py:55
  119.9 0.9 copy.31
  120.8 0.9 copy.32
  121.8 0.9 copy-done.1
  122.7 2.3 %last.2 = (f32[96,5120]{1,0:T(8,128)}, bf16[96,5120]{1,0:T(8,128)(2,1)S(1)}) custom-call(s32[3]{0:T(128)S(1)} %pad_add_fusion.place, bf16[24,3584]{1,0:T(8,128)(2,1)S(1)} %add_convert_fusion.12.p0, bf16[24,3584]{1,0:T(8,128)(2,1)S(1)} %collective-permute-done.20.p1, bf16[24,3584]{1,0:T(8,128)(2,1)S(1)} %collective-permute-done.21.p2, ...), custom_call_target="tpu_custom_call" | custom-call | bytes 1024 | tf_op jit(solution)/shard_map/last/pallas_call | solution.py:279
  125.0 0.0 copy-start.2
  125.0 1.6 %last.3 = (f32[96,5120]{1,0:T(8,128)}, bf16[96,5120]{1,0:T(8,128)(2,1)S(1)}) custom-call(s32[3]{0:T(128)S(1)} %pad_add_fusion.place, bf16[24,1536]{1,0:T(8,128)(2,1)S(1)} %add_convert_fusion.14.p0, bf16[24,1536]{1,0:T(8,128)(2,1)S(1)} %collective-permute-done.23.p1, ...), custom_call_target="tpu_custom_call", output_to_operand_aliasing={{0}: (6, {}), {1}: (7, {})} | custom-call | bytes 1024 | tf_op jit(solution)/shard_map/last/pallas_call | solution.py:279
  126.7 0.8 multiply_add_fusion
  (24 shorter events, 0.2 us)
Async XLA Ops:
  10.7 8.5 %collective-permute-start = (bf16[2,2,2,96,1792]{4,3,2,1,0:T(8,128)(2,1)S(1)}, bf16[2,2,2,96,1792]{4,3,2,1,0:T(8,128)(2,1)S(1)}, u32[]{:S(2)}, u32[]{:S(2)}) collective-permute-start(bf16[2,2,2,96,1792]{4,3,2,1,0:T(8,128)(2,1)S(1)} %product.9), channel_id=1, source_target_pairs={{0,1},{1,0},{2,3},{3,2},{4,5},{5,4},{6,7},{7,6},{8,9},{9,8},{10,11... | collective-permute-start | bytes 8257544 | tf_op jit(solution)/shard_map/ppermute | solution.py:51
  15.1 8.5 %collective-permute-start.1 = (bf16[2,2,2,96,1792]{4,3,2,1,0:T(8,128)(2,1)S(1)}, bf16[2,2,2,96,1792]{4,3,2,1,0:T(8,128)(2,1)S(1)}, u32[]{:S(2)}, u32[]{:S(2)}) collective-permute-start(bf16[2,2,2,96,1792]{4,3,2,1,0:T(8,128)(2,1)S(1)} %product.10), channel_id=1, source_target_pairs={{0,1},{1,0},{2,3},{3,2},{4,5},{5,4},{6,7},{7,6},{8,9},{9,8},{10,11... | collective-permute-start | bytes 8257544 | tf_op jit(solution)/shard_map/ppermute | solution.py:51
  19.1 8.7 %collective-permute-start.2 = (bf16[2,2,2,96,1536]{4,3,2,1,0:T(8,128)(2,1)S(1)}, bf16[2,2,2,96,1536]{4,3,2,1,0:T(8,128)(2,1)S(1)}, u32[]{:S(2)}, u32[]{:S(2)}) collective-permute-start(bf16[2,2,2,96,1536]{4,3,2,1,0:T(8,128)(2,1)S(1)} %product.11), channel_id=1, source_target_pairs={{0,1},{1,0},{2,3},{3,2},{4,5},{5,4},{6,7},{7,6},{8,9},{9,8},{10,11... | collective-permute-start | bytes 7077896 | tf_op jit(solution)/shard_map/ppermute | solution.py:51
  21.9 32.7 %collective-permute-start.3 = (bf16[2,2,96,1792]{3,2,1,0:T(8,128)(2,1)S(1)}, bf16[2,2,96,1792]{3,2,1,0:T(8,128)(2,1)S(1)}, u32[]{:S(2)}, u32[]{:S(2)}) collective-permute-start(bf16[2,2,96,1792]{3,2,1,0:T(8,128)(2,1)S(1)} %product.12), channel_id=1, source_target_pairs={{0,2},{1,3},{2,0},{3,1},{4,6},{5,7},{6,4},{7,5},{8,10},{9,11},{10,... | collective-permute-start | bytes 4128776 | tf_op jit(solution)/shard_map/ppermute | solution.py:51
  26.2 33.1 %collective-permute-start.4 = (bf16[2,2,96,1792]{3,2,1,0:T(8,128)(2,1)S(1)}, bf16[2,2,96,1792]{3,2,1,0:T(8,128)(2,1)S(1)}, u32[]{:S(2)}, u32[]{:S(2)}) collective-permute-start(bf16[2,2,96,1792]{3,2,1,0:T(8,128)(2,1)S(1)} %product.13), channel_id=1, source_target_pairs={{0,4},{1,5},{2,6},{3,7},{4,0},{5,1},{6,2},{7,3},{8,12},{9,13},{10,... | collective-permute-start | bytes 4128776 | tf_op jit(solution)/shard_map/ppermute | solution.py:51
  30.1 32.7 %collective-permute-start.5 = (bf16[2,2,96,1536]{3,2,1,0:T(8,128)(2,1)S(1)}, bf16[2,2,96,1536]{3,2,1,0:T(8,128)(2,1)S(1)}, u32[]{:S(2)}, u32[]{:S(2)}) collective-permute-start(bf16[2,2,96,1536]{3,2,1,0:T(8,128)(2,1)S(1)} %product.14), channel_id=1, source_target_pairs={{0,12},{1,13},{2,14},{3,15},{4,8},{5,9},{6,10},{7,11},{8,4},{9,5},... | collective-permute-start | bytes 3538952 | tf_op jit(solution)/shard_map/ppermute | solution.py:51
  43.4 49.5 %copy-start = (f32[96,5120]{1,0:T(8,128)}, f32[96,5120]{1,0:T(8,128)S(1)}, u32[]{:S(2)}) copy-start(f32[96,5120]{1,0:T(8,128)S(1)} %get-tuple-element.113.refs_5_.anchor_ref) | copy-start | bytes 5898244
  54.9 18.4 %collective-permute-start.6 = (bf16[2,96,1792]{2,1,0:T(8,128)(2,1)S(1)}, bf16[2,96,1792]{2,1,0:T(8,128)(2,1)S(1)}, u32[]{:S(2)}, u32[]{:S(2)}) collective-permute-start(bf16[2,96,1792]{2,1,0:T(8,128)(2,1)S(1)} %get-tuple-element.153), channel_id=1, source_target_pairs={{0,4},{1,5},{2,6},{3,7},{4,0},{5,1},{6,2},{7,3},{8,12},{9,13},{10,... | collective-permute-start | bytes 2064392 | tf_op jit(solution)/shard_map/ppermute | solution.py:51
  59.6 17.4 %collective-permute-start.7 = (bf16[2,96,1792]{2,1,0:T(8,128)(2,1)S(1)}, bf16[2,96,1792]{2,1,0:T(8,128)(2,1)S(1)}, u32[]{:S(2)}, u32[]{:S(2)}) collective-permute-start(bf16[2,96,1792]{2,1,0:T(8,128)(2,1)S(1)} %get-tuple-element.155), channel_id=1, source_target_pairs={{0,12},{1,13},{2,14},{3,15},{4,8},{5,9},{6,10},{7,11},{8,4},{9,5},... | collective-permute-start | bytes 2064392 | tf_op jit(solution)/shard_map/ppermute | solution.py:51
  63.0 15.2 %collective-permute-start.8 = (bf16[2,96,1536]{2,1,0:T(8,128)(2,1)S(1)}, bf16[2,96,1536]{2,1,0:T(8,128)(2,1)S(1)}, u32[]{:S(2)}, u32[]{:S(2)}) collective-permute-start(bf16[2,96,1536]{2,1,0:T(8,128)(2,1)S(1)} %get-tuple-element.156), channel_id=1, source_target_pairs={{0,2},{1,3},{2,0},{3,1},{4,6},{5,7},{6,4},{7,5},{8,10},{9,11},{10,... | collective-permute-start | bytes 1769480 | tf_op jit(solution)/shard_map/ppermute | solution.py:51
  73.5 10.9 %collective-permute-start.9 = (bf16[96,1792]{1,0:T(8,128)(2,1)S(1)}, bf16[96,1792]{1,0:T(8,128)(2,1)S(1)}, u32[]{:S(2)}, u32[]{:S(2)}) collective-permute-start(bf16[96,1792]{1,0:T(8,128)(2,1)S(1)} %get-tuple-element.161), channel_id=1, source_target_pairs={{0,12},{1,13},{2,14},{3,15},{4,8},{5,9},{6,10},{7,11},{8,4},{9,5},... | collective-permute-start | bytes 1032200 | tf_op jit(solution)/shard_map/ppermute | solution.py:51
  77.2 8.6 %collective-permute-start.10 = (bf16[96,1792]{1,0:T(8,128)(2,1)S(1)}, bf16[96,1792]{1,0:T(8,128)(2,1)S(1)}, u32[]{:S(2)}, u32[]{:S(2)}) collective-permute-start(bf16[96,1792]{1,0:T(8,128)(2,1)S(1)} %get-tuple-element.159), channel_id=1, source_target_pairs={{0,2},{1,3},{2,0},{3,1},{4,6},{5,7},{6,4},{7,5},{8,10},{9,11},{10,... | collective-permute-start | bytes 1032200 | tf_op jit(solution)/shard_map/ppermute | solution.py:51
  78.3 14.6 %collective-permute-start.11 = (bf16[96,1536]{1,0:T(8,128)(2,1)S(1)}, bf16[96,1536]{1,0:T(8,128)(2,1)S(1)}, u32[]{:S(2)}, u32[]{:S(2)}) collective-permute-start(bf16[96,1536]{1,0:T(8,128)(2,1)S(1)} %get-tuple-element.163), channel_id=1, source_target_pairs={{0,4},{1,5},{2,6},{3,7},{4,0},{5,1},{6,2},{7,3},{8,12},{9,13},{10,... | collective-permute-start | bytes 884744 | tf_op jit(solution)/shard_map/ppermute | solution.py:51
  87.2 11.7 %collective-permute-start.12 = (bf16[24,3584]{1,0:T(8,128)(2,1)S(1)}, bf16[24,3584]{1,0:T(8,128)(2,1)S(1)}, u32[]{:S(2)}, u32[]{:S(2)}) collective-permute-start(bf16[24,3584]{1,0:T(8,128)(2,1)S(1)} %get-tuple-element.129), channel_id=1, source_target_pairs={{0,16},{16,0},{32,48},{48,32},{64,80},{80,64},{96,112},{112,96},{1... | collective-permute-start | bytes 516104 | tf_op jit(solution)/shard_map/ppermute | solution.py:55
  89.3 11.8 %collective-permute-start.13 = (bf16[24,3584]{1,0:T(8,128)(2,1)S(1)}, bf16[24,3584]{1,0:T(8,128)(2,1)S(1)}, u32[]{:S(2)}, u32[]{:S(2)}) collective-permute-start(bf16[24,3584]{1,0:T(8,128)(2,1)S(1)} %get-tuple-element.130), channel_id=1, source_target_pairs={{0,32},{16,48},{32,0},{48,16},{64,96},{80,112},{96,64},{112,80},{1... | collective-permute-start | bytes 516104 | tf_op jit(solution)/shard_map/ppermute | solution.py:55
  92.9 10.8 %collective-permute-start.14 = (bf16[24,3584]{1,0:T(8,128)(2,1)S(1)}, bf16[24,3584]{1,0:T(8,128)(2,1)S(1)}, u32[]{:S(2)}, u32[]{:S(2)}) collective-permute-start(bf16[24,3584]{1,0:T(8,128)(2,1)S(1)} %get-tuple-element.131), channel_id=1, source_target_pairs={{0,48},{16,32},{32,16},{48,0},{64,112},{80,96},{96,80},{112,64},{1... | collective-permute-start | bytes 516104 | tf_op jit(solution)/shard_map/ppermute | solution.py:55
  94.2 12.4 %collective-permute-start.15 = (bf16[24,1536]{1,0:T(8,128)(2,1)S(1)}, bf16[24,1536]{1,0:T(8,128)(2,1)S(1)}, u32[]{:S(2)}, u32[]{:S(2)}) collective-permute-start(bf16[24,1536]{1,0:T(8,128)(2,1)S(1)} %get-tuple-element.134), channel_id=1, source_target_pairs={{0,16},{16,0},{32,48},{48,32},{64,80},{80,64},{96,112},{112,96},{1... | collective-permute-start | bytes 221192 | tf_op jit(solution)/shard_map/ppermute | solution.py:55
  94.3 12.4 %collective-permute-start.16 = (bf16[24,1536]{1,0:T(8,128)(2,1)S(1)}, bf16[24,1536]{1,0:T(8,128)(2,1)S(1)}, u32[]{:S(2)}, u32[]{:S(2)}) collective-permute-start(bf16[24,1536]{1,0:T(8,128)(2,1)S(1)} %get-tuple-element.135), channel_id=1, source_target_pairs={{0,32},{16,48},{32,0},{48,16},{64,96},{80,112},{96,64},{112,80},{1... | collective-permute-start | bytes 221192 | tf_op jit(solution)/shard_map/ppermute | solution.py:55
  99.0 7.7 %collective-permute-start.17 = (bf16[24,1536]{1,0:T(8,128)(2,1)S(1)}, bf16[24,1536]{1,0:T(8,128)(2,1)S(1)}, u32[]{:S(2)}, u32[]{:S(2)}) collective-permute-start(bf16[24,1536]{1,0:T(8,128)(2,1)S(1)} %get-tuple-element.136), channel_id=1, source_target_pairs={{0,48},{16,32},{32,16},{48,0},{64,112},{80,96},{96,80},{112,64},{1... | collective-permute-start | bytes 221192 | tf_op jit(solution)/shard_map/ppermute | solution.py:55
  103.8 7.0 %collective-permute-start.18 = (bf16[24,3584]{1,0:T(8,128)(2,1)S(1)}, bf16[24,3584]{1,0:T(8,128)(2,1)S(1)}, u32[]{:S(2)}, u32[]{:S(2)}) collective-permute-start(bf16[24,3584]{1,0:T(8,128)(2,1)S(1)} %add_convert_fusion.13), channel_id=1, source_target_pairs={{0,64},{16,80},{32,96},{48,112},{64,0},{80,16},{96,32},{112,48},{1... | collective-permute-start | bytes 516104 | tf_op jit(solution)/shard_map/ppermute | solution.py:55
  106.7 8.4 %collective-permute-start.19 = (bf16[24,1536]{1,0:T(8,128)(2,1)S(1)}, bf16[24,1536]{1,0:T(8,128)(2,1)S(1)}, u32[]{:S(2)}, u32[]{:S(2)}) collective-permute-start(bf16[24,1536]{1,0:T(8,128)(2,1)S(1)} %add_convert_fusion.15), channel_id=1, source_target_pairs={{0,64},{16,80},{32,96},{48,112},{64,0},{80,16},{96,32},{112,48},{1... | collective-permute-start | bytes 221192 | tf_op jit(solution)/shard_map/ppermute | solution.py:55
  110.8 9.0 %collective-permute-start.22 = (bf16[24,3584]{1,0:T(8,128)(2,1)S(1)}, bf16[24,3584]{1,0:T(8,128)(2,1)S(1)}, u32[]{:S(2)}, u32[]{:S(2)}) collective-permute-start(bf16[24,3584]{1,0:T(8,128)(2,1)S(1)} %add_convert_fusion.12.p0), channel_id=1, source_target_pairs={{0,48},{16,32},{32,16},{48,0},{64,112},{80,96},{96,80},{112,64},{1... | collective-permute-start | bytes 516104 | tf_op jit(solution)/shard_map/ppermute | solution.py:55
  111.5 10.3 %collective-permute-start.21 = (bf16[24,3584]{1,0:T(8,128)(2,1)S(1)}, bf16[24,3584]{1,0:T(8,128)(2,1)S(1)}, u32[]{:S(2)}, u32[]{:S(2)}) collective-permute-start(bf16[24,3584]{1,0:T(8,128)(2,1)S(1)} %add_convert_fusion.12.p0), channel_id=1, source_target_pairs={{0,32},{16,48},{32,0},{48,16},{64,96},{80,112},{96,64},{112,80},{1... | collective-permute-start | bytes 516104 | tf_op jit(solution)/shard_map/ppermute | solution.py:55
  112.3 9.5 %collective-permute-start.20 = (bf16[24,3584]{1,0:T(8,128)(2,1)S(1)}, bf16[24,3584]{1,0:T(8,128)(2,1)S(1)}, u32[]{:S(2)}, u32[]{:S(2)}) collective-permute-start(bf16[24,3584]{1,0:T(8,128)(2,1)S(1)} %add_convert_fusion.12.p0), channel_id=1, source_target_pairs={{0,16},{16,0},{32,48},{48,32},{64,80},{80,64},{96,112},{112,96},{1... | collective-permute-start | bytes 516104 | tf_op jit(solution)/shard_map/ppermute | solution.py:55
  115.0 10.0 %collective-permute-start.25 = (bf16[24,1536]{1,0:T(8,128)(2,1)S(1)}, bf16[24,1536]{1,0:T(8,128)(2,1)S(1)}, u32[]{:S(2)}, u32[]{:S(2)}) collective-permute-start(bf16[24,1536]{1,0:T(8,128)(2,1)S(1)} %add_convert_fusion.14.p0), channel_id=1, source_target_pairs={{0,48},{16,32},{32,16},{48,0},{64,112},{80,96},{96,80},{112,64},{1... | collective-permute-start | bytes 221192 | tf_op jit(solution)/shard_map/ppermute | solution.py:55
  115.7 9.3 %collective-permute-start.24 = (bf16[24,1536]{1,0:T(8,128)(2,1)S(1)}, bf16[24,1536]{1,0:T(8,128)(2,1)S(1)}, u32[]{:S(2)}, u32[]{:S(2)}) collective-permute-start(bf16[24,1536]{1,0:T(8,128)(2,1)S(1)} %add_convert_fusion.14.p0), channel_id=1, source_target_pairs={{0,32},{16,48},{32,0},{48,16},{64,96},{80,112},{96,64},{112,80},{1... | collective-permute-start | bytes 221192 | tf_op jit(solution)/shard_map/ppermute | solution.py:55
  119.9 5.1 %collective-permute-start.23 = (bf16[24,1536]{1,0:T(8,128)(2,1)S(1)}, bf16[24,1536]{1,0:T(8,128)(2,1)S(1)}, u32[]{:S(2)}, u32[]{:S(2)}) collective-permute-start(bf16[24,1536]{1,0:T(8,128)(2,1)S(1)} %add_convert_fusion.14.p0), channel_id=1, source_target_pairs={{0,16},{16,0},{32,48},{48,32},{64,80},{80,64},{96,112},{112,96},{1... | collective-permute-start | bytes 221192 | tf_op jit(solution)/shard_map/ppermute | solution.py:55
  120.8 1.9 %copy-start.1 = (f32[96,5120]{1,0:T(8,128)S(1)}, f32[96,5120]{1,0:T(8,128)}, u32[]{:S(2)}) copy-start(f32[96,5120]{1,0:T(8,128)} %copy-done) | copy-start | bytes 5898244
  125.0 1.7 %copy-start.2 = (f32[96,640]{1,0:T(8,128)S(1)}, f32[96,640]{1,0:T(8,128)}, u32[]{:S(2)}) copy-start(f32[96,640]{1,0:T(8,128)} %moment.1) | copy-start | bytes 737284

commit v3 on v2

--- a/solution.py
+++ b/solution.py
@@ -43,6 +43,7 @@
     *(("fold", n) for n in range(3)),
     *(("again", n) for n in range(3)),
     *(("adam", n) for n in range(3)),
+    ("store", 0),
     *((kind, n) for kind in ("sum", "total", "last") for n in range(2)),
 )
 
@@ -68,7 +69,7 @@
 
     def hold(n):
         rows = pl.ds(n * strip, strip)
-        return pltpu.make_async_copy(grad_ref.at[rows], held_ref.at[rows], grad_sems.at[n])
+        return pltpu.make_async_copy(grad_ref.at[rows, pl.ds(0, held_ref.shape[1])], held_ref.at[rows], grad_sems.at[n])
 
     for n in range(count):
         fetch(n).start()
@@ -118,22 +119,26 @@
             pltpu.SemaphoreType.DMA((steps,)),
             pltpu.SemaphoreType.DMA((steps,)),
         ],
-        out_shape=[shape, shape, pltpu.VMEM(out_grad.shape, BF)],
+        out_shape=[shape, shape, pltpu.VMEM((tokens, CHUNKS[0][1]), BF)],
         compiler_params=params(),
         cost_estimate=LIGHT,
         name="turn",
     )(place, in_hbm(hidden), in_hbm(out_grad))
 
 
-def product_kernel(added, spot, turned, first, step, place, left_ref, right_ref, *refs):
+def product_kernel(added, following, spot, turned, step, place, left_ref, right_ref, *refs):
     depth = left_ref.shape[-1]
-    out_ref = refs[-1]
+    out_ref = refs[added + int(following is not None)]
+    if following is not None:
+        grad_ref, next_ref, sem = refs[added], refs[added + 2], refs[added + 3]
+        ahead = pltpu.make_async_copy(grad_ref.at[:, pl.ds(following, next_ref.shape[1])], next_ref, sem)
+        ahead.start()
     left = left_ref[spot].reshape(-1, depth)
     flat = len(out_ref.shape) - 1
 
     def columns(t, _):
         here = pl.ds(pl.multiple_of(t * step, 128), step)
-        total = jnp.dot(left, right_ref[:, pl.ds(pl.multiple_of(first + t * step, 128), step)], preferred_element_type=F32)
+        total = jnp.dot(left, right_ref[:, here], preferred_element_type=F32)
         total = total.reshape(*out_ref.shape[:-1], step)
         for n in range(added):
             total += refs[n][(*spot, slice(None), here)].astype(F32)
@@ -147,24 +152,40 @@
         return 0
 
     lax.fori_loop(0, out_ref.shape[-1] // step, columns, 0)
-
-
-def product(place, left, right, first, width, order=None, bit=0, add=None):
+    if following is not None:
+        ahead.wait()
+
+
+def product(place, left, right, order=None, bit=0, add=None, grad=None, following=None):
     rows = left.shape[3]
+    depth, width = right.shape
     dim = order[0] if order else None
     turned = bool(order) and order[1] > order[2]
     spot = tuple(bit if d == dim else slice(None) for d in range(3))
     kept = (2,) * (3 if dim is None else 2)
     args = [left, right] + ([] if add is None else [add])
+    specs = [WHOLE] * len(args)
+    args = [in_vmem(a) for a in args]
+    outs = [pltpu.VMEM((*kept, rows, width), BF)]
+    scratch = []
+    if following is not None:
+        column, follow_width, _ = CHUNKS[following]
+        specs.append(pl.BlockSpec(memory_space=pltpu.HBM))
+        args.append(in_hbm(grad))
+        outs.append(pltpu.VMEM((depth, follow_width), BF))
+        scratch.append(pltpu.SemaphoreType.DMA(()))
+    else:
+        column = None
     return pl.pallas_call(
-        functools.partial(product_kernel, int(add is not None), spot, turned, first, width // 2),
-        in_specs=[SCALARS] + [WHOLE] * len(args),
-        out_specs=WHOLE,
-        out_shape=pltpu.VMEM((*kept, rows, width), BF),
+        functools.partial(product_kernel, int(add is not None), column, spot, turned, width // 2),
+        in_specs=[SCALARS] + specs,
+        out_specs=[WHOLE] * len(outs),
+        out_shape=outs,
+        scratch_shapes=scratch,
         compiler_params=params(),
         cost_estimate=LIGHT,
         name="product",
-    )(place, *(in_vmem(a) for a in args))
+    )(place, *args)
 
 
 def adam_kernel(chained, column, group_column, place, *refs):
@@ -250,8 +271,36 @@
     )(place, *(in_hbm(a) for a in args))
 
 
-def last_kernel(chained, column, place, p0, p1, p2, p3, anchor_ref, *refs):
-    params_out, total_out, fresh, quarters, sem = refs[chained:]
+def store_kernel(place, first, second, part, first_out, second_out, part_out, sems):
+    copies = [
+        pltpu.make_async_copy(source, target, sems.at[n])
+        for n, (source, target) in enumerate(((first, first_out), (second, second_out)))
+    ]
+    for copy in copies:
+        copy.start()
+    for copy in copies:
+        copy.wait()
+
+
+def store(place, first, second, part):
+    far = pl.BlockSpec(memory_space=pltpu.HBM)
+    return pl.pallas_call(
+        store_kernel,
+        in_specs=[SCALARS, WHOLE, WHOLE, WHOLE],
+        out_specs=[far, far, WHOLE],
+        out_shape=[pltpu.HBM(first.shape, BF)] * 2 + [pltpu.VMEM(part.shape, part.dtype)],
+        scratch_shapes=[pltpu.SemaphoreType.DMA((2,))],
+        input_output_aliases={3: 2},
+        compiler_params=params(),
+        cost_estimate=LIGHT,
+        name="store",
+    )(place, in_vmem(first), in_vmem(second), in_vmem(part))
+
+
+def last_kernel(chained, final, column, place, p0, p1, p2, p3, anchor_ref, moment_ref, *refs):
+    refs = refs[chained:]
+    params_out, total_out = refs[:2]
+    fresh, quarters, sems = refs[-3:]
     step = quarters.shape[-1]
 
     def columns(t, _):
@@ -261,36 +310,49 @@
             quarters[place[1] ^ distance] = piece[:, near].astype(F32)
         total = quarters[...].reshape(-1, step)
         fresh[:, near] = anchor_ref[:, here] - outer_rate * total
-        total_out[:, here] = total.astype(BF)
+        total_out[:, here] = total
         return 0
 
     lax.fori_loop(0, fresh.shape[-1] // step, columns, 0)
-    copy = pltpu.make_async_copy(fresh, params_out.at[:, pl.ds(column, fresh.shape[-1])], sem)
-    copy.start()
-    copy.wait()
-
-
-def last(place, pieces, anchor, column, width, before):
+    copies = [pltpu.make_async_copy(fresh, params_out.at[:, pl.ds(column, fresh.shape[-1])], sems.at[0])]
+    copies[0].start()
+    if final:
+        moment_out, moment = refs[2:4]
+        width = moment.shape[-1]
+        share = pl.ds(pl.multiple_of(place[2] * width, 128), width)
+        weighted = moment_ref[:, share]
+        pseudo = (total_out[:, share] - weighted) * (1.0 / pseudo_weight)
+        moment[...] = weighted * (outer_beta / moment_weight) + pseudo
+        copies.append(pltpu.make_async_copy(moment, moment_out, sems.at[1]))
+        copies[1].start()
+    for copy in copies:
+        copy.wait()
+
+
+def last(place, pieces, anchor, moment, column, width, before, share):
     rows = anchor.shape[0]
     chain = [a for a in before if a is not None]
     if chain:
         chain = [in_hbm(chain[0]), in_vmem(chain[1])]
     far = pl.BlockSpec(memory_space=pltpu.HBM)
+    final = share is not None
     return pl.pallas_call(
-        functools.partial(last_kernel, len(chain), column),
-        in_specs=[SCALARS] + [WHOLE] * 5 + [far, WHOLE][: len(chain)],
-        out_specs=[far, WHOLE],
-        out_shape=[pltpu.HBM(anchor.shape, F32), pltpu.VMEM(anchor.shape, BF)],
-        scratch_shapes=[
+        functools.partial(last_kernel, len(chain), final, column),
+        in_specs=[SCALARS] + [WHOLE] * 6 + [far, WHOLE][: len(chain)],
+        out_specs=[far, WHOLE] + [far] * final,
+        out_shape=[pltpu.HBM(anchor.shape, F32), pltpu.VMEM(anchor.shape, F32)]
+        + ([pltpu.HBM((rows, share), F32)] if final else []),
+        scratch_shapes=([pltpu.VMEM((rows, share), F32)] if final else [])
+        + [
             pltpu.VMEM((rows, width), F32),
             pltpu.VMEM((4, rows // 4, 128), F32),
-            pltpu.SemaphoreType.DMA(()),
+            pltpu.SemaphoreType.DMA((2,)),
         ],
-        input_output_aliases={6 + n: n for n in range(len(chain))},
+        input_output_aliases={7 + n: n for n in range(len(chain))},
         compiler_params=params(),
         cost_estimate=LIGHT,
         name="last",
-    )(place, *(in_vmem(p) for p in pieces), in_vmem(anchor), *chain)
+    )(place, *(in_vmem(a) for a in (*pieces, anchor, moment)), *chain)
 
 
 def add(*values):
@@ -303,9 +365,9 @@
 def body(hidden, out_grad, inner_params, first_moment, second_moment, anchor, outer_moment):
     me = lax.axis_index("shard")
     rep = lax.axis_index("rep")
-    share = outer_moment.shape[1]
     place = jnp.stack([me, rep % 4, rep]).astype(jnp.int32)
     own, other, held = turn(hidden, out_grad, place)
+    held = [held]
     count = len(CHUNKS)
     across, kept, arrived, twice, thrice = ([None] * count for _ in range(5))
     group_of = {n: g for g, group in enumerate(GROUPS) for n in group}
@@ -317,13 +379,16 @@
     for kind, n in PLAN:
         column, width, order = CHUNKS[n]
         if kind == "other":
-            done = product(token, other, held, column, width)
+            following = n + 1 if n + 1 < count else None
+            done, *more = product(token, other, held[n], grad=out_grad, following=following)
+            held += more
             across[n] = swap(done, CORE)
         elif kind == "send":
-            done = product(token, own, held, column, width, order, 1, across[n])
+            (done,) = product(token, own, held[n], order, 1, across[n])
             arrived[n] = swap(done, MASKS[order[0]])
         elif kind == "keep":
-            done = kept[n] = product(token, own, held, column, width, order, 0, across[n])
+            (done,) = product(token, own, held[n], order, 0, across[n])
+            kept[n] = done
         elif kind == "hold":
             first_held, second_held, param_held, anchor_held, moment_held = hold(
                 token, first_moment, second_moment, inner_params, anchor, outer_moment
@@ -349,6 +414,9 @@
             done = parts[group][0]
             if n == GROUPS[group][-1]:
                 parts[group] = [done] + [swap_rep(parts[group][d], d) for d in (1, 2, 3)]
+        elif kind == "store":
+            firsts, seconds, done = store(token, firsts, seconds, parts[n][0])
+            parts[n][0] = done
         elif kind == "sum":
             mine, token = lax.optimization_barrier((parts[n][0], token))
             done = add(mine, *parts[n][1:])
@@ -360,12 +428,11 @@
         elif kind == "last":
             column = CHUNKS[GROUPS[n][0]][0]
             width = sum(CHUNKS[m][1] for m in GROUPS[n])
-            result = last(token, sums[n], anchor_held, column, width, result)
+            share = outer_moment.shape[1] if n == len(GROUPS) - 1 else None
+            result = last(token, sums[n], anchor_held, moment_held, column, width, result, share)
             done = result[1]
         token, _ = lax.optimization_barrier((token, done))
-    params_new, total = result
-    total_share = lax.dynamic_slice_in_dim(total, rep * share, share, 1).astype(F32)
-    moment_new = outer_beta * outer_moment + (total_share - moment_weight * outer_moment) / pseudo_weight
+    params_new, _, moment_new = result
     return (params_new, firsts, seconds, moment_new)
 
 

time: 128 us -> 123 us (0.961)
  waiting for transfers between devices: 41.1 us -> 37.7 us
  local copies, waits for them, and re-layouts: 2.85 us -> 0 us
  starting transfers between devices: 36.2 us -> 38.2 us
    ppermute x14, waiting for transfers between devices: 10.7 us -> 7.26 us  [swap_rep(): return lax.ppermute(value, 'rep', [(i, i ^ mask) for i in range(REPLICAS)])]
    unnamed x8 -> x0, local copies, waits for them, and re-layouts: 2.85 us -> none
    pallas_call x1, Pallas kernels: 5.7 us -> 3.66 us  [turn(): pl.pallas_call(turn_kernel, in_specs=[SCALARS, far, far], out_specs=[WHOL...]
    ppermute x14, starting transfers between devices: 20.4 us -> 22.4 us  [swap_rep(): return lax.ppermute(value, 'rep', [(i, i ^ mask) for i in range(REPLICAS)])]
    pallas_call x11 -> x12, Pallas kernels: 30.9 us -> 32.7 us  [the longest x9 26.9 us: product(): pl.pallas_call(functools.partial(product_kernel, int(add is not None), co...]
  transfers between devices with their start and end apart: 26 -> 26, of which waited for: 10 -> 13; matrix products, arithmetic and copies ran while one was open for 3% -> 1% of each run, Pallas kernels for 25% -> 28%
where the time goes in v3:
time: 123 us; the launch traced here: 122 us
  Pallas kernels  43.6 us (35%)
  starting transfers between devices  38.2 us (31%)
  waiting for transfers between devices  37.7 us (31%)
  other arithmetic  1.7 us (1%)
    ppermute x12, waiting for transfers between devices, swap(): return lax.ppermute(value, 'shard', [(i, i ^ mask) for i in range(SHARDS)])  30.5 us
    pallas_call x9, Pallas kernels, product(): pl.pallas_call(functools.partial(product_kernel, int(add is not None), co...  26.9 us
    ppermute x14, starting transfers between devices, swap_rep(): return lax.ppermute(value, 'rep', [(i, i ^ mask) for i in range(REPLICAS)])  22.4 us
    ppermute x12, starting transfers between devices, swap(): return lax.ppermute(value, 'shard', [(i, i ^ mask) for i in range(SHARDS)])  15.8 us
    ppermute x14, waiting for transfers between devices, swap_rep(): return lax.ppermute(value, 'rep', [(i, i ^ mask) for i in range(REPLICAS)])  7.26 us
    pallas_call x3, Pallas kernels, adam(): pl.pallas_call(functools.partial(adam_kernel, len(chain), column, group_c...  3.97 us
    pallas_call x2, Pallas kernels, last(): pl.pallas_call(functools.partial(last_kernel, len(chain), final, column),...  3.93 us
    pallas_call x1, Pallas kernels, turn(): pl.pallas_call(turn_kernel, in_specs=[SCALARS, far, far], out_specs=[WHOL...  3.66 us
  transfers between devices with their start and end apart: 26, of which 13 were waited for; matrix products, arithmetic and copies ran while one was open for 1% of the time, Pallas kernels for 28%

profile of v3, /device:TPU:0, one launch (start us, length us, event | category | flops | bytes accessed | tf_op | source)
XLA Modules:
  0.0 122.3 jit_solution(7345110170024709189)
XLA Ops:
  0.6 0.1 pad_add_fusion.place
  0.7 3.7 %turn.1 = (bf16[2,2,2,96,1024]{4,3,2,1,0:T(8,128)(2,1)S(1)}, bf16[2,2,2,96,1024]{4,3,2,1,0:T(8,128)(2,1)S(1)}, bf16[1024,1792]{1,0:T(8,128)(2,1)S(1)}) custom-call(s32[3]{0:T(128)S(1)} %pad_add_fusion.place, bf16[1024,1536]{1,0:T(8,128)(2,1)} %hidden_ref.1, bf16[1024,5120]{1,0:T(8,128)(2,1)} %refs_0_.3), custom_call_target="tpu_custom_call" | custom-call | bytes 1024 | tf_op jit(solution)/shard_map/turn/pallas_call | solution.py:112
  4.4 4.3 %product.9 = (bf16[2,2,2,96,1792]{4,3,2,1,0:T(8,128)(2,1)S(1)}, bf16[1024,1792]{1,0:T(8,128)(2,1)S(1)}) custom-call(s32[3]{0:T(128)S(1)} %pad_add_fusion.place, bf16[2,2,2,96,1024]{4,3,2,1,0:T(8,128)(2,1)S(1)} %get-tuple-element.86.left_ref, bf16[1024,1792]{1,0:T(8,128)(2,1)S(1)} %get-tuple-element.87.right_ref, bf16[1024,5120]{1,0:T(8,128)(2,1)} %refs_0_.3), custom_call_target="tpu_custom_call" | custom-call | bytes 1024 | tf_op jit(solution)/shard_map/product/pallas_call | solution.py:179
  8.7 0.1 collective-permute-start
  8.8 4.3 %product.10 = (bf16[2,2,2,96,1792]{4,3,2,1,0:T(8,128)(2,1)S(1)}, bf16[1024,1536]{1,0:T(8,128)(2,1)S(1)}) custom-call(s32[3]{0:T(128)S(1)} %pad_add_fusion.place, bf16[2,2,2,96,1024]{4,3,2,1,0:T(8,128)(2,1)S(1)} %get-tuple-element.86.left_ref, bf16[1024,1792]{1,0:T(8,128)(2,1)S(1)} %get-tuple-element.90.right_ref, bf16[1024,5120]{1,0:T(8,128)(2,1)} %refs_0_.3), custom_call_target="tpu_custom_call" | custom-call | bytes 1024 | tf_op jit(solution)/shard_map/product/pallas_call | solution.py:179
  13.1 0.6 collective-permute-start.1
  13.7 3.4 %product.11 = bf16[2,2,2,96,1536]{4,3,2,1,0:T(8,128)(2,1)S(1)} custom-call(s32[3]{0:T(128)S(1)} %pad_add_fusion.place, bf16[2,2,2,96,1024]{4,3,2,1,0:T(8,128)(2,1)S(1)} %get-tuple-element.86.left_ref, bf16[1024,1536]{1,0:T(8,128)(2,1)S(1)} %get-tuple-element.93.right_ref), custom_call_target="tpu_custom_call" | custom-call | bytes 1024 | tf_op jit(solution)/shard_map/product/pallas_call | solution.py:179
  17.1 0.1 collective-permute-start.2
  17.2 0.0 collective-permute-done.refs_0_
  17.2 2.6 %product.12 = bf16[2,2,96,1792]{3,2,1,0:T(8,128)(2,1)S(1)} custom-call(s32[3]{0:T(128)S(1)} %pad_add_fusion.place, bf16[2,2,2,96,1024]{4,3,2,1,0:T(8,128)(2,1)S(1)} %get-tuple-element.95.left_ref, bf16[1024,1792]{1,0:T(8,128)(2,1)S(1)} %get-tuple-element.87.right_ref, bf16[2,2,2,96,1792]{4,3,2,1,0:T(8,128)(2,1)S(1)} %collective-permute-done.refs_0_), custom_call_target="tpu_custom_call" | custom-call | bytes 1024 | tf_op jit(solution)/shard_map/product/pallas_call | solution.py:179
  19.9 1.7 %collective-permute-start.3 = (bf16[2,2,96,1792]{3,2,1,0:T(8,128)(2,1)S(1)}, bf16[2,2,96,1792]{3,2,1,0:T(8,128)(2,1)S(1)}, u32[]{:S(2)}, u32[]{:S(2)}) collective-permute-start(bf16[2,2,96,1792]{3,2,1,0:T(8,128)(2,1)S(1)} %product.12), channel_id=1, source_target_pairs={{0,2},{1,3},{2,0},{3,1},{4,6},{5,7},{6,4},{7,5},{8,10},{9,11},{10,... | collective-permute-start | bytes 4128776 | tf_op jit(solution)/shard_map/ppermute | solution.py:52
  21.5 0.0 collective-permute-done.1.refs_0_
  21.5 2.6 %product.13 = bf16[2,2,96,1792]{3,2,1,0:T(8,128)(2,1)S(1)} custom-call(s32[3]{0:T(128)S(1)} %pad_add_fusion.place, bf16[2,2,2,96,1024]{4,3,2,1,0:T(8,128)(2,1)S(1)} %get-tuple-element.95.left_ref, bf16[1024,1792]{1,0:T(8,128)(2,1)S(1)} %get-tuple-element.90.right_ref, bf16[2,2,2,96,1792]{4,3,2,1,0:T(8,128)(2,1)S(1)} %collective-permute-done.1.refs_0_), custom_call_target="tpu_custom_call" | custom-call | bytes 1024 | tf_op jit(solution)/shard_map/product/pallas_call | solution.py:179
  24.1 1.7 %collective-permute-start.4 = (bf16[2,2,96,1792]{3,2,1,0:T(8,128)(2,1)S(1)}, bf16[2,2,96,1792]{3,2,1,0:T(8,128)(2,1)S(1)}, u32[]{:S(2)}, u32[]{:S(2)}) collective-permute-start(bf16[2,2,96,1792]{3,2,1,0:T(8,128)(2,1)S(1)} %product.13), channel_id=1, source_target_pairs={{0,4},{1,5},{2,6},{3,7},{4,0},{5,1},{6,2},{7,3},{8,12},{9,13},{10,... | collective-permute-start | bytes 4128776 | tf_op jit(solution)/shard_map/ppermute | solution.py:52
  25.8 0.0 collective-permute-done.2.refs_0_
  25.8 2.2 %product.14 = bf16[2,2,96,1536]{3,2,1,0:T(8,128)(2,1)S(1)} custom-call(s32[3]{0:T(128)S(1)} %pad_add_fusion.place, bf16[2,2,2,96,1024]{4,3,2,1,0:T(8,128)(2,1)S(1)} %get-tuple-element.95.left_ref, bf16[1024,1536]{1,0:T(8,128)(2,1)S(1)} %get-tuple-element.93.right_ref, bf16[2,2,2,96,1536]{4,3,2,1,0:T(8,128)(2,1)S(1)} %collective-permute-done.2.refs_0_), custom_call_target="tpu_custom_call" | custom-call | bytes 1024 | tf_op jit(solution)/shard_map/product/pallas_call | solution.py:179
  28.0 2.4 %collective-permute-start.5 = (bf16[2,2,96,1536]{3,2,1,0:T(8,128)(2,1)S(1)}, bf16[2,2,96,1536]{3,2,1,0:T(8,128)(2,1)S(1)}, u32[]{:S(2)}, u32[]{:S(2)}) collective-permute-start(bf16[2,2,96,1536]{3,2,1,0:T(8,128)(2,1)S(1)} %product.14), channel_id=1, source_target_pairs={{0,12},{1,13},{2,14},{3,15},{4,8},{5,9},{6,10},{7,11},{8,4},{9,5},... | collective-permute-start | bytes 3538952 | tf_op jit(solution)/shard_map/ppermute | solution.py:52
  30.4 2.6 %product.15 = bf16[2,2,96,1792]{3,2,1,0:T(8,128)(2,1)S(1)} custom-call(s32[3]{0:T(128)S(1)} %pad_add_fusion.place, bf16[2,2,2,96,1024]{4,3,2,1,0:T(8,128)(2,1)S(1)} %get-tuple-element.95.left_ref, bf16[1024,1792]{1,0:T(8,128)(2,1)S(1)} %get-tuple-element.87.right_ref, bf16[2,2,2,96,1792]{4,3,2,1,0:T(8,128)(2,1)S(1)} %collective-permute-done.refs_0_), custom_call_target="tpu_custom_call" | custom-call | bytes 1024 | tf_op jit(solution)/shard_map/product/pallas_call | solution.py:179
  33.1 2.6 %product.16 = bf16[2,2,96,1792]{3,2,1,0:T(8,128)(2,1)S(1)} custom-call(s32[3]{0:T(128)S(1)} %pad_add_fusion.place, bf16[2,2,2,96,1024]{4,3,2,1,0:T(8,128)(2,1)S(1)} %get-tuple-element.95.left_ref, bf16[1024,1792]{1,0:T(8,128)(2,1)S(1)} %get-tuple-element.90.right_ref, bf16[2,2,2,96,1792]{4,3,2,1,0:T(8,128)(2,1)S(1)} %collective-permute-done.1.refs_0_), custom_call_target="tpu_custom_call" | custom-call | bytes 1024 | tf_op jit(solution)/shard_map/product/pallas_call | solution.py:179
  35.7 2.2 %product.17 = bf16[2,2,96,1536]{3,2,1,0:T(8,128)(2,1)S(1)} custom-call(s32[3]{0:T(128)S(1)} %pad_add_fusion.place, bf16[2,2,2,96,1024]{4,3,2,1,0:T(8,128)(2,1)S(1)} %get-tuple-element.95.left_ref, bf16[1024,1536]{1,0:T(8,128)(2,1)S(1)} %get-tuple-element.93.right_ref, bf16[2,2,2,96,1536]{4,3,2,1,0:T(8,128)(2,1)S(1)} %collective-permute-done.2.refs_0_), custom_call_target="tpu_custom_call" | custom-call | bytes 1024 | tf_op jit(solution)/shard_map/product/pallas_call | solution.py:179
  37.9 3.3 %hold.1 = (bf16[1,96,5120]{2,1,0:T(8,128)(2,1)S(1)}, bf16[1,96,5120]{2,1,0:T(8,128)(2,1)S(1)}, f32[1,96,5120]{2,1,0:T(8,128)S(1)}, f32[96,5120]{1,0:T(8,128)S(1)}, f32[96,5120]{1,0:T(8,128)S(1)}) custom-call(s32[3]{0:T(128)S(1)} %pad_add_fusion.place, bf16[1,96,5120]{2,1,0:T(8,128)(2,1)} %first.1, bf16[1,96,5120]{2,1,0:T(8,128)(2,1)} %second.1, ...), custom_call_target="tpu_custom_call" | custom-call | bytes 1024 | tf_op jit(solution)/shard_map/hold/pallas_call | solution.py:262
  41.2 11.3 %collective-permute-done.3 = bf16[2,2,96,1792]{3,2,1,0:T(8,128)(2,1)S(1)} collective-permute-done((bf16[2,2,96,1792]{3,2,1,0:T(8,128)(2,1)S(1)}, bf16[2,2,96,1792]{3,2,1,0:T(8,128)(2,1)S(1)}, u32[]{:S(2)}, u32[]{:S(2)}) %collective-permute-start.3) | collective-permute-done | bytes 1376288 | tf_op jit(solution)/shard_map/ppermute | solution.py:52
  52.5 0.3 fusion.3
  52.8 1.7 %collective-permute-start.6 = (bf16[2,96,1792]{2,1,0:T(8,128)(2,1)S(1)}, bf16[2,96,1792]{2,1,0:T(8,128)(2,1)S(1)}, u32[]{:S(2)}, u32[]{:S(2)}) collective-permute-start(bf16[2,96,1792]{2,1,0:T(8,128)(2,1)S(1)} %get-tuple-element.169), channel_id=1, source_target_pairs={{0,4},{1,5},{2,6},{3,7},{4,0},{5,1},{6,2},{7,3},{8,12},{9,13},{10,... | collective-permute-start | bytes 2064392 | tf_op jit(solution)/shard_map/ppermute | solution.py:52
  54.6 2.7 %collective-permute-done.4 = bf16[2,2,96,1792]{3,2,1,0:T(8,128)(2,1)S(1)} collective-permute-done((bf16[2,2,96,1792]{3,2,1,0:T(8,128)(2,1)S(1)}, bf16[2,2,96,1792]{3,2,1,0:T(8,128)(2,1)S(1)}, u32[]{:S(2)}, u32[]{:S(2)}) %collective-permute-start.4) | collective-permute-done | bytes 1376288 | tf_op jit(solution)/shard_map/ppermute | solution.py:52
  57.3 0.3 fusion.2
  57.6 3.1 %collective-permute-start.7 = (bf16[2,96,1792]{2,1,0:T(8,128)(2,1)S(1)}, bf16[2,96,1792]{2,1,0:T(8,128)(2,1)S(1)}, u32[]{:S(2)}, u32[]{:S(2)}) collective-permute-start(bf16[2,96,1792]{2,1,0:T(8,128)(2,1)S(1)} %get-tuple-element.171), channel_id=1, source_target_pairs={{0,12},{1,13},{2,14},{3,15},{4,8},{5,9},{6,10},{7,11},{8,4},{9,5},... | collective-permute-start | bytes 2064392 | tf_op jit(solution)/shard_map/ppermute | solution.py:52
  60.7 0.3 fusion.5
  61.0 0.1 collective-permute-start.8
  61.1 10.2 %collective-permute-done.6 = bf16[2,96,1792]{2,1,0:T(8,128)(2,1)S(1)} collective-permute-done((bf16[2,96,1792]{2,1,0:T(8,128)(2,1)S(1)}, bf16[2,96,1792]{2,1,0:T(8,128)(2,1)S(1)}, u32[]{:S(2)}, u32[]{:S(2)}) %collective-permute-start.6) | collective-permute-done | bytes 688160 | tf_op jit(solution)/shard_map/ppermute | solution.py:52
  71.3 0.2 fusion.8
  71.4 3.1 %collective-permute-start.9 = (bf16[96,1792]{1,0:T(8,128)(2,1)S(1)}, bf16[96,1792]{1,0:T(8,128)(2,1)S(1)}, u32[]{:S(2)}, u32[]{:S(2)}) collective-permute-start(bf16[96,1792]{1,0:T(8,128)(2,1)S(1)} %get-tuple-element.177), channel_id=1, source_target_pairs={{0,12},{1,13},{2,14},{3,15},{4,8},{5,9},{6,10},{7,11},{8,4},{9,5},... | collective-permute-start | bytes 1032200 | tf_op jit(solution)/shard_map/ppermute | solution.py:52
  74.5 0.5 collective-permute-done.7
  75.0 0.2 fusion.9
  75.2 0.9 collective-permute-start.10
  76.1 0.1 fusion.11
  76.3 0.4 collective-permute-start.11
  76.6 5.7 %collective-permute-done.9.refs_1_ = bf16[96,1792]{1,0:T(8,128)(2,1)S(1)} collective-permute-done((bf16[96,1792]{1,0:T(8,128)(2,1)S(1)}, bf16[96,1792]{1,0:T(8,128)(2,1)S(1)}, u32[]{:S(2)}, u32[]{:S(2)}) %collective-permute-start.9) | collective-permute-done | bytes 344096 | tf_op jit(solution)/shard_map/ppermute | solution.py:52
  82.3 1.4 %adam.3 = (bf16[1,96,5120]{2,1,0:T(8,128)(2,1)S(1)}, bf16[1,96,5120]{2,1,0:T(8,128)(2,1)S(1)}, bf16[24,3584]{1,0:T(8,128)(2,1)S(1)}, bf16[24,3584]{1,0:T(8,128)(...) custom-call(s32[3]{0:T(128)S(1)} %pad_add_fusion.place, ...), custom_call_target="tpu_custom_call" | custom-call | bytes 1024 | tf_op jit(solution)/shard_map/adam/pallas_call | solution.py:227
  83.7 0.2 collective-permute-done.10.refs_1_
  83.8 1.4 %adam.4 = (bf16[1,96,5120]{2,1,0:T(8,128)(2,1)S(1)}, bf16[1,96,5120]{2,1,0:T(8,128)(2,1)S(1)}, bf16[24,3584]{1,0:T(8,128)(2,1)S(1)}, bf16[24,3584]{1,0:T(8,128)(...) custom-call(s32[3]{0:T(128)S(1)} %pad_add_fusion.place, ...), custom_call_target="tpu_custom_call", output_to_operand_aliasing={{0}: (8, {}), {1}: (9, {}), {2}: (10, {}), {3}: (11, {}), {... | custom-call | bytes 1024 | tf_op jit(solution)/shard_map/adam/pallas_call | solution.py:227
  85.2 2.0 %collective-permute-start.12 = (bf16[24,3584]{1,0:T(8,128)(2,1)S(1)}, bf16[24,3584]{1,0:T(8,128)(2,1)S(1)}, u32[]{:S(2)}, u32[]{:S(2)}) collective-permute-start(bf16[24,3584]{1,0:T(8,128)(2,1)S(1)} %get-tuple-element.145), channel_id=1, source_target_pairs={{0,16},{16,0},{32,48},{48,32},{64,80},{80,64},{96,112},{112,96},{1... | collective-permute-start | bytes 516104 | tf_op jit(solution)/shard_map/ppermute | solution.py:56
  87.2 3.6 %collective-permute-start.13 = (bf16[24,3584]{1,0:T(8,128)(2,1)S(1)}, bf16[24,3584]{1,0:T(8,128)(2,1)S(1)}, u32[]{:S(2)}, u32[]{:S(2)}) collective-permute-start(bf16[24,3584]{1,0:T(8,128)(2,1)S(1)} %get-tuple-element.146), channel_id=1, source_target_pairs={{0,32},{16,48},{32,0},{48,16},{64,96},{80,112},{96,64},{112,80},{1... | collective-permute-start | bytes 516104 | tf_op jit(solution)/shard_map/ppermute | solution.py:56
  90.8 1.3 %adam.5 = (bf16[1,96,5120]{2,1,0:T(8,128)(2,1)S(1)}, bf16[1,96,5120]{2,1,0:T(8,128)(2,1)S(1)}, bf16[24,1536]{1,0:T(8,128)(2,1)S(1)}, bf16[24,1536]{1,0:T(8,128)(...) custom-call(s32[3]{0:T(128)S(1)} %pad_add_fusion.place, ...), custom_call_target="tpu_custom_call", output_to_operand_aliasing={{0}: (8, {}), {1}: (9, {})} | custom-call | bytes 1024 | tf_op jit(solution)/shard_map/adam/pallas_call | solution.py:227
  92.1 1.8 %store.1 = (bf16[1,96,5120]{2,1,0:T(8,128)(2,1)}, bf16[1,96,5120]{2,1,0:T(8,128)(2,1)}, bf16[24,3584]{1,0:T(8,128)(2,1)S(1)}) custom-call(s32[3]{0:T(128)S(1)} %pad_add_fusion.place, bf16[1,96,5120]{2,1,0:T(8,128)(2,1)S(1)} %get-tuple-element.139.first, bf16[1,96,5120]{2,1,0:T(8,128)(2,1)S(1)} %get-tuple-element.140.second, ...), custom_call_target="tpu_custom_call", output_to_operand_aliasing={{2}: (3, {})} | custom-call | bytes 1024 | tf_op jit(solution)/shard_map/store/pallas_call | solution.py:287
  93.9 0.1 collective-permute-start.15
  94.0 4.7 %collective-permute-start.16 = (bf16[24,1536]{1,0:T(8,128)(2,1)S(1)}, bf16[24,1536]{1,0:T(8,128)(2,1)S(1)}, u32[]{:S(2)}, u32[]{:S(2)}) collective-permute-start(bf16[24,1536]{1,0:T(8,128)(2,1)S(1)} %get-tuple-element.151), channel_id=1, source_target_pairs={{0,32},{16,48},{32,0},{48,16},{64,96},{80,112},{96,64},{112,80},{1... | collective-permute-start | bytes 221192 | tf_op jit(solution)/shard_map/ppermute | solution.py:56
  98.7 1.6 %collective-permute-done.14 = bf16[24,3584]{1,0:T(8,128)(2,1)S(1)} collective-permute-done((bf16[24,3584]{1,0:T(8,128)(2,1)S(1)}, bf16[24,3584]{1,0:T(8,128)(2,1)S(1)}, u32[]{:S(2)}, u32[]{:S(2)}) %collective-permute-start.14) | collective-permute-done | bytes 172064 | tf_op jit(solution)/shard_map/ppermute | solution.py:56
  100.4 0.1 add_convert_fusion.13
  100.5 2.8 %collective-permute-start.18 = (bf16[24,3584]{1,0:T(8,128)(2,1)S(1)}, bf16[24,3584]{1,0:T(8,128)(2,1)S(1)}, u32[]{:S(2)}, u32[]{:S(2)}) collective-permute-start(bf16[24,3584]{1,0:T(8,128)(2,1)S(1)} %add_convert_fusion.13), channel_id=1, source_target_pairs={{0,64},{16,80},{32,96},{48,112},{64,0},{80,16},{96,32},{112,48},{1... | collective-permute-start | bytes 516104 | tf_op jit(solution)/shard_map/ppermute | solution.py:56
  103.3 1.0 collective-permute-done.17
  104.3 2.8 %collective-permute-start.19 = (bf16[24,1536]{1,0:T(8,128)(2,1)S(1)}, bf16[24,1536]{1,0:T(8,128)(2,1)S(1)}, u32[]{:S(2)}, u32[]{:S(2)}) collective-permute-start(bf16[24,1536]{1,0:T(8,128)(2,1)S(1)} %add_convert_fusion.15), channel_id=1, source_target_pairs={{0,64},{16,80},{32,96},{48,112},{64,0},{80,16},{96,32},{112,48},{1... | collective-permute-start | bytes 221192 | tf_op jit(solution)/shard_map/ppermute | solution.py:56
  107.1 0.4 collective-permute-done.18
  107.6 1.6 %collective-permute-start.22 = (bf16[24,3584]{1,0:T(8,128)(2,1)S(1)}, bf16[24,3584]{1,0:T(8,128)(2,1)S(1)}, u32[]{:S(2)}, u32[]{:S(2)}) collective-permute-start(bf16[24,3584]{1,0:T(8,128)(2,1)S(1)} %add_convert_fusion.12.p0), channel_id=1, source_target_pairs={{0,48},{16,32},{32,16},{48,0},{64,112},{80,96},{96,80},{112,64},{1... | collective-permute-start | bytes 516104 | tf_op jit(solution)/shard_map/ppermute | solution.py:56
  109.2 0.0 collective-permute-start.21
  109.2 2.5 %collective-permute-start.20 = (bf16[24,3584]{1,0:T(8,128)(2,1)S(1)}, bf16[24,3584]{1,0:T(8,128)(2,1)S(1)}, u32[]{:S(2)}, u32[]{:S(2)}) collective-permute-start(bf16[24,3584]{1,0:T(8,128)(2,1)S(1)} %add_convert_fusion.12.p0), channel_id=1, source_target_pairs={{0,16},{16,0},{32,48},{48,32},{64,80},{80,64},{96,112},{112,96},{1... | collective-permute-start | bytes 516104 | tf_op jit(solution)/shard_map/ppermute | solution.py:56
  111.8 1.6 %collective-permute-start.25 = (bf16[24,1536]{1,0:T(8,128)(2,1)S(1)}, bf16[24,1536]{1,0:T(8,128)(2,1)S(1)}, u32[]{:S(2)}, u32[]{:S(2)}) collective-permute-start(bf16[24,1536]{1,0:T(8,128)(2,1)S(1)} %add_convert_fusion.14.p0), channel_id=1, source_target_pairs={{0,48},{16,32},{32,16},{48,0},{64,112},{80,96},{96,80},{112,64},{1... | collective-permute-start | bytes 221192 | tf_op jit(solution)/shard_map/ppermute | solution.py:56
  113.4 0.5 collective-permute-start.24
  113.9 2.1 %collective-permute-done.22.p3 = bf16[24,3584]{1,0:T(8,128)(2,1)S(1)} collective-permute-done((bf16[24,3584]{1,0:T(8,128)(2,1)S(1)}, bf16[24,3584]{1,0:T(8,128)(2,1)S(1)}, u32[]{:S(2)}, u32[]{:S(2)}) %collective-permute-start.22) | collective-permute-done | bytes 172064 | tf_op jit(solution)/shard_map/ppermute | solution.py:56
  116.1 0.9 collective-permute-done.21.p2
  116.9 0.8 collective-permute-done.20.p1
  117.8 2.2 %last.2 = (f32[96,5120]{1,0:T(8,128)}, f32[96,5120]{1,0:T(8,128)S(1)}) custom-call(s32[3]{0:T(128)S(1)} %pad_add_fusion.place, bf16[24,3584]{1,0:T(8,128)(2,1)S(1)} %add_convert_fusion.12.p0, bf16[24,3584]{1,0:T(8,128)(2,1)S(1)} %collective-permute-done.20.p1, bf16[24,3584]{1,0:T(8,128)(2,1)S(1)} %collective-permute-done.21.p2, ...), custom_call_target="tpu_custom_call" | custom-call | bytes 1024 | tf_op jit(solution)/shard_map/last/pallas_call | solution.py:339
  120.0 0.4 collective-permute-done.23.p1
  120.4 1.7 %last.3 = (f32[96,5120]{1,0:T(8,128)}, f32[96,5120]{1,0:T(8,128)S(1)}, f32[96,640]{1,0:T(8,128)}) custom-call(s32[3]{0:T(128)S(1)} %pad_add_fusion.place, bf16[24,1536]{1,0:T(8,128)(2,1)S(1)} %add_convert_fusion.14.p0, bf16[24,1536]{1,0:T(8,128)(2,1)S(1)} %collective-permute-done.23.p1, ...), custom_call_target="tpu_custom_call", output_to_operand_aliasing={{0}: (7, {}), {1}: (8, {})} | custom-call | bytes 1024 | tf_op jit(solution)/shard_map/last/pallas_call | solution.py:339
  (16 shorter events, 0.1 us)
Async XLA Ops:
  8.7 8.5 %collective-permute-start = (bf16[2,2,2,96,1792]{4,3,2,1,0:T(8,128)(2,1)S(1)}, bf16[2,2,2,96,1792]{4,3,2,1,0:T(8,128)(2,1)S(1)}, u32[]{:S(2)}, u32[]{:S(2)}) collective-permute-start(bf16[2,2,2,96,1792]{4,3,2,1,0:T(8,128)(2,1)S(1)} %get-tuple-element.88), channel_id=1, source_target_pairs={{0,1},{1,0},{2,3},{3,2},{4,5},{5,4},{6,7},{7,6},{8,9},{9,8},{10,11... | collective-permute-start | bytes 8257544 | tf_op jit(solution)/shard_map/ppermute | solution.py:52
  13.1 8.4 %collective-permute-start.1 = (bf16[2,2,2,96,1792]{4,3,2,1,0:T(8,128)(2,1)S(1)}, bf16[2,2,2,96,1792]{4,3,2,1,0:T(8,128)(2,1)S(1)}, u32[]{:S(2)}, u32[]{:S(2)}) collective-permute-start(bf16[2,2,2,96,1792]{4,3,2,1,0:T(8,128)(2,1)S(1)} %get-tuple-element.91), channel_id=1, source_target_pairs={{0,1},{1,0},{2,3},{3,2},{4,5},{5,4},{6,7},{7,6},{8,9},{9,8},{10,11... | collective-permute-start | bytes 8257544 | tf_op jit(solution)/shard_map/ppermute | solution.py:52
  17.1 8.7 %collective-permute-start.2 = (bf16[2,2,2,96,1536]{4,3,2,1,0:T(8,128)(2,1)S(1)}, bf16[2,2,2,96,1536]{4,3,2,1,0:T(8,128)(2,1)S(1)}, u32[]{:S(2)}, u32[]{:S(2)}) collective-permute-start(bf16[2,2,2,96,1536]{4,3,2,1,0:T(8,128)(2,1)S(1)} %product.11), channel_id=1, source_target_pairs={{0,1},{1,0},{2,3},{3,2},{4,5},{5,4},{6,7},{7,6},{8,9},{9,8},{10,11... | collective-permute-start | bytes 7077896 | tf_op jit(solution)/shard_map/ppermute | solution.py:52
  19.9 32.7 %collective-permute-start.3 = (bf16[2,2,96,1792]{3,2,1,0:T(8,128)(2,1)S(1)}, bf16[2,2,96,1792]{3,2,1,0:T(8,128)(2,1)S(1)}, u32[]{:S(2)}, u32[]{:S(2)}) collective-permute-start(bf16[2,2,96,1792]{3,2,1,0:T(8,128)(2,1)S(1)} %product.12), channel_id=1, source_target_pairs={{0,2},{1,3},{2,0},{3,1},{4,6},{5,7},{6,4},{7,5},{8,10},{9,11},{10,... | collective-permute-start | bytes 4128776 | tf_op jit(solution)/shard_map/ppermute | solution.py:52
  24.1 33.1 %collective-permute-start.4 = (bf16[2,2,96,1792]{3,2,1,0:T(8,128)(2,1)S(1)}, bf16[2,2,96,1792]{3,2,1,0:T(8,128)(2,1)S(1)}, u32[]{:S(2)}, u32[]{:S(2)}) collective-permute-start(bf16[2,2,96,1792]{3,2,1,0:T(8,128)(2,1)S(1)} %product.13), channel_id=1, source_target_pairs={{0,4},{1,5},{2,6},{3,7},{4,0},{5,1},{6,2},{7,3},{8,12},{9,13},{10,... | collective-permute-start | bytes 4128776 | tf_op jit(solution)/shard_map/ppermute | solution.py:52
  28.0 32.7 %collective-permute-start.5 = (bf16[2,2,96,1536]{3,2,1,0:T(8,128)(2,1)S(1)}, bf16[2,2,96,1536]{3,2,1,0:T(8,128)(2,1)S(1)}, u32[]{:S(2)}, u32[]{:S(2)}) collective-permute-start(bf16[2,2,96,1536]{3,2,1,0:T(8,128)(2,1)S(1)} %product.14), channel_id=1, source_target_pairs={{0,12},{1,13},{2,14},{3,15},{4,8},{5,9},{6,10},{7,11},{8,4},{9,5},... | collective-permute-start | bytes 3538952 | tf_op jit(solution)/shard_map/ppermute | solution.py:52
  52.8 18.4 %collective-permute-start.6 = (bf16[2,96,1792]{2,1,0:T(8,128)(2,1)S(1)}, bf16[2,96,1792]{2,1,0:T(8,128)(2,1)S(1)}, u32[]{:S(2)}, u32[]{:S(2)}) collective-permute-start(bf16[2,96,1792]{2,1,0:T(8,128)(2,1)S(1)} %get-tuple-element.169), channel_id=1, source_target_pairs={{0,4},{1,5},{2,6},{3,7},{4,0},{5,1},{6,2},{7,3},{8,12},{9,13},{10,... | collective-permute-start | bytes 2064392 | tf_op jit(solution)/shard_map/ppermute | solution.py:52
  57.6 17.5 %collective-permute-start.7 = (bf16[2,96,1792]{2,1,0:T(8,128)(2,1)S(1)}, bf16[2,96,1792]{2,1,0:T(8,128)(2,1)S(1)}, u32[]{:S(2)}, u32[]{:S(2)}) collective-permute-start(bf16[2,96,1792]{2,1,0:T(8,128)(2,1)S(1)} %get-tuple-element.171), channel_id=1, source_target_pairs={{0,12},{1,13},{2,14},{3,15},{4,8},{5,9},{6,10},{7,11},{8,4},{9,5},... | collective-permute-start | bytes 2064392 | tf_op jit(solution)/shard_map/ppermute | solution.py:52
  61.0 15.1 %collective-permute-start.8 = (bf16[2,96,1536]{2,1,0:T(8,128)(2,1)S(1)}, bf16[2,96,1536]{2,1,0:T(8,128)(2,1)S(1)}, u32[]{:S(2)}, u32[]{:S(2)}) collective-permute-start(bf16[2,96,1536]{2,1,0:T(8,128)(2,1)S(1)} %get-tuple-element.172), channel_id=1, source_target_pairs={{0,2},{1,3},{2,0},{3,1},{4,6},{5,7},{6,4},{7,5},{8,10},{9,11},{10,... | collective-permute-start | bytes 1769480 | tf_op jit(solution)/shard_map/ppermute | solution.py:52
  71.4 10.9 %collective-permute-start.9 = (bf16[96,1792]{1,0:T(8,128)(2,1)S(1)}, bf16[96,1792]{1,0:T(8,128)(2,1)S(1)}, u32[]{:S(2)}, u32[]{:S(2)}) collective-permute-start(bf16[96,1792]{1,0:T(8,128)(2,1)S(1)} %get-tuple-element.177), channel_id=1, source_target_pairs={{0,12},{1,13},{2,14},{3,15},{4,8},{5,9},{6,10},{7,11},{8,4},{9,5},... | collective-permute-start | bytes 1032200 | tf_op jit(solution)/shard_map/ppermute | solution.py:52
  75.2 8.6 %collective-permute-start.10 = (bf16[96,1792]{1,0:T(8,128)(2,1)S(1)}, bf16[96,1792]{1,0:T(8,128)(2,1)S(1)}, u32[]{:S(2)}, u32[]{:S(2)}) collective-permute-start(bf16[96,1792]{1,0:T(8,128)(2,1)S(1)} %get-tuple-element.175), channel_id=1, source_target_pairs={{0,2},{1,3},{2,0},{3,1},{4,6},{5,7},{6,4},{7,5},{8,10},{9,11},{10,... | collective-permute-start | bytes 1032200 | tf_op jit(solution)/shard_map/ppermute | solution.py:52
  76.3 14.6 %collective-permute-start.11 = (bf16[96,1536]{1,0:T(8,128)(2,1)S(1)}, bf16[96,1536]{1,0:T(8,128)(2,1)S(1)}, u32[]{:S(2)}, u32[]{:S(2)}) collective-permute-start(bf16[96,1536]{1,0:T(8,128)(2,1)S(1)} %get-tuple-element.179), channel_id=1, source_target_pairs={{0,4},{1,5},{2,6},{3,7},{4,0},{5,1},{6,2},{7,3},{8,12},{9,13},{10,... | collective-permute-start | bytes 884744 | tf_op jit(solution)/shard_map/ppermute | solution.py:52
  85.2 13.5 %collective-permute-start.12 = (bf16[24,3584]{1,0:T(8,128)(2,1)S(1)}, bf16[24,3584]{1,0:T(8,128)(2,1)S(1)}, u32[]{:S(2)}, u32[]{:S(2)}) collective-permute-start(bf16[24,3584]{1,0:T(8,128)(2,1)S(1)} %get-tuple-element.145), channel_id=1, source_target_pairs={{0,16},{16,0},{32,48},{48,32},{64,80},{80,64},{96,112},{112,96},{1... | collective-permute-start | bytes 516104 | tf_op jit(solution)/shard_map/ppermute | solution.py:56
  87.2 11.5 %collective-permute-start.13 = (bf16[24,3584]{1,0:T(8,128)(2,1)S(1)}, bf16[24,3584]{1,0:T(8,128)(2,1)S(1)}, u32[]{:S(2)}, u32[]{:S(2)}) collective-permute-start(bf16[24,3584]{1,0:T(8,128)(2,1)S(1)} %get-tuple-element.146), channel_id=1, source_target_pairs={{0,32},{16,48},{32,0},{48,16},{64,96},{80,112},{96,64},{112,80},{1... | collective-permute-start | bytes 516104 | tf_op jit(solution)/shard_map/ppermute | solution.py:56
  90.8 9.5 %collective-permute-start.14 = (bf16[24,3584]{1,0:T(8,128)(2,1)S(1)}, bf16[24,3584]{1,0:T(8,128)(2,1)S(1)}, u32[]{:S(2)}, u32[]{:S(2)}) collective-permute-start(bf16[24,3584]{1,0:T(8,128)(2,1)S(1)} %get-tuple-element.147), channel_id=1, source_target_pairs={{0,48},{16,32},{32,16},{48,0},{64,112},{80,96},{96,80},{112,64},{1... | collective-permute-start | bytes 516104 | tf_op jit(solution)/shard_map/ppermute | solution.py:56
  93.9 9.4 %collective-permute-start.15 = (bf16[24,1536]{1,0:T(8,128)(2,1)S(1)}, bf16[24,1536]{1,0:T(8,128)(2,1)S(1)}, u32[]{:S(2)}, u32[]{:S(2)}) collective-permute-start(bf16[24,1536]{1,0:T(8,128)(2,1)S(1)} %get-tuple-element.150), channel_id=1, source_target_pairs={{0,16},{16,0},{32,48},{48,32},{64,80},{80,64},{96,112},{112,96},{1... | collective-permute-start | bytes 221192 | tf_op jit(solution)/shard_map/ppermute | solution.py:56
  94.0 9.3 %collective-permute-start.16 = (bf16[24,1536]{1,0:T(8,128)(2,1)S(1)}, bf16[24,1536]{1,0:T(8,128)(2,1)S(1)}, u32[]{:S(2)}, u32[]{:S(2)}) collective-permute-start(bf16[24,1536]{1,0:T(8,128)(2,1)S(1)} %get-tuple-element.151), channel_id=1, source_target_pairs={{0,32},{16,48},{32,0},{48,16},{64,96},{80,112},{96,64},{112,80},{1... | collective-permute-start | bytes 221192 | tf_op jit(solution)/shard_map/ppermute | solution.py:56
  98.7 5.6 %collective-permute-start.17 = (bf16[24,1536]{1,0:T(8,128)(2,1)S(1)}, bf16[24,1536]{1,0:T(8,128)(2,1)S(1)}, u32[]{:S(2)}, u32[]{:S(2)}) collective-permute-start(bf16[24,1536]{1,0:T(8,128)(2,1)S(1)} %get-tuple-element.152), channel_id=1, source_target_pairs={{0,48},{16,32},{32,16},{48,0},{64,112},{80,96},{96,80},{112,64},{1... | collective-permute-start | bytes 221192 | tf_op jit(solution)/shard_map/ppermute | solution.py:56
  100.5 7.1 %collective-permute-start.18 = (bf16[24,3584]{1,0:T(8,128)(2,1)S(1)}, bf16[24,3584]{1,0:T(8,128)(2,1)S(1)}, u32[]{:S(2)}, u32[]{:S(2)}) collective-permute-start(bf16[24,3584]{1,0:T(8,128)(2,1)S(1)} %add_convert_fusion.13), channel_id=1, source_target_pairs={{0,64},{16,80},{32,96},{48,112},{64,0},{80,16},{96,32},{112,48},{1... | collective-permute-start | bytes 516104 | tf_op jit(solution)/shard_map/ppermute | solution.py:56
  104.3 7.4 %collective-permute-start.19 = (bf16[24,1536]{1,0:T(8,128)(2,1)S(1)}, bf16[24,1536]{1,0:T(8,128)(2,1)S(1)}, u32[]{:S(2)}, u32[]{:S(2)}) collective-permute-start(bf16[24,1536]{1,0:T(8,128)(2,1)S(1)} %add_convert_fusion.15), channel_id=1, source_target_pairs={{0,64},{16,80},{32,96},{48,112},{64,0},{80,16},{96,32},{112,48},{1... | collective-permute-start | bytes 221192 | tf_op jit(solution)/shard_map/ppermute | solution.py:56
  107.6 8.5 %collective-permute-start.22 = (bf16[24,3584]{1,0:T(8,128)(2,1)S(1)}, bf16[24,3584]{1,0:T(8,128)(2,1)S(1)}, u32[]{:S(2)}, u32[]{:S(2)}) collective-permute-start(bf16[24,3584]{1,0:T(8,128)(2,1)S(1)} %add_convert_fusion.12.p0), channel_id=1, source_target_pairs={{0,48},{16,32},{32,16},{48,0},{64,112},{80,96},{96,80},{112,64},{1... | collective-permute-start | bytes 516104 | tf_op jit(solution)/shard_map/ppermute | solution.py:56
  109.2 7.7 %collective-permute-start.21 = (bf16[24,3584]{1,0:T(8,128)(2,1)S(1)}, bf16[24,3584]{1,0:T(8,128)(2,1)S(1)}, u32[]{:S(2)}, u32[]{:S(2)}) collective-permute-start(bf16[24,3584]{1,0:T(8,128)(2,1)S(1)} %add_convert_fusion.12.p0), channel_id=1, source_target_pairs={{0,32},{16,48},{32,0},{48,16},{64,96},{80,112},{96,64},{112,80},{1... | collective-permute-start | bytes 516104 | tf_op jit(solution)/shard_map/ppermute | solution.py:56
  109.2 8.5 %collective-permute-start.20 = (bf16[24,3584]{1,0:T(8,128)(2,1)S(1)}, bf16[24,3584]{1,0:T(8,128)(2,1)S(1)}, u32[]{:S(2)}, u32[]{:S(2)}) collective-permute-start(bf16[24,3584]{1,0:T(8,128)(2,1)S(1)} %add_convert_fusion.12.p0), channel_id=1, source_target_pairs={{0,16},{16,0},{32,48},{48,32},{64,80},{80,64},{96,112},{112,96},{1... | collective-permute-start | bytes 516104 | tf_op jit(solution)/shard_map/ppermute | solution.py:56
  111.8 8.2 %collective-permute-start.25 = (bf16[24,1536]{1,0:T(8,128)(2,1)S(1)}, bf16[24,1536]{1,0:T(8,128)(2,1)S(1)}, u32[]{:S(2)}, u32[]{:S(2)}) collective-permute-start(bf16[24,1536]{1,0:T(8,128)(2,1)S(1)} %add_convert_fusion.14.p0), channel_id=1, source_target_pairs={{0,48},{16,32},{32,16},{48,0},{64,112},{80,96},{96,80},{112,64},{1... | collective-permute-start | bytes 221192 | tf_op jit(solution)/shard_map/ppermute | solution.py:56
  113.4 6.6 %collective-permute-start.24 = (bf16[24,1536]{1,0:T(8,128)(2,1)S(1)}, bf16[24,1536]{1,0:T(8,128)(2,1)S(1)}, u32[]{:S(2)}, u32[]{:S(2)}) collective-permute-start(bf16[24,1536]{1,0:T(8,128)(2,1)S(1)} %add_convert_fusion.14.p0), channel_id=1, source_target_pairs={{0,32},{16,48},{32,0},{48,16},{64,96},{80,112},{96,64},{112,80},{1... | collective-permute-start | bytes 221192 | tf_op jit(solution)/shard_map/ppermute | solution.py:56
  116.1 4.4 %collective-permute-start.23 = (bf16[24,1536]{1,0:T(8,128)(2,1)S(1)}, bf16[24,1536]{1,0:T(8,128)(2,1)S(1)}, u32[]{:S(2)}, u32[]{:S(2)}) collective-permute-start(bf16[24,1536]{1,0:T(8,128)(2,1)S(1)} %add_convert_fusion.14.p0), channel_id=1, source_target_pairs={{0,16},{16,0},{32,48},{48,32},{64,80},{80,64},{96,112},{112,96},{1... | collective-permute-start | bytes 221192 | tf_op jit(solution)/shard_map/ppermute | solution.py:56

commit v4 on v3

--- a/solution.py
+++ b/solution.py
@@ -29,10 +29,11 @@
 
 CORE = 1
 MASKS = (2, 4, 12)
+Z_ORDER = (2, 1, 3)
 CHUNKS = (
-    (0, 1792, (0, 1, 2)),
-    (1792, 1792, (1, 2, 0)),
-    (3584, 1536, (2, 0, 1)),
+    (0, 1792, (2, 0, 1)),
+    (1792, 1792, (0, 1, 2)),
+    (3584, 1536, (1, 2, 0)),
 )
 GROUPS = ((0, 1), (2,))
 PLAN = (
@@ -54,6 +55,11 @@
 
 def swap_rep(value, mask):
     return lax.ppermute(value, "rep", [(i, i ^ mask) for i in range(REPLICAS)])
+
+
+def spread(values):
+    got = {d: swap_rep(values[d - 1], d) for d in Z_ORDER}
+    return [got[d] for d in (1, 2, 3)]
 
 
 def params(**kw):
@@ -133,11 +139,11 @@
         grad_ref, next_ref, sem = refs[added], refs[added + 2], refs[added + 3]
         ahead = pltpu.make_async_copy(grad_ref.at[:, pl.ds(following, next_ref.shape[1])], next_ref, sem)
         ahead.start()
-    left = left_ref[spot].reshape(-1, depth)
     flat = len(out_ref.shape) - 1
 
     def columns(t, _):
         here = pl.ds(pl.multiple_of(t * step, 128), step)
+        left = left_ref[spot].reshape(-1, depth)
         total = jnp.dot(left, right_ref[:, here], preferred_element_type=F32)
         total = total.reshape(*out_ref.shape[:-1], step)
         for n in range(added):
@@ -313,9 +319,16 @@
         total_out[:, here] = total
         return 0
 
-    lax.fori_loop(0, fresh.shape[-1] // step, columns, 0)
-    copies = [pltpu.make_async_copy(fresh, params_out.at[:, pl.ds(column, fresh.shape[-1])], sems.at[0])]
-    copies[0].start()
+    copies = []
+    tiles = fresh.shape[-1] // step
+    for n, (begin, end) in enumerate(((0, tiles // 2), (tiles // 2, tiles))):
+        lax.fori_loop(begin, end, columns, 0)
+        wide = (end - begin) * step
+        copy = pltpu.make_async_copy(
+            fresh.at[:, pl.ds(begin * step, wide)], params_out.at[:, pl.ds(column + begin * step, wide)], sems.at[n]
+        )
+        copy.start()
+        copies.append(copy)
     if final:
         moment_out, moment = refs[2:4]
         width = moment.shape[-1]
@@ -323,8 +336,8 @@
         weighted = moment_ref[:, share]
         pseudo = (total_out[:, share] - weighted) * (1.0 / pseudo_weight)
         moment[...] = weighted * (outer_beta / moment_weight) + pseudo
-        copies.append(pltpu.make_async_copy(moment, moment_out, sems.at[1]))
-        copies[1].start()
+        copies.append(pltpu.make_async_copy(moment, moment_out, sems.at[2]))
+        copies[2].start()
     for copy in copies:
         copy.wait()
 
@@ -346,7 +359,7 @@
         + [
             pltpu.VMEM((rows, width), F32),
             pltpu.VMEM((4, rows // 4, 128), F32),
-            pltpu.SemaphoreType.DMA((2,)),
+            pltpu.SemaphoreType.DMA((3,)),
         ],
         input_output_aliases={7 + n: n for n in range(len(chain))},
         compiler_params=params(),
@@ -413,7 +426,7 @@
             )
             done = parts[group][0]
             if n == GROUPS[group][-1]:
-                parts[group] = [done] + [swap_rep(parts[group][d], d) for d in (1, 2, 3)]
+                parts[group] = [done] + spread([parts[group][d] for d in (1, 2, 3)])
         elif kind == "store":
             firsts, seconds, done = store(token, firsts, seconds, parts[n][0])
             parts[n][0] = done
@@ -424,7 +437,7 @@
         elif kind == "total":
             mine, token = lax.optimization_barrier((sums[n][0], token))
             done = add(mine, sums[n][1])
-            sums[n] = [done] + [swap_rep(done, d) for d in (1, 2, 3)]
+            sums[n] = [done] + spread([done] * 3)
         elif kind == "last":
             column = CHUNKS[GROUPS[n][0]][0]
             width = sum(CHUNKS[m][1] for m in GROUPS[n])

time: 123 us -> 123 us (level)
  waiting for transfers between devices: 37.7 us -> 44.9 us
  starting transfers between devices: 38.2 us -> 33 us
  Pallas kernels: 43.6 us -> 42.3 us
    ppermute x12, waiting for transfers between devices: 30.5 us -> 37.3 us  [swap(): return lax.ppermute(value, 'shard', [(i, i ^ mask) for i in range(SHARDS)])]
    ppermute x12, starting transfers between devices: 15.8 us -> 10.1 us  [swap(): return lax.ppermute(value, 'shard', [(i, i ^ mask) for i in range(SHARDS)])]
  transfers between devices with their start and end apart: 26 -> 26, of which waited for: 13 -> 11; matrix products, arithmetic and copies ran while one was open for 1% -> 1% of each run, Pallas kernels for 28% -> 27%
where the time goes in v4:
time: 123 us
  waiting for transfers between devices  44.9 us (37%)
  Pallas kernels  42.3 us (34%)
  starting transfers between devices  33 us (27%)
  other arithmetic  1.7 us (1%)
    ppermute x12, waiting for transfers between devices, swap(): return lax.ppermute(value, 'shard', [(i, i ^ mask) for i in range(SHARDS)])  37.3 us
    pallas_call x9, Pallas kernels, product(): pl.pallas_call(functools.partial(product_kernel, int(add is not None), co...  25.9 us
    ppermute x14, starting transfers between devices, swap_rep(): return lax.ppermute(value, 'rep', [(i, i ^ mask) for i in range(REPLICAS)])  22.9 us
    ppermute x12, starting transfers between devices, swap(): return lax.ppermute(value, 'shard', [(i, i ^ mask) for i in range(SHARDS)])  10.1 us
    ppermute x14, waiting for transfers between devices, swap_rep(): return lax.ppermute(value, 'rep', [(i, i ^ mask) for i in range(REPLICAS)])  7.66 us
    pallas_call x3, Pallas kernels, adam(): pl.pallas_call(functools.partial(adam_kernel, len(chain), column, group_c...  3.97 us
    pallas_call x1, Pallas kernels, turn(): pl.pallas_call(turn_kernel, in_specs=[SCALARS, far, far], out_specs=[WHOL...  3.66 us
    pallas_call x2, Pallas kernels, last(): pl.pallas_call(functools.partial(last_kernel, len(chain), final, column),...  3.63 us
  transfers between devices with their start and end apart: 26, of which 11 were waited for; matrix products, arithmetic and copies ran while one was open for 1% of the time, Pallas kernels for 27%

profile of v4, /device:TPU:0, one launch (start us, length us, event | category | flops | bytes accessed | tf_op | source)
XLA Modules:
  0.0 123.0 jit_solution(5739924157197243921)
XLA Ops:
  0.6 0.1 pad_add_fusion.place
  0.7 3.7 %turn.1 = (bf16[2,2,2,96,1024]{4,3,2,1,0:T(8,128)(2,1)S(1)}, bf16[2,2,2,96,1024]{4,3,2,1,0:T(8,128)(2,1)S(1)}, bf16[1024,1792]{1,0:T(8,128)(2,1)S(1)}) custom-call(s32[3]{0:T(128)S(1)} %pad_add_fusion.place, bf16[1024,1536]{1,0:T(8,128)(2,1)} %hidden_ref.1, bf16[1024,5120]{1,0:T(8,128)(2,1)} %refs_0_.3), custom_call_target="tpu_custom_call" | custom-call | bytes 1024 | tf_op jit(solution)/shard_map/turn/pallas_call | solution.py:118
  4.4 4.1 %product.9 = (bf16[2,2,2,96,1792]{4,3,2,1,0:T(8,128)(2,1)S(1)}, bf16[1024,1792]{1,0:T(8,128)(2,1)S(1)}) custom-call(s32[3]{0:T(128)S(1)} %pad_add_fusion.place, bf16[2,2,2,96,1024]{4,3,2,1,0:T(8,128)(2,1)S(1)} %get-tuple-element.86.left_ref, bf16[1024,1792]{1,0:T(8,128)(2,1)S(1)} %get-tuple-element.87.right_ref, bf16[1024,5120]{1,0:T(8,128)(2,1)} %refs_0_.3), custom_call_target="tpu_custom_call" | custom-call | bytes 1024 | tf_op jit(solution)/shard_map/product/pallas_call | solution.py:185
  8.5 0.1 collective-permute-start
  8.6 4.1 %product.10 = (bf16[2,2,2,96,1792]{4,3,2,1,0:T(8,128)(2,1)S(1)}, bf16[1024,1536]{1,0:T(8,128)(2,1)S(1)}) custom-call(s32[3]{0:T(128)S(1)} %pad_add_fusion.place, bf16[2,2,2,96,1024]{4,3,2,1,0:T(8,128)(2,1)S(1)} %get-tuple-element.86.left_ref, bf16[1024,1792]{1,0:T(8,128)(2,1)S(1)} %get-tuple-element.90.right_ref, bf16[1024,5120]{1,0:T(8,128)(2,1)} %refs_0_.3), custom_call_target="tpu_custom_call" | custom-call | bytes 1024 | tf_op jit(solution)/shard_map/product/pallas_call | solution.py:185
  12.8 0.6 collective-permute-start.1
  13.4 3.3 %product.11 = bf16[2,2,2,96,1536]{4,3,2,1,0:T(8,128)(2,1)S(1)} custom-call(s32[3]{0:T(128)S(1)} %pad_add_fusion.place, bf16[2,2,2,96,1024]{4,3,2,1,0:T(8,128)(2,1)S(1)} %get-tuple-element.86.left_ref, bf16[1024,1536]{1,0:T(8,128)(2,1)S(1)} %get-tuple-element.93.right_ref), custom_call_target="tpu_custom_call" | custom-call | bytes 1024 | tf_op jit(solution)/shard_map/product/pallas_call | solution.py:185
  16.7 0.1 collective-permute-start.2
  16.8 2.5 %product.12 = bf16[2,2,96,1792]{3,2,1,0:T(8,128)(2,1)S(1)} custom-call(s32[3]{0:T(128)S(1)} %pad_add_fusion.place, bf16[2,2,2,96,1024]{4,3,2,1,0:T(8,128)(2,1)S(1)} %get-tuple-element.95.left_ref, bf16[1024,1792]{1,0:T(8,128)(2,1)S(1)} %get-tuple-element.87.right_ref, bf16[2,2,2,96,1792]{4,3,2,1,0:T(8,128)(2,1)S(1)} %collective-permute-done.refs_0_), custom_call_target="tpu_custom_call" | custom-call | bytes 1024 | tf_op jit(solution)/shard_map/product/pallas_call | solution.py:185
  19.3 3.2 %collective-permute-start.3 = (bf16[2,2,96,1792]{3,2,1,0:T(8,128)(2,1)S(1)}, bf16[2,2,96,1792]{3,2,1,0:T(8,128)(2,1)S(1)}, u32[]{:S(2)}, u32[]{:S(2)}) collective-permute-start(bf16[2,2,96,1792]{3,2,1,0:T(8,128)(2,1)S(1)} %product.12), channel_id=1, source_target_pairs={{0,12},{1,13},{2,14},{3,15},{4,8},{5,9},{6,10},{7,11},{8,4},{9,5},... | collective-permute-start | bytes 4128776 | tf_op jit(solution)/shard_map/ppermute | solution.py:53
  22.5 0.0 collective-permute-done.1.refs_0_
  22.5 2.5 %product.13 = bf16[2,2,96,1792]{3,2,1,0:T(8,128)(2,1)S(1)} custom-call(s32[3]{0:T(128)S(1)} %pad_add_fusion.place, bf16[2,2,2,96,1024]{4,3,2,1,0:T(8,128)(2,1)S(1)} %get-tuple-element.95.left_ref, bf16[1024,1792]{1,0:T(8,128)(2,1)S(1)} %get-tuple-element.90.right_ref, bf16[2,2,2,96,1792]{4,3,2,1,0:T(8,128)(2,1)S(1)} %collective-permute-done.1.refs_0_), custom_call_target="tpu_custom_call" | custom-call | bytes 1024 | tf_op jit(solution)/shard_map/product/pallas_call | solution.py:185
  25.0 1.6 %collective-permute-start.4 = (bf16[2,2,96,1792]{3,2,1,0:T(8,128)(2,1)S(1)}, bf16[2,2,96,1792]{3,2,1,0:T(8,128)(2,1)S(1)}, u32[]{:S(2)}, u32[]{:S(2)}) collective-permute-start(bf16[2,2,96,1792]{3,2,1,0:T(8,128)(2,1)S(1)} %product.13), channel_id=1, source_target_pairs={{0,2},{1,3},{2,0},{3,1},{4,6},{5,7},{6,4},{7,5},{8,10},{9,11},{10,... | collective-permute-start | bytes 4128776 | tf_op jit(solution)/shard_map/ppermute | solution.py:53
  26.6 2.1 %product.14 = bf16[2,2,96,1536]{3,2,1,0:T(8,128)(2,1)S(1)} custom-call(s32[3]{0:T(128)S(1)} %pad_add_fusion.place, bf16[2,2,2,96,1024]{4,3,2,1,0:T(8,128)(2,1)S(1)} %get-tuple-element.95.left_ref, bf16[1024,1536]{1,0:T(8,128)(2,1)S(1)} %get-tuple-element.93.right_ref, bf16[2,2,2,96,1536]{4,3,2,1,0:T(8,128)(2,1)S(1)} %collective-permute-done.2.refs_0_), custom_call_target="tpu_custom_call" | custom-call | bytes 1024 | tf_op jit(solution)/shard_map/product/pallas_call | solution.py:185
  28.7 0.2 collective-permute-start.5
  28.9 2.5 %product.15 = bf16[2,2,96,1792]{3,2,1,0:T(8,128)(2,1)S(1)} custom-call(s32[3]{0:T(128)S(1)} %pad_add_fusion.place, bf16[2,2,2,96,1024]{4,3,2,1,0:T(8,128)(2,1)S(1)} %get-tuple-element.95.left_ref, bf16[1024,1792]{1,0:T(8,128)(2,1)S(1)} %get-tuple-element.87.right_ref, bf16[2,2,2,96,1792]{4,3,2,1,0:T(8,128)(2,1)S(1)} %collective-permute-done.refs_0_), custom_call_target="tpu_custom_call" | custom-call | bytes 1024 | tf_op jit(solution)/shard_map/product/pallas_call | solution.py:185
  31.5 2.5 %product.16 = bf16[2,2,96,1792]{3,2,1,0:T(8,128)(2,1)S(1)} custom-call(s32[3]{0:T(128)S(1)} %pad_add_fusion.place, bf16[2,2,2,96,1024]{4,3,2,1,0:T(8,128)(2,1)S(1)} %get-tuple-element.95.left_ref, bf16[1024,1792]{1,0:T(8,128)(2,1)S(1)} %get-tuple-element.90.right_ref, bf16[2,2,2,96,1792]{4,3,2,1,0:T(8,128)(2,1)S(1)} %collective-permute-done.1.refs_0_), custom_call_target="tpu_custom_call" | custom-call | bytes 1024 | tf_op jit(solution)/shard_map/product/pallas_call | solution.py:185
  34.0 2.1 %product.17 = bf16[2,2,96,1536]{3,2,1,0:T(8,128)(2,1)S(1)} custom-call(s32[3]{0:T(128)S(1)} %pad_add_fusion.place, bf16[2,2,2,96,1024]{4,3,2,1,0:T(8,128)(2,1)S(1)} %get-tuple-element.95.left_ref, bf16[1024,1536]{1,0:T(8,128)(2,1)S(1)} %get-tuple-element.93.right_ref, bf16[2,2,2,96,1536]{4,3,2,1,0:T(8,128)(2,1)S(1)} %collective-permute-done.2.refs_0_), custom_call_target="tpu_custom_call" | custom-call | bytes 1024 | tf_op jit(solution)/shard_map/product/pallas_call | solution.py:185
  36.1 3.3 %hold.1 = (bf16[1,96,5120]{2,1,0:T(8,128)(2,1)S(1)}, bf16[1,96,5120]{2,1,0:T(8,128)(2,1)S(1)}, f32[1,96,5120]{2,1,0:T(8,128)S(1)}, f32[96,5120]{1,0:T(8,128)S(1)}, f32[96,5120]{1,0:T(8,128)S(1)}) custom-call(s32[3]{0:T(128)S(1)} %pad_add_fusion.place, bf16[1,96,5120]{2,1,0:T(8,128)(2,1)} %first.1, bf16[1,96,5120]{2,1,0:T(8,128)(2,1)} %second.1, ...), custom_call_target="tpu_custom_call" | custom-call | bytes 1024 | tf_op jit(solution)/shard_map/hold/pallas_call | solution.py:268
  39.5 13.9 %collective-permute-done.3 = bf16[2,2,96,1792]{3,2,1,0:T(8,128)(2,1)S(1)} collective-permute-done((bf16[2,2,96,1792]{3,2,1,0:T(8,128)(2,1)S(1)}, bf16[2,2,96,1792]{3,2,1,0:T(8,128)(2,1)S(1)}, u32[]{:S(2)}, u32[]{:S(2)}) %collective-permute-start.3) | collective-permute-done | bytes 1376288 | tf_op jit(solution)/shard_map/ppermute | solution.py:53
  53.3 0.3 fusion.3
  53.7 1.6 %collective-permute-start.6 = (bf16[2,96,1792]{2,1,0:T(8,128)(2,1)S(1)}, bf16[2,96,1792]{2,1,0:T(8,128)(2,1)S(1)}, u32[]{:S(2)}, u32[]{:S(2)}) collective-permute-start(bf16[2,96,1792]{2,1,0:T(8,128)(2,1)S(1)} %get-tuple-element.169), channel_id=1, source_target_pairs={{0,2},{1,3},{2,0},{3,1},{4,6},{5,7},{6,4},{7,5},{8,10},{9,11},{10,... | collective-permute-start | bytes 2064392 | tf_op jit(solution)/shard_map/ppermute | solution.py:53
  55.2 2.9 %collective-permute-done.4 = bf16[2,2,96,1792]{3,2,1,0:T(8,128)(2,1)S(1)} collective-permute-done((bf16[2,2,96,1792]{3,2,1,0:T(8,128)(2,1)S(1)}, bf16[2,2,96,1792]{3,2,1,0:T(8,128)(2,1)S(1)}, u32[]{:S(2)}, u32[]{:S(2)}) %collective-permute-start.4) | collective-permute-done | bytes 1376288 | tf_op jit(solution)/shard_map/ppermute | solution.py:53
  58.1 0.3 fusion.2
  58.5 0.4 collective-permute-start.7
  58.9 0.0 collective-permute-done.5
  58.9 0.3 fusion.5
  59.2 0.4 collective-permute-start.8
  59.6 12.6 %collective-permute-done.6 = bf16[2,96,1792]{2,1,0:T(8,128)(2,1)S(1)} collective-permute-done((bf16[2,96,1792]{2,1,0:T(8,128)(2,1)S(1)}, bf16[2,96,1792]{2,1,0:T(8,128)(2,1)S(1)}, u32[]{:S(2)}, u32[]{:S(2)}) %collective-permute-start.6) | collective-permute-done | bytes 688160 | tf_op jit(solution)/shard_map/ppermute | solution.py:53
  72.2 0.2 fusion.8
  72.3 0.2 collective-permute-start.9
  72.5 2.5 %collective-permute-done.7 = bf16[2,96,1792]{2,1,0:T(8,128)(2,1)S(1)} collective-permute-done((bf16[2,96,1792]{2,1,0:T(8,128)(2,1)S(1)}, bf16[2,96,1792]{2,1,0:T(8,128)(2,1)S(1)}, u32[]{:S(2)}, u32[]{:S(2)}) %collective-permute-start.7) | collective-permute-done | bytes 688160 | tf_op jit(solution)/shard_map/ppermute | solution.py:53
  75.0 0.2 fusion.9
  75.2 0.7 collective-permute-start.10
  75.9 0.1 fusion.11
  76.0 1.1 collective-permute-start.11
  77.1 5.0 %collective-permute-done.9.refs_1_ = bf16[96,1792]{1,0:T(8,128)(2,1)S(1)} collective-permute-done((bf16[96,1792]{1,0:T(8,128)(2,1)S(1)}, bf16[96,1792]{1,0:T(8,128)(2,1)S(1)}, u32[]{:S(2)}, u32[]{:S(2)}) %collective-permute-start.9) | collective-permute-done | bytes 344096 | tf_op jit(solution)/shard_map/ppermute | solution.py:53
  82.1 1.4 %adam.3 = (bf16[1,96,5120]{2,1,0:T(8,128)(2,1)S(1)}, bf16[1,96,5120]{2,1,0:T(8,128)(2,1)S(1)}, bf16[24,3584]{1,0:T(8,128)(2,1)S(1)}, bf16[24,3584]{1,0:T(8,128)(...) custom-call(s32[3]{0:T(128)S(1)} %pad_add_fusion.place, ...), custom_call_target="tpu_custom_call" | custom-call | bytes 1024 | tf_op jit(solution)/shard_map/adam/pallas_call | solution.py:233
  83.5 0.4 collective-permute-done.10.refs_1_
  83.9 1.4 %adam.4 = (bf16[1,96,5120]{2,1,0:T(8,128)(2,1)S(1)}, bf16[1,96,5120]{2,1,0:T(8,128)(2,1)S(1)}, bf16[24,3584]{1,0:T(8,128)(2,1)S(1)}, bf16[24,3584]{1,0:T(8,128)(...) custom-call(s32[3]{0:T(128)S(1)} %pad_add_fusion.place, ...), custom_call_target="tpu_custom_call", output_to_operand_aliasing={{0}: (8, {}), {1}: (9, {}), {2}: (10, {}), {3}: (11, {}), {... | custom-call | bytes 1024 | tf_op jit(solution)/shard_map/adam/pallas_call | solution.py:233
  85.3 2.0 %collective-permute-start.12 = (bf16[24,3584]{1,0:T(8,128)(2,1)S(1)}, bf16[24,3584]{1,0:T(8,128)(2,1)S(1)}, u32[]{:S(2)}, u32[]{:S(2)}) collective-permute-start(bf16[24,3584]{1,0:T(8,128)(2,1)S(1)} %get-tuple-element.145), channel_id=1, source_target_pairs={{0,16},{16,0},{32,48},{48,32},{64,80},{80,64},{96,112},{112,96},{1... | collective-permute-start | bytes 516104 | tf_op jit(solution)/shard_map/ppermute | solution.py:57
  87.3 3.6 %collective-permute-start.13 = (bf16[24,3584]{1,0:T(8,128)(2,1)S(1)}, bf16[24,3584]{1,0:T(8,128)(2,1)S(1)}, u32[]{:S(2)}, u32[]{:S(2)}) collective-permute-start(bf16[24,3584]{1,0:T(8,128)(2,1)S(1)} %get-tuple-element.146), channel_id=1, source_target_pairs={{0,32},{16,48},{32,0},{48,16},{64,96},{80,112},{96,64},{112,80},{1... | collective-permute-start | bytes 516104 | tf_op jit(solution)/shard_map/ppermute | solution.py:57
  90.9 0.0 collective-permute-start.14
  90.9 0.0 collective-permute-done.11.refs_1_
  90.9 1.3 %adam.5 = (bf16[1,96,5120]{2,1,0:T(8,128)(2,1)S(1)}, bf16[1,96,5120]{2,1,0:T(8,128)(2,1)S(1)}, bf16[24,1536]{1,0:T(8,128)(2,1)S(1)}, bf16[24,1536]{1,0:T(8,128)(...) custom-call(s32[3]{0:T(128)S(1)} %pad_add_fusion.place, ...), custom_call_target="tpu_custom_call", output_to_operand_aliasing={{0}: (8, {}), {1}: (9, {})} | custom-call | bytes 1024 | tf_op jit(solution)/shard_map/adam/pallas_call | solution.py:233
  92.1 1.8 %store.1 = (bf16[1,96,5120]{2,1,0:T(8,128)(2,1)}, bf16[1,96,5120]{2,1,0:T(8,128)(2,1)}, bf16[24,3584]{1,0:T(8,128)(2,1)S(1)}) custom-call(s32[3]{0:T(128)S(1)} %pad_add_fusion.place, bf16[1,96,5120]{2,1,0:T(8,128)(2,1)S(1)} %get-tuple-element.139.first, bf16[1,96,5120]{2,1,0:T(8,128)(2,1)S(1)} %get-tuple-element.140.second, ...), custom_call_target="tpu_custom_call", output_to_operand_aliasing={{2}: (3, {})} | custom-call | bytes 1024 | tf_op jit(solution)/shard_map/store/pallas_call | solution.py:293
  94.0 0.1 collective-permute-start.15
  94.1 4.7 %collective-permute-start.16 = (bf16[24,1536]{1,0:T(8,128)(2,1)S(1)}, bf16[24,1536]{1,0:T(8,128)(2,1)S(1)}, u32[]{:S(2)}, u32[]{:S(2)}) collective-permute-start(bf16[24,1536]{1,0:T(8,128)(2,1)S(1)} %get-tuple-element.151), channel_id=1, source_target_pairs={{0,32},{16,48},{32,0},{48,16},{64,96},{80,112},{96,64},{112,80},{1... | collective-permute-start | bytes 221192 | tf_op jit(solution)/shard_map/ppermute | solution.py:57
  98.8 0.0 collective-permute-done.13
  98.8 1.3 %collective-permute-done.14 = bf16[24,3584]{1,0:T(8,128)(2,1)S(1)} collective-permute-done((bf16[24,3584]{1,0:T(8,128)(2,1)S(1)}, bf16[24,3584]{1,0:T(8,128)(2,1)S(1)}, u32[]{:S(2)}, u32[]{:S(2)}) %collective-permute-start.14) | collective-permute-done | bytes 172064 | tf_op jit(solution)/shard_map/ppermute | solution.py:57
  100.1 0.1 add_convert_fusion.13
  100.2 3.1 %collective-permute-start.18 = (bf16[24,3584]{1,0:T(8,128)(2,1)S(1)}, bf16[24,3584]{1,0:T(8,128)(2,1)S(1)}, u32[]{:S(2)}, u32[]{:S(2)}) collective-permute-start(bf16[24,3584]{1,0:T(8,128)(2,1)S(1)} %add_convert_fusion.13), channel_id=1, source_target_pairs={{0,64},{16,80},{32,96},{48,112},{64,0},{80,16},{96,32},{112,48},{1... | collective-permute-start | bytes 516104 | tf_op jit(solution)/shard_map/ppermute | solution.py:57
  103.3 0.0 collective-permute-done.15
  103.3 1.0 collective-permute-done.17
  104.4 3.1 %collective-permute-start.19 = (bf16[24,1536]{1,0:T(8,128)(2,1)S(1)}, bf16[24,1536]{1,0:T(8,128)(2,1)S(1)}, u32[]{:S(2)}, u32[]{:S(2)}) collective-permute-start(bf16[24,1536]{1,0:T(8,128)(2,1)S(1)} %add_convert_fusion.15), channel_id=1, source_target_pairs={{0,64},{16,80},{32,96},{48,112},{64,0},{80,16},{96,32},{112,48},{1... | collective-permute-start | bytes 221192 | tf_op jit(solution)/shard_map/ppermute | solution.py:57
  107.5 1.7 %collective-permute-start.22 = (bf16[24,3584]{1,0:T(8,128)(2,1)S(1)}, bf16[24,3584]{1,0:T(8,128)(2,1)S(1)}, u32[]{:S(2)}, u32[]{:S(2)}) collective-permute-start(bf16[24,3584]{1,0:T(8,128)(2,1)S(1)} %add_convert_fusion.12.p0), channel_id=1, source_target_pairs={{0,48},{16,32},{32,16},{48,0},{64,112},{80,96},{96,80},{112,64},{1... | collective-permute-start | bytes 516104 | tf_op jit(solution)/shard_map/ppermute | solution.py:57
  109.2 2.4 %collective-permute-start.20 = (bf16[24,3584]{1,0:T(8,128)(2,1)S(1)}, bf16[24,3584]{1,0:T(8,128)(2,1)S(1)}, u32[]{:S(2)}, u32[]{:S(2)}) collective-permute-start(bf16[24,3584]{1,0:T(8,128)(2,1)S(1)} %add_convert_fusion.12.p0), channel_id=1, source_target_pairs={{0,16},{16,0},{32,48},{48,32},{64,80},{80,64},{96,112},{112,96},{1... | collective-permute-start | bytes 516104 | tf_op jit(solution)/shard_map/ppermute | solution.py:57
  111.7 1.7 %collective-permute-start.25 = (bf16[24,1536]{1,0:T(8,128)(2,1)S(1)}, bf16[24,1536]{1,0:T(8,128)(2,1)S(1)}, u32[]{:S(2)}, u32[]{:S(2)}) collective-permute-start(bf16[24,1536]{1,0:T(8,128)(2,1)S(1)} %add_convert_fusion.14.p0), channel_id=1, source_target_pairs={{0,48},{16,32},{32,16},{48,0},{64,112},{80,96},{96,80},{112,64},{1... | collective-permute-start | bytes 221192 | tf_op jit(solution)/shard_map/ppermute | solution.py:57
  113.4 0.4 collective-permute-start.24
  113.9 3.0 %collective-permute-done.22.p3 = bf16[24,3584]{1,0:T(8,128)(2,1)S(1)} collective-permute-done((bf16[24,3584]{1,0:T(8,128)(2,1)S(1)}, bf16[24,3584]{1,0:T(8,128)(2,1)S(1)}, u32[]{:S(2)}, u32[]{:S(2)}) %collective-permute-start.22) | collective-permute-done | bytes 172064 | tf_op jit(solution)/shard_map/ppermute | solution.py:57
  116.9 0.9 collective-permute-done.20.p1
  117.7 2.0 %last.2 = (f32[96,5120]{1,0:T(8,128)}, f32[96,5120]{1,0:T(8,128)S(1)}) custom-call(s32[3]{0:T(128)S(1)} %pad_add_fusion.place, bf16[24,3584]{1,0:T(8,128)(2,1)S(1)} %add_convert_fusion.12.p0, bf16[24,3584]{1,0:T(8,128)(2,1)S(1)} %collective-permute-done.20.p1, bf16[24,3584]{1,0:T(8,128)(2,1)S(1)} %collective-permute-done.21.p2, ...), custom_call_target="tpu_custom_call" | custom-call | bytes 1024 | tf_op jit(solution)/shard_map/last/pallas_call | solution.py:352
  119.8 1.5 %collective-permute-done.23.p1 = bf16[24,1536]{1,0:T(8,128)(2,1)S(1)} collective-permute-done((bf16[24,1536]{1,0:T(8,128)(2,1)S(1)}, bf16[24,1536]{1,0:T(8,128)(2,1)S(1)}, u32[]{:S(2)}, u32[]{:S(2)}) %collective-permute-start.23) | collective-permute-done | bytes 73760 | tf_op jit(solution)/shard_map/ppermute | solution.py:57
  121.2 1.6 %last.3 = (f32[96,5120]{1,0:T(8,128)}, f32[96,5120]{1,0:T(8,128)S(1)}, f32[96,640]{1,0:T(8,128)}) custom-call(s32[3]{0:T(128)S(1)} %pad_add_fusion.place, bf16[24,1536]{1,0:T(8,128)(2,1)S(1)} %add_convert_fusion.14.p0, bf16[24,1536]{1,0:T(8,128)(2,1)S(1)} %collective-permute-done.23.p1, ...), custom_call_target="tpu_custom_call", output_to_operand_aliasing={{0}: (7, {}), {1}: (8, {})} | custom-call | bytes 1024 | tf_op jit(solution)/shard_map/last/pallas_call | solution.py:352
  (16 shorter events, 0.1 us)
Async XLA Ops:
  8.5 8.2 %collective-permute-start = (bf16[2,2,2,96,1792]{4,3,2,1,0:T(8,128)(2,1)S(1)}, bf16[2,2,2,96,1792]{4,3,2,1,0:T(8,128)(2,1)S(1)}, u32[]{:S(2)}, u32[]{:S(2)}) collective-permute-start(bf16[2,2,2,96,1792]{4,3,2,1,0:T(8,128)(2,1)S(1)} %get-tuple-element.88), channel_id=1, source_target_pairs={{0,1},{1,0},{2,3},{3,2},{4,5},{5,4},{6,7},{7,6},{8,9},{9,8},{10,11... | collective-permute-start | bytes 8257544 | tf_op jit(solution)/shard_map/ppermute | solution.py:53
  12.8 9.7 %collective-permute-start.1 = (bf16[2,2,2,96,1792]{4,3,2,1,0:T(8,128)(2,1)S(1)}, bf16[2,2,2,96,1792]{4,3,2,1,0:T(8,128)(2,1)S(1)}, u32[]{:S(2)}, u32[]{:S(2)}) collective-permute-start(bf16[2,2,2,96,1792]{4,3,2,1,0:T(8,128)(2,1)S(1)} %get-tuple-element.91), channel_id=1, source_target_pairs={{0,1},{1,0},{2,3},{3,2},{4,5},{5,4},{6,7},{7,6},{8,9},{9,8},{10,11... | collective-permute-start | bytes 8257544 | tf_op jit(solution)/shard_map/ppermute | solution.py:53
  16.7 9.9 %collective-permute-start.2 = (bf16[2,2,2,96,1536]{4,3,2,1,0:T(8,128)(2,1)S(1)}, bf16[2,2,2,96,1536]{4,3,2,1,0:T(8,128)(2,1)S(1)}, u32[]{:S(2)}, u32[]{:S(2)}) collective-permute-start(bf16[2,2,2,96,1536]{4,3,2,1,0:T(8,128)(2,1)S(1)} %product.11), channel_id=1, source_target_pairs={{0,1},{1,0},{2,3},{3,2},{4,5},{5,4},{6,7},{7,6},{8,9},{9,8},{10,11... | collective-permute-start | bytes 7077896 | tf_op jit(solution)/shard_map/ppermute | solution.py:53
  19.3 34.0 %collective-permute-start.3 = (bf16[2,2,96,1792]{3,2,1,0:T(8,128)(2,1)S(1)}, bf16[2,2,96,1792]{3,2,1,0:T(8,128)(2,1)S(1)}, u32[]{:S(2)}, u32[]{:S(2)}) collective-permute-start(bf16[2,2,96,1792]{3,2,1,0:T(8,128)(2,1)S(1)} %product.12), channel_id=1, source_target_pairs={{0,12},{1,13},{2,14},{3,15},{4,8},{5,9},{6,10},{7,11},{8,4},{9,5},... | collective-permute-start | bytes 4128776 | tf_op jit(solution)/shard_map/ppermute | solution.py:53
  25.0 33.1 %collective-permute-start.4 = (bf16[2,2,96,1792]{3,2,1,0:T(8,128)(2,1)S(1)}, bf16[2,2,96,1792]{3,2,1,0:T(8,128)(2,1)S(1)}, u32[]{:S(2)}, u32[]{:S(2)}) collective-permute-start(bf16[2,2,96,1792]{3,2,1,0:T(8,128)(2,1)S(1)} %product.13), channel_id=1, source_target_pairs={{0,2},{1,3},{2,0},{3,1},{4,6},{5,7},{6,4},{7,5},{8,10},{9,11},{10,... | collective-permute-start | bytes 4128776 | tf_op jit(solution)/shard_map/ppermute | solution.py:53
  28.7 30.1 %collective-permute-start.5 = (bf16[2,2,96,1536]{3,2,1,0:T(8,128)(2,1)S(1)}, bf16[2,2,96,1536]{3,2,1,0:T(8,128)(2,1)S(1)}, u32[]{:S(2)}, u32[]{:S(2)}) collective-permute-start(bf16[2,2,96,1536]{3,2,1,0:T(8,128)(2,1)S(1)} %product.14), channel_id=1, source_target_pairs={{0,4},{1,5},{2,6},{3,7},{4,0},{5,1},{6,2},{7,3},{8,12},{9,13},{10,... | collective-permute-start | bytes 3538952 | tf_op jit(solution)/shard_map/ppermute | solution.py:53
  53.7 18.5 %collective-permute-start.6 = (bf16[2,96,1792]{2,1,0:T(8,128)(2,1)S(1)}, bf16[2,96,1792]{2,1,0:T(8,128)(2,1)S(1)}, u32[]{:S(2)}, u32[]{:S(2)}) collective-permute-start(bf16[2,96,1792]{2,1,0:T(8,128)(2,1)S(1)} %get-tuple-element.169), channel_id=1, source_target_pairs={{0,2},{1,3},{2,0},{3,1},{4,6},{5,7},{6,4},{7,5},{8,10},{9,11},{10,... | collective-permute-start | bytes 2064392 | tf_op jit(solution)/shard_map/ppermute | solution.py:53
  58.5 16.6 %collective-permute-start.7 = (bf16[2,96,1792]{2,1,0:T(8,128)(2,1)S(1)}, bf16[2,96,1792]{2,1,0:T(8,128)(2,1)S(1)}, u32[]{:S(2)}, u32[]{:S(2)}) collective-permute-start(bf16[2,96,1792]{2,1,0:T(8,128)(2,1)S(1)} %get-tuple-element.171), channel_id=1, source_target_pairs={{0,4},{1,5},{2,6},{3,7},{4,0},{5,1},{6,2},{7,3},{8,12},{9,13},{10,... | collective-permute-start | bytes 2064392 | tf_op jit(solution)/shard_map/ppermute | solution.py:53
  59.2 16.7 %collective-permute-start.8 = (bf16[2,96,1536]{2,1,0:T(8,128)(2,1)S(1)}, bf16[2,96,1536]{2,1,0:T(8,128)(2,1)S(1)}, u32[]{:S(2)}, u32[]{:S(2)}) collective-permute-start(bf16[2,96,1536]{2,1,0:T(8,128)(2,1)S(1)} %get-tuple-element.172), channel_id=1, source_target_pairs={{0,12},{1,13},{2,14},{3,15},{4,8},{5,9},{6,10},{7,11},{8,4},{9,5},... | collective-permute-start | bytes 1769480 | tf_op jit(solution)/shard_map/ppermute | solution.py:53
  72.3 9.8 %collective-permute-start.9 = (bf16[96,1792]{1,0:T(8,128)(2,1)S(1)}, bf16[96,1792]{1,0:T(8,128)(2,1)S(1)}, u32[]{:S(2)}, u32[]{:S(2)}) collective-permute-start(bf16[96,1792]{1,0:T(8,128)(2,1)S(1)} %get-tuple-element.177), channel_id=1, source_target_pairs={{0,4},{1,5},{2,6},{3,7},{4,0},{5,1},{6,2},{7,3},{8,12},{9,13},{10,... | collective-permute-start | bytes 1032200 | tf_op jit(solution)/shard_map/ppermute | solution.py:53
  75.2 8.7 %collective-permute-start.10 = (bf16[96,1792]{1,0:T(8,128)(2,1)S(1)}, bf16[96,1792]{1,0:T(8,128)(2,1)S(1)}, u32[]{:S(2)}, u32[]{:S(2)}) collective-permute-start(bf16[96,1792]{1,0:T(8,128)(2,1)S(1)} %get-tuple-element.175), channel_id=1, source_target_pairs={{0,12},{1,13},{2,14},{3,15},{4,8},{5,9},{6,10},{7,11},{8,4},{9,5},... | collective-permute-start | bytes 1032200 | tf_op jit(solution)/shard_map/ppermute | solution.py:53
  76.0 14.9 %collective-permute-start.11 = (bf16[96,1536]{1,0:T(8,128)(2,1)S(1)}, bf16[96,1536]{1,0:T(8,128)(2,1)S(1)}, u32[]{:S(2)}, u32[]{:S(2)}) collective-permute-start(bf16[96,1536]{1,0:T(8,128)(2,1)S(1)} %get-tuple-element.179), channel_id=1, source_target_pairs={{0,2},{1,3},{2,0},{3,1},{4,6},{5,7},{6,4},{7,5},{8,10},{9,11},{10,... | collective-permute-start | bytes 884744 | tf_op jit(solution)/shard_map/ppermute | solution.py:53
  85.3 13.5 %collective-permute-start.12 = (bf16[24,3584]{1,0:T(8,128)(2,1)S(1)}, bf16[24,3584]{1,0:T(8,128)(2,1)S(1)}, u32[]{:S(2)}, u32[]{:S(2)}) collective-permute-start(bf16[24,3584]{1,0:T(8,128)(2,1)S(1)} %get-tuple-element.145), channel_id=1, source_target_pairs={{0,16},{16,0},{32,48},{48,32},{64,80},{80,64},{96,112},{112,96},{1... | collective-permute-start | bytes 516104 | tf_op jit(solution)/shard_map/ppermute | solution.py:57
  87.3 11.5 %collective-permute-start.13 = (bf16[24,3584]{1,0:T(8,128)(2,1)S(1)}, bf16[24,3584]{1,0:T(8,128)(2,1)S(1)}, u32[]{:S(2)}, u32[]{:S(2)}) collective-permute-start(bf16[24,3584]{1,0:T(8,128)(2,1)S(1)} %get-tuple-element.146), channel_id=1, source_target_pairs={{0,32},{16,48},{32,0},{48,16},{64,96},{80,112},{96,64},{112,80},{1... | collective-permute-start | bytes 516104 | tf_op jit(solution)/shard_map/ppermute | solution.py:57
  90.9 9.3 %collective-permute-start.14 = (bf16[24,3584]{1,0:T(8,128)(2,1)S(1)}, bf16[24,3584]{1,0:T(8,128)(2,1)S(1)}, u32[]{:S(2)}, u32[]{:S(2)}) collective-permute-start(bf16[24,3584]{1,0:T(8,128)(2,1)S(1)} %get-tuple-element.147), channel_id=1, source_target_pairs={{0,48},{16,32},{32,16},{48,0},{64,112},{80,96},{96,80},{112,64},{1... | collective-permute-start | bytes 516104 | tf_op jit(solution)/shard_map/ppermute | solution.py:57
  94.0 9.4 %collective-permute-start.15 = (bf16[24,1536]{1,0:T(8,128)(2,1)S(1)}, bf16[24,1536]{1,0:T(8,128)(2,1)S(1)}, u32[]{:S(2)}, u32[]{:S(2)}) collective-permute-start(bf16[24,1536]{1,0:T(8,128)(2,1)S(1)} %get-tuple-element.150), channel_id=1, source_target_pairs={{0,16},{16,0},{32,48},{48,32},{64,80},{80,64},{96,112},{112,96},{1... | collective-permute-start | bytes 221192 | tf_op jit(solution)/shard_map/ppermute | solution.py:57
  94.1 9.3 %collective-permute-start.16 = (bf16[24,1536]{1,0:T(8,128)(2,1)S(1)}, bf16[24,1536]{1,0:T(8,128)(2,1)S(1)}, u32[]{:S(2)}, u32[]{:S(2)}) collective-permute-start(bf16[24,1536]{1,0:T(8,128)(2,1)S(1)} %get-tuple-element.151), channel_id=1, source_target_pairs={{0,32},{16,48},{32,0},{48,16},{64,96},{80,112},{96,64},{112,80},{1... | collective-permute-start | bytes 221192 | tf_op jit(solution)/shard_map/ppermute | solution.py:57
  98.8 5.6 %collective-permute-start.17 = (bf16[24,1536]{1,0:T(8,128)(2,1)S(1)}, bf16[24,1536]{1,0:T(8,128)(2,1)S(1)}, u32[]{:S(2)}, u32[]{:S(2)}) collective-permute-start(bf16[24,1536]{1,0:T(8,128)(2,1)S(1)} %get-tuple-element.152), channel_id=1, source_target_pairs={{0,48},{16,32},{32,16},{48,0},{64,112},{80,96},{96,80},{112,64},{1... | collective-permute-start | bytes 221192 | tf_op jit(solution)/shard_map/ppermute | solution.py:57
  100.2 7.2 %collective-permute-start.18 = (bf16[24,3584]{1,0:T(8,128)(2,1)S(1)}, bf16[24,3584]{1,0:T(8,128)(2,1)S(1)}, u32[]{:S(2)}, u32[]{:S(2)}) collective-permute-start(bf16[24,3584]{1,0:T(8,128)(2,1)S(1)} %add_convert_fusion.13), channel_id=1, source_target_pairs={{0,64},{16,80},{32,96},{48,112},{64,0},{80,16},{96,32},{112,48},{1... | collective-permute-start | bytes 516104 | tf_op jit(solution)/shard_map/ppermute | solution.py:57
  104.4 7.3 %collective-permute-start.19 = (bf16[24,1536]{1,0:T(8,128)(2,1)S(1)}, bf16[24,1536]{1,0:T(8,128)(2,1)S(1)}, u32[]{:S(2)}, u32[]{:S(2)}) collective-permute-start(bf16[24,1536]{1,0:T(8,128)(2,1)S(1)} %add_convert_fusion.15), channel_id=1, source_target_pairs={{0,64},{16,80},{32,96},{48,112},{64,0},{80,16},{96,32},{112,48},{1... | collective-permute-start | bytes 221192 | tf_op jit(solution)/shard_map/ppermute | solution.py:57
  107.5 9.3 %collective-permute-start.22 = (bf16[24,3584]{1,0:T(8,128)(2,1)S(1)}, bf16[24,3584]{1,0:T(8,128)(2,1)S(1)}, u32[]{:S(2)}, u32[]{:S(2)}) collective-permute-start(bf16[24,3584]{1,0:T(8,128)(2,1)S(1)} %add_convert_fusion.12.p0), channel_id=1, source_target_pairs={{0,48},{16,32},{32,16},{48,0},{64,112},{80,96},{96,80},{112,64},{1... | collective-permute-start | bytes 516104 | tf_op jit(solution)/shard_map/ppermute | solution.py:57
  109.2 7.6 %collective-permute-start.21 = (bf16[24,3584]{1,0:T(8,128)(2,1)S(1)}, bf16[24,3584]{1,0:T(8,128)(2,1)S(1)}, u32[]{:S(2)}, u32[]{:S(2)}) collective-permute-start(bf16[24,3584]{1,0:T(8,128)(2,1)S(1)} %add_convert_fusion.12.p0), channel_id=1, source_target_pairs={{0,32},{16,48},{32,0},{48,16},{64,96},{80,112},{96,64},{112,80},{1... | collective-permute-start | bytes 516104 | tf_op jit(solution)/shard_map/ppermute | solution.py:57
  109.2 8.5 %collective-permute-start.20 = (bf16[24,3584]{1,0:T(8,128)(2,1)S(1)}, bf16[24,3584]{1,0:T(8,128)(2,1)S(1)}, u32[]{:S(2)}, u32[]{:S(2)}) collective-permute-start(bf16[24,3584]{1,0:T(8,128)(2,1)S(1)} %add_convert_fusion.12.p0), channel_id=1, source_target_pairs={{0,16},{16,0},{32,48},{48,32},{64,80},{80,64},{96,112},{112,96},{1... | collective-permute-start | bytes 516104 | tf_op jit(solution)/shard_map/ppermute | solution.py:57
  111.7 8.0 %collective-permute-start.25 = (bf16[24,1536]{1,0:T(8,128)(2,1)S(1)}, bf16[24,1536]{1,0:T(8,128)(2,1)S(1)}, u32[]{:S(2)}, u32[]{:S(2)}) collective-permute-start(bf16[24,1536]{1,0:T(8,128)(2,1)S(1)} %add_convert_fusion.14.p0), channel_id=1, source_target_pairs={{0,48},{16,32},{32,16},{48,0},{64,112},{80,96},{96,80},{112,64},{1... | collective-permute-start | bytes 221192 | tf_op jit(solution)/shard_map/ppermute | solution.py:57
  113.4 6.3 %collective-permute-start.24 = (bf16[24,1536]{1,0:T(8,128)(2,1)S(1)}, bf16[24,1536]{1,0:T(8,128)(2,1)S(1)}, u32[]{:S(2)}, u32[]{:S(2)}) collective-permute-start(bf16[24,1536]{1,0:T(8,128)(2,1)S(1)} %add_convert_fusion.14.p0), channel_id=1, source_target_pairs={{0,32},{16,48},{32,0},{48,16},{64,96},{80,112},{96,64},{112,80},{1... | collective-permute-start | bytes 221192 | tf_op jit(solution)/shard_map/ppermute | solution.py:57
  116.8 4.4 %collective-permute-start.23 = (bf16[24,1536]{1,0:T(8,128)(2,1)S(1)}, bf16[24,1536]{1,0:T(8,128)(2,1)S(1)}, u32[]{:S(2)}, u32[]{:S(2)}) collective-permute-start(bf16[24,1536]{1,0:T(8,128)(2,1)S(1)} %add_convert_fusion.14.p0), channel_id=1, source_target_pairs={{0,16},{16,0},{32,48},{48,32},{64,80},{80,64},{96,112},{112,96},{1... | collective-permute-start | bytes 221192 | tf_op jit(solution)/shard_map/ppermute | solution.py:57

commit v5 on v3

--- a/solution.py
+++ b/solution.py
@@ -39,8 +39,8 @@
     *(("other", n) for n in range(3)),
     *(("send", n) for n in range(3)),
     *(("keep", n) for n in range(3)),
+    *(("fold", n) for n in range(3)),
     ("hold", 0),
-    *(("fold", n) for n in range(3)),
     *(("again", n) for n in range(3)),
     *(("adam", n) for n in range(3)),
     ("store", 0),
@@ -133,11 +133,11 @@
         grad_ref, next_ref, sem = refs[added], refs[added + 2], refs[added + 3]
         ahead = pltpu.make_async_copy(grad_ref.at[:, pl.ds(following, next_ref.shape[1])], next_ref, sem)
         ahead.start()
-    left = left_ref[spot].reshape(-1, depth)
     flat = len(out_ref.shape) - 1
 
     def columns(t, _):
         here = pl.ds(pl.multiple_of(t * step, 128), step)
+        left = left_ref[spot].reshape(-1, depth)
         total = jnp.dot(left, right_ref[:, here], preferred_element_type=F32)
         total = total.reshape(*out_ref.shape[:-1], step)
         for n in range(added):

time: 123 us -> 123 us (level)
  waiting for transfers between devices: 37.7 us -> 39.7 us
    ppermute x14, waiting for transfers between devices: 7.26 us -> 8.95 us  [swap_rep(): return lax.ppermute(value, 'rep', [(i, i ^ mask) for i in range(REPLICAS)])]
  transfers between devices with their start and end apart: 26 -> 26, of which waited for: 13 -> 11; matrix products, arithmetic and copies ran while one was open for 1% -> 1% of each run, Pallas kernels for 28% -> 27%
where the time goes in v5:
time: 123 us
  Pallas kernels  42.7 us (35%)
  waiting for transfers between devices  39.7 us (32%)
  starting transfers between devices  38.3 us (31%)
  other arithmetic  1.7 us (1%)
    ppermute x12, waiting for transfers between devices, swap(): return lax.ppermute(value, 'shard', [(i, i ^ mask) for i in range(SHARDS)])  30.7 us
    pallas_call x9, Pallas kernels, product(): pl.pallas_call(functools.partial(product_kernel, int(add is not None), co...  25.9 us
    ppermute x14, starting transfers between devices, swap_rep(): return lax.ppermute(value, 'rep', [(i, i ^ mask) for i in range(REPLICAS)])  22.4 us
    ppermute x12, starting transfers between devices, swap(): return lax.ppermute(value, 'shard', [(i, i ^ mask) for i in range(SHARDS)])  15.9 us
    ppermute x14, waiting for transfers between devices, swap_rep(): return lax.ppermute(value, 'rep', [(i, i ^ mask) for i in range(REPLICAS)])  8.95 us
    pallas_call x3, Pallas kernels, adam(): pl.pallas_call(functools.partial(adam_kernel, len(chain), column, group_c...  3.98 us
    pallas_call x2, Pallas kernels, last(): pl.pallas_call(functools.partial(last_kernel, len(chain), final, column),...  3.93 us
    pallas_call x1, Pallas kernels, turn(): pl.pallas_call(turn_kernel, in_specs=[SCALARS, far, far], out_specs=[WHOL...  3.66 us
  transfers between devices with their start and end apart: 26, of which 11 were waited for; matrix products, arithmetic and copies ran while one was open for 1% of the time, Pallas kernels for 27%

profile of v5, /device:TPU:0, one launch (start us, length us, event | category | flops | bytes accessed | tf_op | source)
XLA Modules:
  0.0 123.4 jit_solution(17402883299841443222)
XLA Ops:
  0.6 0.1 pad_add_fusion.place
  0.7 3.7 %turn.1 = (bf16[2,2,2,96,1024]{4,3,2,1,0:T(8,128)(2,1)S(1)}, bf16[2,2,2,96,1024]{4,3,2,1,0:T(8,128)(2,1)S(1)}, bf16[1024,1792]{1,0:T(8,128)(2,1)S(1)}) custom-call(s32[3]{0:T(128)S(1)} %pad_add_fusion.place, bf16[1024,1536]{1,0:T(8,128)(2,1)} %hidden_ref.1, bf16[1024,5120]{1,0:T(8,128)(2,1)} %refs_0_.3), custom_call_target="tpu_custom_call" | custom-call | bytes 1024 | tf_op jit(solution)/shard_map/turn/pallas_call | solution.py:112
  4.4 4.1 %product.9 = (bf16[2,2,2,96,1792]{4,3,2,1,0:T(8,128)(2,1)S(1)}, bf16[1024,1792]{1,0:T(8,128)(2,1)S(1)}) custom-call(s32[3]{0:T(128)S(1)} %pad_add_fusion.place, bf16[2,2,2,96,1024]{4,3,2,1,0:T(8,128)(2,1)S(1)} %get-tuple-element.86.left_ref, bf16[1024,1792]{1,0:T(8,128)(2,1)S(1)} %get-tuple-element.87.right_ref, bf16[1024,5120]{1,0:T(8,128)(2,1)} %refs_0_.3), custom_call_target="tpu_custom_call" | custom-call | bytes 1024 | tf_op jit(solution)/shard_map/product/pallas_call | solution.py:179
  8.5 0.1 collective-permute-start
  8.6 4.1 %product.10 = (bf16[2,2,2,96,1792]{4,3,2,1,0:T(8,128)(2,1)S(1)}, bf16[1024,1536]{1,0:T(8,128)(2,1)S(1)}) custom-call(s32[3]{0:T(128)S(1)} %pad_add_fusion.place, bf16[2,2,2,96,1024]{4,3,2,1,0:T(8,128)(2,1)S(1)} %get-tuple-element.86.left_ref, bf16[1024,1792]{1,0:T(8,128)(2,1)S(1)} %get-tuple-element.90.right_ref, bf16[1024,5120]{1,0:T(8,128)(2,1)} %refs_0_.3), custom_call_target="tpu_custom_call" | custom-call | bytes 1024 | tf_op jit(solution)/shard_map/product/pallas_call | solution.py:179
  12.8 0.6 collective-permute-start.1
  13.4 3.3 %product.11 = bf16[2,2,2,96,1536]{4,3,2,1,0:T(8,128)(2,1)S(1)} custom-call(s32[3]{0:T(128)S(1)} %pad_add_fusion.place, bf16[2,2,2,96,1024]{4,3,2,1,0:T(8,128)(2,1)S(1)} %get-tuple-element.86.left_ref, bf16[1024,1536]{1,0:T(8,128)(2,1)S(1)} %get-tuple-element.93.right_ref), custom_call_target="tpu_custom_call" | custom-call | bytes 1024 | tf_op jit(solution)/shard_map/product/pallas_call | solution.py:179
  16.7 0.1 collective-permute-start.2
  16.8 0.0 collective-permute-done.refs_0_
  16.8 2.5 %product.12 = bf16[2,2,96,1792]{3,2,1,0:T(8,128)(2,1)S(1)} custom-call(s32[3]{0:T(128)S(1)} %pad_add_fusion.place, bf16[2,2,2,96,1024]{4,3,2,1,0:T(8,128)(2,1)S(1)} %get-tuple-element.95.left_ref, bf16[1024,1792]{1,0:T(8,128)(2,1)S(1)} %get-tuple-element.87.right_ref, bf16[2,2,2,96,1792]{4,3,2,1,0:T(8,128)(2,1)S(1)} %collective-permute-done.refs_0_), custom_call_target="tpu_custom_call" | custom-call | bytes 1024 | tf_op jit(solution)/shard_map/product/pallas_call | solution.py:179
  19.3 1.7 %collective-permute-start.3 = (bf16[2,2,96,1792]{3,2,1,0:T(8,128)(2,1)S(1)}, bf16[2,2,96,1792]{3,2,1,0:T(8,128)(2,1)S(1)}, u32[]{:S(2)}, u32[]{:S(2)}) collective-permute-start(bf16[2,2,96,1792]{3,2,1,0:T(8,128)(2,1)S(1)} %product.12), channel_id=1, source_target_pairs={{0,2},{1,3},{2,0},{3,1},{4,6},{5,7},{6,4},{7,5},{8,10},{9,11},{10,... | collective-permute-start | bytes 4128776 | tf_op jit(solution)/shard_map/ppermute | solution.py:52
  21.0 0.0 collective-permute-done.1.refs_0_
  21.0 2.5 %product.13 = bf16[2,2,96,1792]{3,2,1,0:T(8,128)(2,1)S(1)} custom-call(s32[3]{0:T(128)S(1)} %pad_add_fusion.place, bf16[2,2,2,96,1024]{4,3,2,1,0:T(8,128)(2,1)S(1)} %get-tuple-element.95.left_ref, bf16[1024,1792]{1,0:T(8,128)(2,1)S(1)} %get-tuple-element.90.right_ref, bf16[2,2,2,96,1792]{4,3,2,1,0:T(8,128)(2,1)S(1)} %collective-permute-done.1.refs_0_), custom_call_target="tpu_custom_call" | custom-call | bytes 1024 | tf_op jit(solution)/shard_map/product/pallas_call | solution.py:179
  23.5 1.7 %collective-permute-start.4 = (bf16[2,2,96,1792]{3,2,1,0:T(8,128)(2,1)S(1)}, bf16[2,2,96,1792]{3,2,1,0:T(8,128)(2,1)S(1)}, u32[]{:S(2)}, u32[]{:S(2)}) collective-permute-start(bf16[2,2,96,1792]{3,2,1,0:T(8,128)(2,1)S(1)} %product.13), channel_id=1, source_target_pairs={{0,4},{1,5},{2,6},{3,7},{4,0},{5,1},{6,2},{7,3},{8,12},{9,13},{10,... | collective-permute-start | bytes 4128776 | tf_op jit(solution)/shard_map/ppermute | solution.py:52
  25.2 2.1 %product.14 = bf16[2,2,96,1536]{3,2,1,0:T(8,128)(2,1)S(1)} custom-call(s32[3]{0:T(128)S(1)} %pad_add_fusion.place, bf16[2,2,2,96,1024]{4,3,2,1,0:T(8,128)(2,1)S(1)} %get-tuple-element.95.left_ref, bf16[1024,1536]{1,0:T(8,128)(2,1)S(1)} %get-tuple-element.93.right_ref, bf16[2,2,2,96,1536]{4,3,2,1,0:T(8,128)(2,1)S(1)} %collective-permute-done.2.refs_0_), custom_call_target="tpu_custom_call" | custom-call | bytes 1024 | tf_op jit(solution)/shard_map/product/pallas_call | solution.py:179
  27.3 2.3 %collective-permute-start.5 = (bf16[2,2,96,1536]{3,2,1,0:T(8,128)(2,1)S(1)}, bf16[2,2,96,1536]{3,2,1,0:T(8,128)(2,1)S(1)}, u32[]{:S(2)}, u32[]{:S(2)}) collective-permute-start(bf16[2,2,96,1536]{3,2,1,0:T(8,128)(2,1)S(1)} %product.14), channel_id=1, source_target_pairs={{0,12},{1,13},{2,14},{3,15},{4,8},{5,9},{6,10},{7,11},{8,4},{9,5},... | collective-permute-start | bytes 3538952 | tf_op jit(solution)/shard_map/ppermute | solution.py:52
  29.5 2.5 %product.15 = bf16[2,2,96,1792]{3,2,1,0:T(8,128)(2,1)S(1)} custom-call(s32[3]{0:T(128)S(1)} %pad_add_fusion.place, bf16[2,2,2,96,1024]{4,3,2,1,0:T(8,128)(2,1)S(1)} %get-tuple-element.95.left_ref, bf16[1024,1792]{1,0:T(8,128)(2,1)S(1)} %get-tuple-element.87.right_ref, bf16[2,2,2,96,1792]{4,3,2,1,0:T(8,128)(2,1)S(1)} %collective-permute-done.refs_0_), custom_call_target="tpu_custom_call" | custom-call | bytes 1024 | tf_op jit(solution)/shard_map/product/pallas_call | solution.py:179
  32.1 2.5 %product.16 = bf16[2,2,96,1792]{3,2,1,0:T(8,128)(2,1)S(1)} custom-call(s32[3]{0:T(128)S(1)} %pad_add_fusion.place, bf16[2,2,2,96,1024]{4,3,2,1,0:T(8,128)(2,1)S(1)} %get-tuple-element.95.left_ref, bf16[1024,1792]{1,0:T(8,128)(2,1)S(1)} %get-tuple-element.90.right_ref, bf16[2,2,2,96,1792]{4,3,2,1,0:T(8,128)(2,1)S(1)} %collective-permute-done.1.refs_0_), custom_call_target="tpu_custom_call" | custom-call | bytes 1024 | tf_op jit(solution)/shard_map/product/pallas_call | solution.py:179
  34.6 2.1 %product.17 = bf16[2,2,96,1536]{3,2,1,0:T(8,128)(2,1)S(1)} custom-call(s32[3]{0:T(128)S(1)} %pad_add_fusion.place, bf16[2,2,2,96,1024]{4,3,2,1,0:T(8,128)(2,1)S(1)} %get-tuple-element.95.left_ref, bf16[1024,1536]{1,0:T(8,128)(2,1)S(1)} %get-tuple-element.93.right_ref, bf16[2,2,2,96,1536]{4,3,2,1,0:T(8,128)(2,1)S(1)} %collective-permute-done.2.refs_0_), custom_call_target="tpu_custom_call" | custom-call | bytes 1024 | tf_op jit(solution)/shard_map/product/pallas_call | solution.py:179
  36.7 15.2 %collective-permute-done.3 = bf16[2,2,96,1792]{3,2,1,0:T(8,128)(2,1)S(1)} collective-permute-done((bf16[2,2,96,1792]{3,2,1,0:T(8,128)(2,1)S(1)}, bf16[2,2,96,1792]{3,2,1,0:T(8,128)(2,1)S(1)}, u32[]{:S(2)}, u32[]{:S(2)}) %collective-permute-start.3) | collective-permute-done | bytes 1376288 | tf_op jit(solution)/shard_map/ppermute | solution.py:52
  52.0 0.3 fusion.3
  52.3 1.7 %collective-permute-start.6 = (bf16[2,96,1792]{2,1,0:T(8,128)(2,1)S(1)}, bf16[2,96,1792]{2,1,0:T(8,128)(2,1)S(1)}, u32[]{:S(2)}, u32[]{:S(2)}) collective-permute-start(bf16[2,96,1792]{2,1,0:T(8,128)(2,1)S(1)} %get-tuple-element.169), channel_id=1, source_target_pairs={{0,4},{1,5},{2,6},{3,7},{4,0},{5,1},{6,2},{7,3},{8,12},{9,13},{10,... | collective-permute-start | bytes 2064392 | tf_op jit(solution)/shard_map/ppermute | solution.py:52
  54.0 2.5 %collective-permute-done.4 = bf16[2,2,96,1792]{3,2,1,0:T(8,128)(2,1)S(1)} collective-permute-done((bf16[2,2,96,1792]{3,2,1,0:T(8,128)(2,1)S(1)}, bf16[2,2,96,1792]{3,2,1,0:T(8,128)(2,1)S(1)}, u32[]{:S(2)}, u32[]{:S(2)}) %collective-permute-start.4) | collective-permute-done | bytes 1376288 | tf_op jit(solution)/shard_map/ppermute | solution.py:52
  56.6 0.3 fusion.2
  56.9 3.3 %collective-permute-start.7 = (bf16[2,96,1792]{2,1,0:T(8,128)(2,1)S(1)}, bf16[2,96,1792]{2,1,0:T(8,128)(2,1)S(1)}, u32[]{:S(2)}, u32[]{:S(2)}) collective-permute-start(bf16[2,96,1792]{2,1,0:T(8,128)(2,1)S(1)} %get-tuple-element.171), channel_id=1, source_target_pairs={{0,12},{1,13},{2,14},{3,15},{4,8},{5,9},{6,10},{7,11},{8,4},{9,5},... | collective-permute-start | bytes 2064392 | tf_op jit(solution)/shard_map/ppermute | solution.py:52
  60.2 0.3 fusion.5
  60.5 0.1 collective-permute-start.8
  60.6 3.3 %hold.1 = (bf16[1,96,5120]{2,1,0:T(8,128)(2,1)S(1)}, bf16[1,96,5120]{2,1,0:T(8,128)(2,1)S(1)}, f32[1,96,5120]{2,1,0:T(8,128)S(1)}, f32[96,5120]{1,0:T(8,128)S(1)}, f32[96,5120]{1,0:T(8,128)S(1)}) custom-call(s32[3]{0:T(128)S(1)} %pad_add_fusion.place, bf16[1,96,5120]{2,1,0:T(8,128)(2,1)} %first.1, bf16[1,96,5120]{2,1,0:T(8,128)(2,1)} %second.1, ...), custom_call_target="tpu_custom_call" | custom-call | bytes 1024 | tf_op jit(solution)/shard_map/hold/pallas_call | solution.py:262
  64.0 6.7 %collective-permute-done.6 = bf16[2,96,1792]{2,1,0:T(8,128)(2,1)S(1)} collective-permute-done((bf16[2,96,1792]{2,1,0:T(8,128)(2,1)S(1)}, bf16[2,96,1792]{2,1,0:T(8,128)(2,1)S(1)}, u32[]{:S(2)}, u32[]{:S(2)}) %collective-permute-start.6) | collective-permute-done | bytes 688160 | tf_op jit(solution)/shard_map/ppermute | solution.py:52
  70.6 0.2 fusion.8
  70.8 3.1 %collective-permute-start.9 = (bf16[96,1792]{1,0:T(8,128)(2,1)S(1)}, bf16[96,1792]{1,0:T(8,128)(2,1)S(1)}, u32[]{:S(2)}, u32[]{:S(2)}) collective-permute-start(bf16[96,1792]{1,0:T(8,128)(2,1)S(1)} %get-tuple-element.177), channel_id=1, source_target_pairs={{0,12},{1,13},{2,14},{3,15},{4,8},{5,9},{6,10},{7,11},{8,4},{9,5},... | collective-permute-start | bytes 1032200 | tf_op jit(solution)/shard_map/ppermute | solution.py:52
  73.9 0.9 collective-permute-done.7
  74.8 0.2 fusion.9
  74.9 1.0 collective-permute-start.10
  76.0 0.1 fusion.11
  76.1 0.4 collective-permute-start.11
  76.5 5.4 %collective-permute-done.9.refs_1_ = bf16[96,1792]{1,0:T(8,128)(2,1)S(1)} collective-permute-done((bf16[96,1792]{1,0:T(8,128)(2,1)S(1)}, bf16[96,1792]{1,0:T(8,128)(2,1)S(1)}, u32[]{:S(2)}, u32[]{:S(2)}) %collective-permute-start.9) | collective-permute-done | bytes 344096 | tf_op jit(solution)/shard_map/ppermute | solution.py:52
  81.9 1.4 %adam.3 = (bf16[1,96,5120]{2,1,0:T(8,128)(2,1)S(1)}, bf16[1,96,5120]{2,1,0:T(8,128)(2,1)S(1)}, bf16[24,3584]{1,0:T(8,128)(2,1)S(1)}, bf16[24,3584]{1,0:T(8,128)(...) custom-call(s32[3]{0:T(128)S(1)} %pad_add_fusion.place, ...), custom_call_target="tpu_custom_call" | custom-call | bytes 1024 | tf_op jit(solution)/shard_map/adam/pallas_call | solution.py:227
  83.2 0.0 collective-permute-done.10.refs_1_
  83.2 1.4 %adam.4 = (bf16[1,96,5120]{2,1,0:T(8,128)(2,1)S(1)}, bf16[1,96,5120]{2,1,0:T(8,128)(2,1)S(1)}, bf16[24,3584]{1,0:T(8,128)(2,1)S(1)}, bf16[24,3584]{1,0:T(8,128)(...) custom-call(s32[3]{0:T(128)S(1)} %pad_add_fusion.place, ...), custom_call_target="tpu_custom_call", output_to_operand_aliasing={{0}: (8, {}), {1}: (9, {}), {2}: (10, {}), {3}: (11, {}), {... | custom-call | bytes 1024 | tf_op jit(solution)/shard_map/adam/pallas_call | solution.py:227
  84.6 2.0 %collective-permute-start.12 = (bf16[24,3584]{1,0:T(8,128)(2,1)S(1)}, bf16[24,3584]{1,0:T(8,128)(2,1)S(1)}, u32[]{:S(2)}, u32[]{:S(2)}) collective-permute-start(bf16[24,3584]{1,0:T(8,128)(2,1)S(1)} %get-tuple-element.145), channel_id=1, source_target_pairs={{0,16},{16,0},{32,48},{48,32},{64,80},{80,64},{96,112},{112,96},{1... | collective-permute-start | bytes 516104 | tf_op jit(solution)/shard_map/ppermute | solution.py:56
  86.6 3.6 %collective-permute-start.13 = (bf16[24,3584]{1,0:T(8,128)(2,1)S(1)}, bf16[24,3584]{1,0:T(8,128)(2,1)S(1)}, u32[]{:S(2)}, u32[]{:S(2)}) collective-permute-start(bf16[24,3584]{1,0:T(8,128)(2,1)S(1)} %get-tuple-element.146), channel_id=1, source_target_pairs={{0,32},{16,48},{32,0},{48,16},{64,96},{80,112},{96,64},{112,80},{1... | collective-permute-start | bytes 516104 | tf_op jit(solution)/shard_map/ppermute | solution.py:56
  90.2 0.0 collective-permute-start.14
  90.2 0.0 collective-permute-done.11.refs_1_
  90.2 1.3 %adam.5 = (bf16[1,96,5120]{2,1,0:T(8,128)(2,1)S(1)}, bf16[1,96,5120]{2,1,0:T(8,128)(2,1)S(1)}, bf16[24,1536]{1,0:T(8,128)(2,1)S(1)}, bf16[24,1536]{1,0:T(8,128)(...) custom-call(s32[3]{0:T(128)S(1)} %pad_add_fusion.place, ...), custom_call_target="tpu_custom_call", output_to_operand_aliasing={{0}: (8, {}), {1}: (9, {})} | custom-call | bytes 1024 | tf_op jit(solution)/shard_map/adam/pallas_call | solution.py:227
  91.5 1.8 %store.1 = (bf16[1,96,5120]{2,1,0:T(8,128)(2,1)}, bf16[1,96,5120]{2,1,0:T(8,128)(2,1)}, bf16[24,3584]{1,0:T(8,128)(2,1)S(1)}) custom-call(s32[3]{0:T(128)S(1)} %pad_add_fusion.place, bf16[1,96,5120]{2,1,0:T(8,128)(2,1)S(1)} %get-tuple-element.139.first, bf16[1,96,5120]{2,1,0:T(8,128)(2,1)S(1)} %get-tuple-element.140.second, ...), custom_call_target="tpu_custom_call", output_to_operand_aliasing={{2}: (3, {})} | custom-call | bytes 1024 | tf_op jit(solution)/shard_map/store/pallas_call | solution.py:287
  93.3 0.1 collective-permute-start.15
  93.4 4.7 %collective-permute-start.16 = (bf16[24,1536]{1,0:T(8,128)(2,1)S(1)}, bf16[24,1536]{1,0:T(8,128)(2,1)S(1)}, u32[]{:S(2)}, u32[]{:S(2)}) collective-permute-start(bf16[24,1536]{1,0:T(8,128)(2,1)S(1)} %get-tuple-element.151), channel_id=1, source_target_pairs={{0,32},{16,48},{32,0},{48,16},{64,96},{80,112},{96,64},{112,80},{1... | collective-permute-start | bytes 221192 | tf_op jit(solution)/shard_map/ppermute | solution.py:56
  98.2 2.3 %collective-permute-done.14 = bf16[24,3584]{1,0:T(8,128)(2,1)S(1)} collective-permute-done((bf16[24,3584]{1,0:T(8,128)(2,1)S(1)}, bf16[24,3584]{1,0:T(8,128)(2,1)S(1)}, u32[]{:S(2)}, u32[]{:S(2)}) %collective-permute-start.14) | collective-permute-done | bytes 172064 | tf_op jit(solution)/shard_map/ppermute | solution.py:56
  100.4 0.1 add_convert_fusion.13
  100.5 2.8 %collective-permute-start.18 = (bf16[24,3584]{1,0:T(8,128)(2,1)S(1)}, bf16[24,3584]{1,0:T(8,128)(2,1)S(1)}, u32[]{:S(2)}, u32[]{:S(2)}) collective-permute-start(bf16[24,3584]{1,0:T(8,128)(2,1)S(1)} %add_convert_fusion.13), channel_id=1, source_target_pairs={{0,64},{16,80},{32,96},{48,112},{64,0},{80,16},{96,32},{112,48},{1... | collective-permute-start | bytes 516104 | tf_op jit(solution)/shard_map/ppermute | solution.py:56
  103.3 0.4 collective-permute-done.17
  103.8 2.8 %collective-permute-start.19 = (bf16[24,1536]{1,0:T(8,128)(2,1)S(1)}, bf16[24,1536]{1,0:T(8,128)(2,1)S(1)}, u32[]{:S(2)}, u32[]{:S(2)}) collective-permute-start(bf16[24,1536]{1,0:T(8,128)(2,1)S(1)} %add_convert_fusion.15), channel_id=1, source_target_pairs={{0,64},{16,80},{32,96},{48,112},{64,0},{80,16},{96,32},{112,48},{1... | collective-permute-start | bytes 221192 | tf_op jit(solution)/shard_map/ppermute | solution.py:56
  106.6 1.7 %collective-permute-done.18 = bf16[24,3584]{1,0:T(8,128)(2,1)S(1)} collective-permute-done((bf16[24,3584]{1,0:T(8,128)(2,1)S(1)}, bf16[24,3584]{1,0:T(8,128)(2,1)S(1)}, u32[]{:S(2)}, u32[]{:S(2)}) %collective-permute-start.18) | collective-permute-done | bytes 172064 | tf_op jit(solution)/shard_map/ppermute | solution.py:56
  108.3 0.4 collective-permute-start.22
  108.7 0.2 collective-permute-start.21
  108.9 3.6 %collective-permute-start.20 = (bf16[24,3584]{1,0:T(8,128)(2,1)S(1)}, bf16[24,3584]{1,0:T(8,128)(2,1)S(1)}, u32[]{:S(2)}, u32[]{:S(2)}) collective-permute-start(bf16[24,3584]{1,0:T(8,128)(2,1)S(1)} %add_convert_fusion.12.p0), channel_id=1, source_target_pairs={{0,16},{16,0},{32,48},{48,32},{64,80},{80,64},{96,112},{112,96},{1... | collective-permute-start | bytes 516104 | tf_op jit(solution)/shard_map/ppermute | solution.py:56
  112.5 0.4 collective-permute-start.25
  112.9 1.7 %collective-permute-start.24 = (bf16[24,1536]{1,0:T(8,128)(2,1)S(1)}, bf16[24,1536]{1,0:T(8,128)(2,1)S(1)}, u32[]{:S(2)}, u32[]{:S(2)}) collective-permute-start(bf16[24,1536]{1,0:T(8,128)(2,1)S(1)} %add_convert_fusion.14.p0), channel_id=1, source_target_pairs={{0,32},{16,48},{32,0},{48,16},{64,96},{80,112},{96,64},{112,80},{1... | collective-permute-start | bytes 221192 | tf_op jit(solution)/shard_map/ppermute | solution.py:56
  114.6 2.5 %collective-permute-done.22.p3 = bf16[24,3584]{1,0:T(8,128)(2,1)S(1)} collective-permute-done((bf16[24,3584]{1,0:T(8,128)(2,1)S(1)}, bf16[24,3584]{1,0:T(8,128)(2,1)S(1)}, u32[]{:S(2)}, u32[]{:S(2)}) %collective-permute-start.22) | collective-permute-done | bytes 172064 | tf_op jit(solution)/shard_map/ppermute | solution.py:56
  117.2 1.3 %collective-permute-done.20.p1 = bf16[24,3584]{1,0:T(8,128)(2,1)S(1)} collective-permute-done((bf16[24,3584]{1,0:T(8,128)(2,1)S(1)}, bf16[24,3584]{1,0:T(8,128)(2,1)S(1)}, u32[]{:S(2)}, u32[]{:S(2)}) %collective-permute-start.20) | collective-permute-done | bytes 172064 | tf_op jit(solution)/shard_map/ppermute | solution.py:56
  118.5 2.2 %last.2 = (f32[96,5120]{1,0:T(8,128)}, f32[96,5120]{1,0:T(8,128)S(1)}) custom-call(s32[3]{0:T(128)S(1)} %pad_add_fusion.place, bf16[24,3584]{1,0:T(8,128)(2,1)S(1)} %add_convert_fusion.12.p0, bf16[24,3584]{1,0:T(8,128)(2,1)S(1)} %collective-permute-done.20.p1, bf16[24,3584]{1,0:T(8,128)(2,1)S(1)} %collective-permute-done.21.p2, ...), custom_call_target="tpu_custom_call" | custom-call | bytes 1024 | tf_op jit(solution)/shard_map/last/pallas_call | solution.py:339
  120.7 0.8 collective-permute-done.23.p1
  121.5 1.7 %last.3 = (f32[96,5120]{1,0:T(8,128)}, f32[96,5120]{1,0:T(8,128)S(1)}, f32[96,640]{1,0:T(8,128)}) custom-call(s32[3]{0:T(128)S(1)} %pad_add_fusion.place, bf16[24,1536]{1,0:T(8,128)(2,1)S(1)} %add_convert_fusion.14.p0, bf16[24,1536]{1,0:T(8,128)(2,1)S(1)} %collective-permute-done.23.p1, ...), custom_call_target="tpu_custom_call", output_to_operand_aliasing={{0}: (7, {}), {1}: (8, {})} | custom-call | bytes 1024 | tf_op jit(solution)/shard_map/last/pallas_call | solution.py:339
  (16 shorter events, 0.1 us)
Async XLA Ops:
  8.5 8.2 %collective-permute-start = (bf16[2,2,2,96,1792]{4,3,2,1,0:T(8,128)(2,1)S(1)}, bf16[2,2,2,96,1792]{4,3,2,1,0:T(8,128)(2,1)S(1)}, u32[]{:S(2)}, u32[]{:S(2)}) collective-permute-start(bf16[2,2,2,96,1792]{4,3,2,1,0:T(8,128)(2,1)S(1)} %get-tuple-element.88), channel_id=1, source_target_pairs={{0,1},{1,0},{2,3},{3,2},{4,5},{5,4},{6,7},{7,6},{8,9},{9,8},{10,11... | collective-permute-start | bytes 8257544 | tf_op jit(solution)/shard_map/ppermute | solution.py:52
  12.8 8.2 %collective-permute-start.1 = (bf16[2,2,2,96,1792]{4,3,2,1,0:T(8,128)(2,1)S(1)}, bf16[2,2,2,96,1792]{4,3,2,1,0:T(8,128)(2,1)S(1)}, u32[]{:S(2)}, u32[]{:S(2)}) collective-permute-start(bf16[2,2,2,96,1792]{4,3,2,1,0:T(8,128)(2,1)S(1)} %get-tuple-element.91), channel_id=1, source_target_pairs={{0,1},{1,0},{2,3},{3,2},{4,5},{5,4},{6,7},{7,6},{8,9},{9,8},{10,11... | collective-permute-start | bytes 8257544 | tf_op jit(solution)/shard_map/ppermute | solution.py:52
  16.7 8.5 %collective-permute-start.2 = (bf16[2,2,2,96,1536]{4,3,2,1,0:T(8,128)(2,1)S(1)}, bf16[2,2,2,96,1536]{4,3,2,1,0:T(8,128)(2,1)S(1)}, u32[]{:S(2)}, u32[]{:S(2)}) collective-permute-start(bf16[2,2,2,96,1536]{4,3,2,1,0:T(8,128)(2,1)S(1)} %product.11), channel_id=1, source_target_pairs={{0,1},{1,0},{2,3},{3,2},{4,5},{5,4},{6,7},{7,6},{8,9},{9,8},{10,11... | collective-permute-start | bytes 7077896 | tf_op jit(solution)/shard_map/ppermute | solution.py:52
  19.3 32.7 %collective-permute-start.3 = (bf16[2,2,96,1792]{3,2,1,0:T(8,128)(2,1)S(1)}, bf16[2,2,96,1792]{3,2,1,0:T(8,128)(2,1)S(1)}, u32[]{:S(2)}, u32[]{:S(2)}) collective-permute-start(bf16[2,2,96,1792]{3,2,1,0:T(8,128)(2,1)S(1)} %product.12), channel_id=1, source_target_pairs={{0,2},{1,3},{2,0},{3,1},{4,6},{5,7},{6,4},{7,5},{8,10},{9,11},{10,... | collective-permute-start | bytes 4128776 | tf_op jit(solution)/shard_map/ppermute | solution.py:52
  23.5 33.1 %collective-permute-start.4 = (bf16[2,2,96,1792]{3,2,1,0:T(8,128)(2,1)S(1)}, bf16[2,2,96,1792]{3,2,1,0:T(8,128)(2,1)S(1)}, u32[]{:S(2)}, u32[]{:S(2)}) collective-permute-start(bf16[2,2,96,1792]{3,2,1,0:T(8,128)(2,1)S(1)} %product.13), channel_id=1, source_target_pairs={{0,4},{1,5},{2,6},{3,7},{4,0},{5,1},{6,2},{7,3},{8,12},{9,13},{10,... | collective-permute-start | bytes 4128776 | tf_op jit(solution)/shard_map/ppermute | solution.py:52
  27.3 32.9 %collective-permute-start.5 = (bf16[2,2,96,1536]{3,2,1,0:T(8,128)(2,1)S(1)}, bf16[2,2,96,1536]{3,2,1,0:T(8,128)(2,1)S(1)}, u32[]{:S(2)}, u32[]{:S(2)}) collective-permute-start(bf16[2,2,96,1536]{3,2,1,0:T(8,128)(2,1)S(1)} %product.14), channel_id=1, source_target_pairs={{0,12},{1,13},{2,14},{3,15},{4,8},{5,9},{6,10},{7,11},{8,4},{9,5},... | collective-permute-start | bytes 3538952 | tf_op jit(solution)/shard_map/ppermute | solution.py:52
  52.3 18.3 %collective-permute-start.6 = (bf16[2,96,1792]{2,1,0:T(8,128)(2,1)S(1)}, bf16[2,96,1792]{2,1,0:T(8,128)(2,1)S(1)}, u32[]{:S(2)}, u32[]{:S(2)}) collective-permute-start(bf16[2,96,1792]{2,1,0:T(8,128)(2,1)S(1)} %get-tuple-element.169), channel_id=1, source_target_pairs={{0,4},{1,5},{2,6},{3,7},{4,0},{5,1},{6,2},{7,3},{8,12},{9,13},{10,... | collective-permute-start | bytes 2064392 | tf_op jit(solution)/shard_map/ppermute | solution.py:52
  56.9 17.8 %collective-permute-start.7 = (bf16[2,96,1792]{2,1,0:T(8,128)(2,1)S(1)}, bf16[2,96,1792]{2,1,0:T(8,128)(2,1)S(1)}, u32[]{:S(2)}, u32[]{:S(2)}) collective-permute-start(bf16[2,96,1792]{2,1,0:T(8,128)(2,1)S(1)} %get-tuple-element.171), channel_id=1, source_target_pairs={{0,12},{1,13},{2,14},{3,15},{4,8},{5,9},{6,10},{7,11},{8,4},{9,5},... | collective-permute-start | bytes 2064392 | tf_op jit(solution)/shard_map/ppermute | solution.py:52
  60.5 15.4 %collective-permute-start.8 = (bf16[2,96,1536]{2,1,0:T(8,128)(2,1)S(1)}, bf16[2,96,1536]{2,1,0:T(8,128)(2,1)S(1)}, u32[]{:S(2)}, u32[]{:S(2)}) collective-permute-start(bf16[2,96,1536]{2,1,0:T(8,128)(2,1)S(1)} %get-tuple-element.172), channel_id=1, source_target_pairs={{0,2},{1,3},{2,0},{3,1},{4,6},{5,7},{6,4},{7,5},{8,10},{9,11},{10,... | collective-permute-start | bytes 1769480 | tf_op jit(solution)/shard_map/ppermute | solution.py:52
  70.8 11.1 %collective-permute-start.9 = (bf16[96,1792]{1,0:T(8,128)(2,1)S(1)}, bf16[96,1792]{1,0:T(8,128)(2,1)S(1)}, u32[]{:S(2)}, u32[]{:S(2)}) collective-permute-start(bf16[96,1792]{1,0:T(8,128)(2,1)S(1)} %get-tuple-element.177), channel_id=1, source_target_pairs={{0,12},{1,13},{2,14},{3,15},{4,8},{5,9},{6,10},{7,11},{8,4},{9,5},... | collective-permute-start | bytes 1032200 | tf_op jit(solution)/shard_map/ppermute | solution.py:52
  74.9 8.3 %collective-permute-start.10 = (bf16[96,1792]{1,0:T(8,128)(2,1)S(1)}, bf16[96,1792]{1,0:T(8,128)(2,1)S(1)}, u32[]{:S(2)}, u32[]{:S(2)}) collective-permute-start(bf16[96,1792]{1,0:T(8,128)(2,1)S(1)} %get-tuple-element.175), channel_id=1, source_target_pairs={{0,2},{1,3},{2,0},{3,1},{4,6},{5,7},{6,4},{7,5},{8,10},{9,11},{10,... | collective-permute-start | bytes 1032200 | tf_op jit(solution)/shard_map/ppermute | solution.py:52
  76.1 14.1 %collective-permute-start.11 = (bf16[96,1536]{1,0:T(8,128)(2,1)S(1)}, bf16[96,1536]{1,0:T(8,128)(2,1)S(1)}, u32[]{:S(2)}, u32[]{:S(2)}) collective-permute-start(bf16[96,1536]{1,0:T(8,128)(2,1)S(1)} %get-tuple-element.179), channel_id=1, source_target_pairs={{0,4},{1,5},{2,6},{3,7},{4,0},{5,1},{6,2},{7,3},{8,12},{9,13},{10,... | collective-permute-start | bytes 884744 | tf_op jit(solution)/shard_map/ppermute | solution.py:52
  84.6 13.5 %collective-permute-start.12 = (bf16[24,3584]{1,0:T(8,128)(2,1)S(1)}, bf16[24,3584]{1,0:T(8,128)(2,1)S(1)}, u32[]{:S(2)}, u32[]{:S(2)}) collective-permute-start(bf16[24,3584]{1,0:T(8,128)(2,1)S(1)} %get-tuple-element.145), channel_id=1, source_target_pairs={{0,16},{16,0},{32,48},{48,32},{64,80},{80,64},{96,112},{112,96},{1... | collective-permute-start | bytes 516104 | tf_op jit(solution)/shard_map/ppermute | solution.py:56
  86.6 11.5 %collective-permute-start.13 = (bf16[24,3584]{1,0:T(8,128)(2,1)S(1)}, bf16[24,3584]{1,0:T(8,128)(2,1)S(1)}, u32[]{:S(2)}, u32[]{:S(2)}) collective-permute-start(bf16[24,3584]{1,0:T(8,128)(2,1)S(1)} %get-tuple-element.146), channel_id=1, source_target_pairs={{0,32},{16,48},{32,0},{48,16},{64,96},{80,112},{96,64},{112,80},{1... | collective-permute-start | bytes 516104 | tf_op jit(solution)/shard_map/ppermute | solution.py:56
  90.2 10.2 %collective-permute-start.14 = (bf16[24,3584]{1,0:T(8,128)(2,1)S(1)}, bf16[24,3584]{1,0:T(8,128)(2,1)S(1)}, u32[]{:S(2)}, u32[]{:S(2)}) collective-permute-start(bf16[24,3584]{1,0:T(8,128)(2,1)S(1)} %get-tuple-element.147), channel_id=1, source_target_pairs={{0,48},{16,32},{32,16},{48,0},{64,112},{80,96},{96,80},{112,64},{1... | collective-permute-start | bytes 516104 | tf_op jit(solution)/shard_map/ppermute | solution.py:56
  93.3 10.0 %collective-permute-start.15 = (bf16[24,1536]{1,0:T(8,128)(2,1)S(1)}, bf16[24,1536]{1,0:T(8,128)(2,1)S(1)}, u32[]{:S(2)}, u32[]{:S(2)}) collective-permute-start(bf16[24,1536]{1,0:T(8,128)(2,1)S(1)} %get-tuple-element.150), channel_id=1, source_target_pairs={{0,16},{16,0},{32,48},{48,32},{64,80},{80,64},{96,112},{112,96},{1... | collective-permute-start | bytes 221192 | tf_op jit(solution)/shard_map/ppermute | solution.py:56
  93.4 9.9 %collective-permute-start.16 = (bf16[24,1536]{1,0:T(8,128)(2,1)S(1)}, bf16[24,1536]{1,0:T(8,128)(2,1)S(1)}, u32[]{:S(2)}, u32[]{:S(2)}) collective-permute-start(bf16[24,1536]{1,0:T(8,128)(2,1)S(1)} %get-tuple-element.151), channel_id=1, source_target_pairs={{0,32},{16,48},{32,0},{48,16},{64,96},{80,112},{96,64},{112,80},{1... | collective-permute-start | bytes 221192 | tf_op jit(solution)/shard_map/ppermute | solution.py:56
  98.1 5.6 %collective-permute-start.17 = (bf16[24,1536]{1,0:T(8,128)(2,1)S(1)}, bf16[24,1536]{1,0:T(8,128)(2,1)S(1)}, u32[]{:S(2)}, u32[]{:S(2)}) collective-permute-start(bf16[24,1536]{1,0:T(8,128)(2,1)S(1)} %get-tuple-element.152), channel_id=1, source_target_pairs={{0,48},{16,32},{32,16},{48,0},{64,112},{80,96},{96,80},{112,64},{1... | collective-permute-start | bytes 221192 | tf_op jit(solution)/shard_map/ppermute | solution.py:56
  100.5 7.7 %collective-permute-start.18 = (bf16[24,3584]{1,0:T(8,128)(2,1)S(1)}, bf16[24,3584]{1,0:T(8,128)(2,1)S(1)}, u32[]{:S(2)}, u32[]{:S(2)}) collective-permute-start(bf16[24,3584]{1,0:T(8,128)(2,1)S(1)} %add_convert_fusion.13), channel_id=1, source_target_pairs={{0,64},{16,80},{32,96},{48,112},{64,0},{80,16},{96,32},{112,48},{1... | collective-permute-start | bytes 516104 | tf_op jit(solution)/shard_map/ppermute | solution.py:56
  103.8 8.7 %collective-permute-start.19 = (bf16[24,1536]{1,0:T(8,128)(2,1)S(1)}, bf16[24,1536]{1,0:T(8,128)(2,1)S(1)}, u32[]{:S(2)}, u32[]{:S(2)}) collective-permute-start(bf16[24,1536]{1,0:T(8,128)(2,1)S(1)} %add_convert_fusion.15), channel_id=1, source_target_pairs={{0,64},{16,80},{32,96},{48,112},{64,0},{80,16},{96,32},{112,48},{1... | collective-permute-start | bytes 221192 | tf_op jit(solution)/shard_map/ppermute | solution.py:56
  108.3 8.9 %collective-permute-start.22 = (bf16[24,3584]{1,0:T(8,128)(2,1)S(1)}, bf16[24,3584]{1,0:T(8,128)(2,1)S(1)}, u32[]{:S(2)}, u32[]{:S(2)}) collective-permute-start(bf16[24,3584]{1,0:T(8,128)(2,1)S(1)} %add_convert_fusion.12.p0), channel_id=1, source_target_pairs={{0,48},{16,32},{32,16},{48,0},{64,112},{80,96},{96,80},{112,64},{1... | collective-permute-start | bytes 516104 | tf_op jit(solution)/shard_map/ppermute | solution.py:56
  108.7 8.5 %collective-permute-start.21 = (bf16[24,3584]{1,0:T(8,128)(2,1)S(1)}, bf16[24,3584]{1,0:T(8,128)(2,1)S(1)}, u32[]{:S(2)}, u32[]{:S(2)}) collective-permute-start(bf16[24,3584]{1,0:T(8,128)(2,1)S(1)} %add_convert_fusion.12.p0), channel_id=1, source_target_pairs={{0,32},{16,48},{32,0},{48,16},{64,96},{80,112},{96,64},{112,80},{1... | collective-permute-start | bytes 516104 | tf_op jit(solution)/shard_map/ppermute | solution.py:56
  108.9 9.6 %collective-permute-start.20 = (bf16[24,3584]{1,0:T(8,128)(2,1)S(1)}, bf16[24,3584]{1,0:T(8,128)(2,1)S(1)}, u32[]{:S(2)}, u32[]{:S(2)}) collective-permute-start(bf16[24,3584]{1,0:T(8,128)(2,1)S(1)} %add_convert_fusion.12.p0), channel_id=1, source_target_pairs={{0,16},{16,0},{32,48},{48,32},{64,80},{80,64},{96,112},{112,96},{1... | collective-permute-start | bytes 516104 | tf_op jit(solution)/shard_map/ppermute | solution.py:56
  112.5 8.2 %collective-permute-start.25 = (bf16[24,1536]{1,0:T(8,128)(2,1)S(1)}, bf16[24,1536]{1,0:T(8,128)(2,1)S(1)}, u32[]{:S(2)}, u32[]{:S(2)}) collective-permute-start(bf16[24,1536]{1,0:T(8,128)(2,1)S(1)} %add_convert_fusion.14.p0), channel_id=1, source_target_pairs={{0,48},{16,32},{32,16},{48,0},{64,112},{80,96},{96,80},{112,64},{1... | collective-permute-start | bytes 221192 | tf_op jit(solution)/shard_map/ppermute | solution.py:56
  112.9 7.8 %collective-permute-start.24 = (bf16[24,1536]{1,0:T(8,128)(2,1)S(1)}, bf16[24,1536]{1,0:T(8,128)(2,1)S(1)}, u32[]{:S(2)}, u32[]{:S(2)}) collective-permute-start(bf16[24,1536]{1,0:T(8,128)(2,1)S(1)} %add_convert_fusion.14.p0), channel_id=1, source_target_pairs={{0,32},{16,48},{32,0},{48,16},{64,96},{80,112},{96,64},{112,80},{1... | collective-permute-start | bytes 221192 | tf_op jit(solution)/shard_map/ppermute | solution.py:56
  117.2 4.4 %collective-permute-start.23 = (bf16[24,1536]{1,0:T(8,128)(2,1)S(1)}, bf16[24,1536]{1,0:T(8,128)(2,1)S(1)}, u32[]{:S(2)}, u32[]{:S(2)}) collective-permute-start(bf16[24,1536]{1,0:T(8,128)(2,1)S(1)} %add_convert_fusion.14.p0), channel_id=1, source_target_pairs={{0,16},{16,0},{32,48},{48,32},{64,80},{80,64},{96,112},{112,96},{1... | collective-permute-start | bytes 221192 | tf_op jit(solution)/shard_map/ppermute | solution.py:56
